TPU v7x, 32 devices: a whole 2x2x4 slice. The times are simulated.
32 devices in a mesh: blk: 16 (over z, y, core), grp: 2 (over x).
Axes of the slice: x: 2, y: 2, z: 4, core: 2. Of those that a mesh axis runs over, the one named last changes fastest.
Arguments:
- dual_rhs: float32 [2, 16, 16384], P('grp', None, 'blk'), may hold values from -32 to 32
- dual_ops: bfloat16 [2, 16384, 1024], P('grp', 'blk'), may hold values from -1 to 6, as said below
- prec_ops: bfloat16 [2, 16384, 1024], P('grp', 'blk'), may hold values from -1 to 4, as said below
- corner_coupling: bfloat16 [2, 384, 512], P('grp', 'blk'), may hold values from -0.25 to 0.25
- corner_map: int32 [2, 384], P('grp', 'blk'), may hold values from 0 to 767
- signs: int32 [2, 16384], P('grp', 'blk'), may hold values from -1 to 1, as said below
- coarse_inverse: float32 [768, 768], replicated, may hold values from -1 to 5, as said below
Outputs:
- multipliers: float32 [2, 16, 16384], P('grp', None, 'blk')
- residual: float32 [2, 16, 16384], P('grp', None, 'blk')
Inputs may be any that keep to these rules, and one draw needn't show every extreme that they name: `dual_ops`: each subdomain's 1024 x 1024 block is symmetric positive definite. `prec_ops`: each subdomain's 1024 x 1024 block is symmetric positive definite. `signs`: every entry is 1 or -1; the lower face of each subdomain after the first of a group carries the negated signs of the upper face of the subdomain before it. `coarse_inverse`: symmetric positive definite.
All inputs are finite; a program needn't handle non-finite values.
Results may differ from a plain program's by a relative error of at most 0.003.
Values sent between devices are 32-bit elements; how exact they have to be, the bound alone decides.
No kernel may reach another device: no remote copies, remote signals or barrier semaphores. Data moves between devices by JAX's collectives and lax.ppermute only.
A program may use at most 64 MiB of HBM per device.

v0:
```python
import jax
import jax.numpy as jnp
from jax import lax
from jax.sharding import PartitionSpec as P

ITERS = 2


def extended(block, sides, width):
    for axis, dim in sides:
        count = lax.axis_size(axis)
        forward = [(i, i + 1) for i in range(count - 1)]
        backward = [(target, source) for source, target in forward]
        low = lax.ppermute(
            lax.slice_in_dim(block, block.shape[dim] - width, None, axis=dim), axis, forward
        )
        high = lax.ppermute(lax.slice_in_dim(block, 0, width, axis=dim), axis, backward)
        block = jnp.concatenate([low, block, high], axis=dim)
    return block


def gram_solve(matrix, target):
    balanced = 0.5 * (matrix + matrix.T)
    factor = jnp.linalg.cholesky(balanced)
    middle = lax.linalg.triangular_solve(factor, target, left_side=True, lower=True)
    return lax.linalg.triangular_solve(factor, middle, left_side=True, lower=True, transpose_a=True)


def local(dual_rhs, dual_ops, prec_ops, corner_coupling, corner_map, signs, coarse_inverse):
    highest = lax.Precision.HIGHEST
    width = dual_rhs.shape[2]
    face_width = width // 2
    blk_index = lax.axis_index("blk")
    blk_count = lax.axis_size("blk")
    lower_live = jnp.where(blk_index > 0, 1.0, 0.0).astype(jnp.float32)
    upper_live = jnp.where(blk_index < blk_count - 1, 1.0, 0.0).astype(jnp.float32)
    live_face = jnp.concatenate(
        [
            jnp.full((face_width,), 1.0, jnp.float32) * lower_live,
            jnp.full((face_width,), 1.0, jnp.float32) * upper_live,
        ]
    )
    face_sign = signs[0].astype(jnp.float32) * live_face
    couple = corner_coupling[0].astype(jnp.float32)
    corner_rows = couple.shape[0] // 2
    couple_lower = couple[:corner_rows]
    couple_upper = couple[corner_rows:]
    corners = coarse_inverse.shape[0]
    onehot = (corner_map[0][:, None] == jnp.arange(corners, dtype=jnp.int32)[None, :]).astype(
        jnp.float32
    )
    contract_last = (((1,), (1,)), ((), ()))
    contract_first = (((0,), (0,)), ((), ()))

    def assemble(local_out):
        signed_out = face_sign * local_out
        beside_all = extended(signed_out, (("blk", 1),), face_width)
        partner = jnp.concatenate(
            [beside_all[:, :face_width], beside_all[:, face_width + width :]], axis=1
        )
        return live_face * (signed_out + partner)

    def local_product(signed_in, blocks):
        rounded = signed_in.astype(jnp.bfloat16)
        return lax.dot_general(
            rounded, blocks[0], contract_last, preferred_element_type=jnp.float32
        )

    def corner_terms(values):
        signed_in = face_sign * values
        lower_part = lax.dot_general(
            signed_in[:, :face_width], couple_lower, contract_last, precision=highest
        )
        upper_part = lax.dot_general(
            signed_in[:, face_width:], couple_upper, contract_last, precision=highest
        )
        partial_value = jnp.concatenate([lower_part, upper_part], axis=1)
        return jnp.dot(partial_value, onehot, precision=highest)

    def precondition(values):
        return assemble(local_product(face_sign * values, prec_ops))

    def region(values):
        return lax.psum(values, ("blk", "grp"))

    def gram_of(first, second):
        return lax.dot_general(first, second, contract_last, precision=highest)

    def combine(weights, values):
        return lax.dot_general(weights, values, contract_first, precision=highest)

    residual = live_face * dual_rhs[0]
    multipliers = jnp.zeros_like(residual)
    precond = precondition(residual)
    gram_old, corner_sum = region((gram_of(residual, precond), corner_terms(precond)))
    direction = precond
    for iteration in range(ITERS):
        solved = lax.dot_general(corner_sum, coarse_inverse, contract_last, precision=highest)
        picked = lax.dot_general(solved, onehot, contract_last, precision=highest)
        lower_out = jnp.dot(picked[:, :corner_rows], couple_lower, precision=highest)
        upper_out = jnp.dot(picked[:, corner_rows:], couple_upper, precision=highest)
        image_dir = assemble(
            local_product(face_sign * direction, dual_ops)
            + jnp.concatenate([lower_out, upper_out], axis=1)
        )
        step_alpha = gram_solve(region(gram_of(direction, image_dir)), gram_old)
        multipliers = multipliers + combine(step_alpha, direction)
        residual = residual - combine(step_alpha, image_dir)
        if iteration + 1 < ITERS:
            precond = precondition(residual)
            gram_new, corner_new = region((gram_of(residual, precond), corner_terms(precond)))
            step_beta = gram_solve(gram_old, gram_new)
            corner_sum = corner_new + combine(step_beta, corner_sum)
            direction = precond + combine(step_beta, direction)
            gram_old = gram_new
    return (multipliers[None], residual[None])


def solution(mesh):
    in_specs = (
        P("grp", None, "blk"),
        P("grp", "blk", None),
        P("grp", "blk", None),
        P("grp", "blk", None),
        P("grp", "blk"),
        P("grp", "blk"),
        P(),
    )
    out_specs = (P("grp", None, "blk"), P("grp", None, "blk"))
    return jax.shard_map(local, mesh=mesh, in_specs=in_specs, out_specs=out_specs, check_vma=False)
```

profile of v0, /device:TPU:0, one launch (start us, length us, event | category | flops | bytes accessed | tf_op | source)
XLA Modules:
  0.0 224.3 jit_solution(3706977054849594740)
XLA Ops:
  0.7 0.8 convert_element_type.23
  1.5 2.3 %fusion.8 = f32[16,1024]{1,0:T(8,128)S(1)} fusion(bf16[1,1024,1024]{2,1,0:T(8,128)(2,1)} %param.14, f32[1,16,1024]{2,1,0:T(8,128)} %param.12, f32[1024]{0:T(1024)S(1)} %get-tuple-element.21, f32[1024]{0:T(1024)S(1)} %get-tuple-element.22), kind=kOutput, calls=%fused_computation.8 | convolution fusion | flops 33619968 | bytes 2236416 | tf_op jit(solution)/shard_map/dot_general | solution.py:65
  3.8 2.4 %collective-permute-start = (f32[16,512]{1,0:T(8,128)S(1)}, f32[16,512]{1,0:T(8,128)S(1)}, u32[]{:S(2)}, u32[]{:S(2)}) collective-permute-start(f32[16,512]{1,0:T(8,128)S(1)} %get-tuple-element.19), channel_id=1, source_target_pairs={{0,2},{2,4},{4,6},{6,8},{8,10},{10,12},{12,14},{14,16},{16,18},{18... | collective-permute-start | bytes 98312 | tf_op jit(solution)/shard_map/ppermute | solution.py:14
  6.2 1.3 collective-permute-start.1
  7.5 3.9 %collective-permute-done.1 = f32[16,512]{1,0:T(8,128)S(1)} collective-permute-done((f32[16,512]{1,0:T(8,128)S(1)}, f32[16,512]{1,0:T(8,128)S(1)}, u32[]{:S(2)}, u32[]{:S(2)}) %collective-permute-start.1) | collective-permute-done | bytes 32800 | tf_op jit(solution)/shard_map/ppermute | solution.py:17
  11.7 0.2 fusion.31
  12.0 42.9 %psum.42 = f32[16,768]{1,0:T(8,128)S(1)} all-reduce(f32[16,768]{1,0:T(8,128)S(1)} %fusion.31), channel_id=1, replica_groups=mesh['blk'=16,'grp'=2] {'blk','grp'}, use_global_device_ids=true, to_apply=%region_0.1 | all-reduce | flops 12288 | bytes 98304 | tf_op jit(solution)/shard_map/psum | solution.py:84
  55.0 2.0 fusion.127
  57.2 0.2 fusion.60
  57.6 0.6 fusion.17
  58.3 1.3 collective-permute-start.2
  59.6 1.3 collective-permute-start.3
  61.1 4.1 %collective-permute-done.3 = f32[16,512]{1,0:T(8,128)S(1)} collective-permute-done((f32[16,512]{1,0:T(8,128)S(1)}, f32[16,512]{1,0:T(8,128)S(1)}, u32[]{:S(2)}, u32[]{:S(2)}) %collective-permute-start.3) | collective-permute-done | bytes 32800 | tf_op jit(solution)/shard_map/ppermute | solution.py:17
  65.3 40.8 %all-reduce.2 = (f32[16,16]{1,0:T(8,128)S(1)}, f32[16,16]{1,0:T(8,128)S(1)}) all-reduce(f32[16,16]{1,0:T(8,128)S(1)} %fusion.36, f32[16,16]{1,0:T(8,128)S(1)} %fusion.70), channel_id=1, replica_groups=mesh['blk'=16,'grp'=2] {'blk','grp'}, use_global_device_ids=true, to_apply=%region_4.6 | all-reduce | flops 512 | bytes 4096 | tf_op jit(solution)/shard_map/psum | solution.py:84
  106.4 1.5 cholesky.70
  107.9 0.6 compare_reduce_fusion.1
  108.6 1.5 cholesky.59
  110.1 0.6 compare_reduce_fusion.2
  110.7 0.6 fusion.83
  111.4 1.2 custom-call.13
  112.6 0.2 fusion.108
  113.0 0.3 convolution_subtract_fusion.1
  113.3 2.2 fusion.11
  115.5 1.3 collective-permute-start.4
  116.8 1.3 collective-permute-start.5
  118.1 0.7 fusion.84
  118.8 1.2 custom-call.15
  120.0 2.5 %collective-permute-done.5 = f32[16,512]{1,0:T(8,128)S(1)} collective-permute-done((f32[16,512]{1,0:T(8,128)S(1)}, f32[16,512]{1,0:T(8,128)S(1)}, u32[]{:S(2)}, u32[]{:S(2)}) %collective-permute-start.5) | collective-permute-done | bytes 32800 | tf_op jit(solution)/shard_map/ppermute | solution.py:17
  123.0 0.3 fusion.29
  123.2 41.8 %all-reduce.1 = (f32[16,16]{1,0:T(8,128)S(1)}, f32[16,768]{1,0:T(8,128)S(1)}) all-reduce(f32[16,16]{1,0:T(8,128)S(1)} %fusion.128, f32[16,768]{1,0:T(8,128)S(1)} %fusion.29), channel_id=1, replica_groups=mesh['blk'=16,'grp'=2] {'blk','grp'}, use_global_device_ids=true, to_apply=%region_5.9 | all-reduce | flops 12544 | bytes 100352 | tf_op jit(solution)/shard_map/psum | solution.py:84
  165.4 0.3 convolution_add_fusion
  165.7 0.2 convolution_add_fusion.2
  165.9 2.0 fusion.129
  167.9 0.2 fusion.28
  168.2 0.2 fusion.57
  168.6 0.6 fusion.23
  169.2 1.3 collective-permute-start.6
  170.5 1.3 collective-permute-start.7
  171.8 4.3 %collective-permute-done.7 = f32[16,512]{1,0:T(8,128)S(1)} collective-permute-done((f32[16,512]{1,0:T(8,128)S(1)}, f32[16,512]{1,0:T(8,128)S(1)}, u32[]{:S(2)}, u32[]{:S(2)}) %collective-permute-start.7) | collective-permute-done | bytes 32800 | tf_op jit(solution)/shard_map/ppermute | solution.py:17
  176.3 41.4 %psum.47 = f32[16,16]{1,0:T(8,128)S(1)} all-reduce(f32[16,16]{1,0:T(8,128)S(1)} %fusion.73), channel_id=1, replica_groups=mesh['blk'=16,'grp'=2] {'blk','grp'}, use_global_device_ids=true, to_apply=%region_7.11 | all-reduce | flops 256 | bytes 2048 | tf_op jit(solution)/shard_map/psum | solution.py:84
  217.9 1.5 cholesky.81
  219.4 0.6 compare_reduce_fusion
  220.0 0.6 fusion.85
  220.7 1.2 custom-call.17
  221.9 0.2 fusion.96
  222.2 0.3 fusion.130
  222.5 0.9 fusion.27
  223.4 0.9 fusion.26
  (53 shorter events, 3.1 us)
Async XLA Ops:
  0.6 54.3 %copy-start = (f32[768,768]{1,0:T(8,128)S(1)}, f32[768,768]{1,0:T(8,128)}, u32[]{:S(2)}) copy-start(f32[768,768]{1,0:T(8,128)} %param.18) | copy-start | bytes 7077892
  0.6 10.8 %copy-start.4 = (bf16[1,24,512]{2,1,0:T(8,128)(2,1)S(1)}, bf16[1,24,512]{2,1,0:T(8,128)(2,1)}, u32[]{:S(2)}) copy-start(bf16[1,24,512]{2,1,0:T(8,128)(2,1)} %param.15) | copy-start | bytes 73732
  0.7 11.1 %copy-start.5 = (s32[1,24]{1,0:T(1,128)S(1)}, s32[1,24]{1,0:T(1,128)}, u32[]{:S(2)}) copy-start(s32[1,24]{1,0:T(1,128)} %param.16) | copy-start | bytes 292
  3.8 3.7 %collective-permute-start = (f32[16,512]{1,0:T(8,128)S(1)}, f32[16,512]{1,0:T(8,128)S(1)}, u32[]{:S(2)}, u32[]{:S(2)}) collective-permute-start(f32[16,512]{1,0:T(8,128)S(1)} %get-tuple-element.19), channel_id=1, source_target_pairs={{0,2},{2,4},{4,6},{6,8},{8,10},{10,12},{12,14},{14,16},{16,18},{18... | collective-permute-start | bytes 98312 | tf_op jit(solution)/shard_map/ppermute | solution.py:14
  6.2 5.2 %collective-permute-start.1 = (f32[16,512]{1,0:T(8,128)S(1)}, f32[16,512]{1,0:T(8,128)S(1)}, u32[]{:S(2)}, u32[]{:S(2)}) collective-permute-start(f32[16,512]{1,0:T(8,128)S(1)} %get-tuple-element.20), channel_id=1, source_target_pairs={{2,0},{4,2},{6,4},{8,6},{10,8},{12,10},{14,12},{16,14},{18,16},{20... | collective-permute-start | bytes 98312 | tf_op jit(solution)/shard_map/ppermute | solution.py:17
  54.9 2.6 %copy-start.1 = (bf16[1,1024,1024]{2,1,0:T(8,128)(2,1)S(1)}, bf16[1,1024,1024]{2,1,0:T(8,128)(2,1)}, u32[]{:S(2)}) copy-start(bf16[1,1024,1024]{2,1,0:T(8,128)(2,1)} %param.13) | copy-start | bytes 6291460
  55.0 5.9 %copy-start.3 = (f32[1,16,1024]{2,1,0:T(8,128)S(1)}, f32[1,16,1024]{2,1,0:T(8,128)}, u32[]{:S(2)}) copy-start(f32[1,16,1024]{2,1,0:T(8,128)} %param.12) | copy-start | bytes 196612
  58.3 2.8 %collective-permute-start.2 = (f32[16,512]{1,0:T(8,128)S(1)}, f32[16,512]{1,0:T(8,128)S(1)}, u32[]{:S(2)}, u32[]{:S(2)}) collective-permute-start(f32[16,512]{1,0:T(8,128)S(1)} %get-tuple-element.17), channel_id=1, source_target_pairs={{0,2},{2,4},{4,6},{6,8},{8,10},{10,12},{12,14},{14,16},{16,18},{18... | collective-permute-start | bytes 98312 | tf_op jit(solution)/shard_map/ppermute | solution.py:14
  59.6 5.6 %collective-permute-start.3 = (f32[16,512]{1,0:T(8,128)S(1)}, f32[16,512]{1,0:T(8,128)S(1)}, u32[]{:S(2)}, u32[]{:S(2)}) collective-permute-start(f32[16,512]{1,0:T(8,128)S(1)} %get-tuple-element.18), channel_id=1, source_target_pairs={{2,0},{4,2},{6,4},{8,6},{10,8},{12,10},{14,12},{16,14},{18,16},{20... | collective-permute-start | bytes 98312 | tf_op jit(solution)/shard_map/ppermute | solution.py:17
  115.5 4.5 %collective-permute-start.4 = (f32[16,512]{1,0:T(8,128)S(1)}, f32[16,512]{1,0:T(8,128)S(1)}, u32[]{:S(2)}, u32[]{:S(2)}) collective-permute-start(f32[16,512]{1,0:T(8,128)S(1)} %get-tuple-element.15), channel_id=1, source_target_pairs={{0,2},{2,4},{4,6},{6,8},{8,10},{10,12},{12,14},{14,16},{16,18},{18... | collective-permute-start | bytes 98312 | tf_op jit(solution)/shard_map/ppermute | solution.py:14
  116.8 5.7 %collective-permute-start.5 = (f32[16,512]{1,0:T(8,128)S(1)}, f32[16,512]{1,0:T(8,128)S(1)}, u32[]{:S(2)}, u32[]{:S(2)}) collective-permute-start(f32[16,512]{1,0:T(8,128)S(1)} %get-tuple-element.16), channel_id=1, source_target_pairs={{2,0},{4,2},{6,4},{8,6},{10,8},{12,10},{14,12},{16,14},{18,16},{20... | collective-permute-start | bytes 98312 | tf_op jit(solution)/shard_map/ppermute | solution.py:17
  165.1 3.5 %copy-start.2 = (bf16[1,1024,1024]{2,1,0:T(8,128)(2,1)S(1)}, bf16[1,1024,1024]{2,1,0:T(8,128)(2,1)}, u32[]{:S(2)}) copy-start(bf16[1,1024,1024]{2,1,0:T(8,128)(2,1)} %param.13) | copy-start | bytes 6291460
  169.2 2.6 %collective-permute-start.6 = (f32[16,512]{1,0:T(8,128)S(1)}, f32[16,512]{1,0:T(8,128)S(1)}, u32[]{:S(2)}, u32[]{:S(2)}) collective-permute-start(f32[16,512]{1,0:T(8,128)S(1)} %get-tuple-element.13), channel_id=1, source_target_pairs={{0,2},{2,4},{4,6},{6,8},{8,10},{10,12},{12,14},{14,16},{16,18},{18... | collective-permute-start | bytes 98312 | tf_op jit(solution)/shard_map/ppermute | solution.py:14
  170.5 5.6 %collective-permute-start.7 = (f32[16,512]{1,0:T(8,128)S(1)}, f32[16,512]{1,0:T(8,128)S(1)}, u32[]{:S(2)}, u32[]{:S(2)}) collective-permute-start(f32[16,512]{1,0:T(8,128)S(1)} %get-tuple-element.14), channel_id=1, source_target_pairs={{2,0},{4,2},{6,4},{8,6},{10,8},{12,10},{14,12},{16,14},{18,16},{20... | collective-permute-start | bytes 98312 | tf_op jit(solution)/shard_map/ppermute | solution.py:17
where the time goes:
time: 225 us; the launch traced here: 224 us
  blocking collectives  167 us (74%)
  matrix products  16.6 us (7%)
  waiting for transfers between devices  14.8 us (7%)
  other arithmetic  12.9 us (6%)
  starting transfers between devices  11.4 us (5%)
    psum x4, blocking collectives, region(): return lax.psum(values, ('blk', 'grp'))  167 us
    ppermute x4, waiting for transfers between devices, extended(): lax.ppermute(lax.slice_in_dim(block, 0, width, axis=dim), axis, backward)  14.8 us
    another operation x9, other arithmetic, gram_solve(): factor = jnp.linalg.cholesky(balanced)  6.39 us
    ppermute x4, starting transfers between devices, extended(): lax.ppermute(lax.slice_in_dim(block, block.shape[dim] - width, None, axis...  6.23 us
    dot_general x4, matrix products, local_product(): lax.dot_general(rounded, blocks[0], contract_last, preferred_element_type...  5.81 us
    another operation x6, other arithmetic, gram_solve(): lax.linalg.triangular_solve(factor, middle, left_side=True, lower=True, t...  5.63 us
    ppermute x4, starting transfers between devices, extended(): lax.ppermute(lax.slice_in_dim(block, 0, width, axis=dim), axis, backward)  5.17 us
  transfers between devices with their start and end apart: 8, of which 4 were waited for; matrix products, arithmetic and copies ran while one was open for 1% of the time, Pallas kernels for 0%

commit v1 on v0

v1 whole, which is shorter than its diff:
```python
import functools
import jax
import jax.numpy as jnp
from jax import lax
from jax.sharding import PartitionSpec as P

ITERS = 2
AXES = ("blk", "grp")
HIGHEST = lax.Precision.HIGHEST
NT = (((1,), (1,)), ((), ()))
TN = (((0,), (0,)), ((), ()))


def radices(count):
    found = []
    factor = 2
    while count > 1:
        while count % factor == 0:
            found.append(factor)
            count //= factor
        factor += 1
    return found


def swap(count, groups, partner):
    pairs = []
    for blk in range(count):
        for grp in range(groups):
            other = partner(blk)
            if 0 <= other < count:
                target = other * groups + grp
            elif grp ^ 1 < groups:
                target = blk * groups + (grp ^ 1)
            else:
                target = blk * groups + grp
            pairs.append((blk * groups + grp, target))
    return pairs


def inner_pairs(count, groups):
    return swap(count, groups, lambda blk: blk ^ 1)


def outer_pairs(count, groups):
    return swap(count, groups, lambda blk: blk + 1 if blk % 2 == 1 else blk - 1)


def rotations(count, groups):
    core = 2 if count % 2 == 0 else 1
    steps = []

    def flipped(blk, turn):
        return (blk ^ 1) if (core == 2 and turn) else blk

    def add_axis(step_target, factor):
        steps.append(
            [
                [
                    (blk * groups + grp, step_target(blk, grp, turn))
                    for blk in range(count)
                    for grp in range(groups)
                ]
                for turn in range(1, factor)
            ]
        )

    stride = 1
    blk_steps = []
    for factor in radices(count // core):
        blk_steps.append((stride, factor))
        stride *= factor
    grp_steps = []
    stride = 1
    for factor in radices(groups):
        grp_steps.append((stride, factor))
        stride *= factor

    def blk_target(stride, factor):
        def target(blk, grp, turn):
            chip = blk // core
            digit = (chip // stride) % factor
            moved = chip + ((digit + turn) % factor - digit) * stride
            return flipped(moved * core + blk % core, turn) * groups + grp

        return target

    def grp_target(stride, factor):
        def target(blk, grp, turn):
            digit = (grp // stride) % factor
            moved = grp + ((digit + turn) % factor - digit) * stride
            return flipped(blk, turn) * groups + moved

        return target

    for stride, factor in blk_steps[:1]:
        add_axis(blk_target(stride, factor), factor)
    for stride, factor in grp_steps:
        add_axis(grp_target(stride, factor), factor)
    for stride, factor in blk_steps[1:]:
        add_axis(blk_target(stride, factor), factor)
    return steps


def gram_solve(matrix, target):
    balanced = 0.5 * (matrix + matrix.T)
    factor = jnp.linalg.cholesky(balanced)
    middle = lax.linalg.triangular_solve(factor, target, left_side=True, lower=True)
    return lax.linalg.triangular_solve(factor, middle, left_side=True, lower=True, transpose_a=True)


def local(count, groups, dual_rhs, dual_ops, prec_ops, corner_coupling, corner_map, signs, coarse_inverse):
    nrhs, width = dual_rhs.shape[1:]
    half = width // 2
    corners = coarse_inverse.shape[0]
    blk = lax.axis_index("blk")
    even = blk % 2 == 0
    lower_live = jnp.where(blk > 0, 1.0, 0.0).astype(jnp.float32)
    upper_live = jnp.where(blk < count - 1, 1.0, 0.0).astype(jnp.float32)
    live = jnp.concatenate(
        [
            jnp.full((1, half), 1.0, jnp.float32) * lower_live,
            jnp.full((1, half), 1.0, jnp.float32) * upper_live,
        ],
        axis=1,
    )
    sign = signs.astype(jnp.float32) * live
    slots = corner_coupling.shape[1] // 2
    faces = corner_coupling[0].astype(jnp.float32).reshape(2, slots, half)
    maps = corner_map.astype(jnp.float32).reshape(2, slots)
    inner, outer = inner_pairs(count, groups), outer_pairs(count, groups)
    steps = rotations(count, groups)

    def split(low, up):
        return jnp.where(even, up, low), jnp.where(even, low, up)

    def joined(from_inner, from_outer):
        return jnp.where(even, from_outer, from_inner), jnp.where(even, from_inner, from_outer)

    def permute(values, pairs):
        return lax.ppermute(values, AXES, pairs)

    def region(values, low, up):
        to_inner, to_outer = split(low, up)
        from_outer = permute(to_outer, outer)
        lanes = values.shape[1]
        got = permute(jnp.concatenate([values, to_inner], axis=1), inner)
        values, from_inner = values + got[:, :lanes], got[:, lanes:]
        for turns in steps:
            values = values + sum(permute(values, pairs) for pairs in turns)
        return values, *joined(from_inner, from_outer)

    def beside(values):
        to_inner, to_outer = split(values[:, :half], values[:, half:])
        from_outer = permute(to_outer, outer)
        return jnp.concatenate(joined(permute(to_inner, inner), from_outer), axis=1)

    def block_product(values, blocks):
        return lax.dot_general(
            values.astype(jnp.bfloat16), blocks[0], NT, preferred_element_type=jnp.float32
        )

    def dots(first, second):
        return lax.dot_general(first, second, NT, precision=HIGHEST)

    def combine(weights, values):
        return lax.dot_general(weights, values, TN, precision=HIGHEST)

    def onehot_of(rows):
        index = jnp.arange(corners, dtype=jnp.int32)[None, :].astype(jnp.float32)
        return (rows.reshape(-1)[:, None] == index).astype(jnp.float32)

    onehot = onehot_of(maps)

    def corner_part(values):
        low = dots(values[:, :half], faces[0])
        up = dots(values[:, half:], faces[1])
        return jnp.dot(jnp.concatenate([low, up], axis=1), onehot, precision=HIGHEST)

    def spread(solved, chosen, blocks):
        picked = dots(solved, chosen)
        return jnp.concatenate(
            [
                jnp.dot(picked[:, :slots], blocks[0], precision=HIGHEST),
                jnp.dot(picked[:, slots:], blocks[1], precision=HIGHEST),
            ],
            axis=1,
        )

    def extras(face):
        map_row = jnp.pad(maps[face][None], ((0, 0), (0, half - slots)))
        fill = jnp.zeros((nrhs - slots - 1, half), jnp.float32)
        return jnp.concatenate([faces[face], map_row, fill], axis=0)

    residual = sign * dual_rhs[0]
    product = block_product(residual, prec_ops)
    precond = live * (product - beside(product))
    image_local = block_product(precond, dual_ops)
    grams = jnp.concatenate([dots(residual, precond), dots(precond, image_local)], axis=1)
    payload = jnp.concatenate([corner_part(precond), grams], axis=1)
    payload = jnp.pad(payload, ((0, 0), (0, -payload.shape[1] % 128)))
    summed, low, up = region(
        payload,
        jnp.concatenate([image_local[:, :half], extras(0)], axis=1),
        jnp.concatenate([image_local[:, half:], extras(1)], axis=1),
    )
    image_beside = jnp.concatenate([low[:, :half], up[:, :half]], axis=1)
    faces_beside = (low[:slots, half:], up[:slots, half:])
    onehot_beside = onehot_of(jnp.stack([low[slots, half : half + slots], up[slots, half : half + slots]]))
    corner_sum = summed[:, :corners]
    gram_old = summed[:, corners : corners + nrhs]
    solved = dots(corner_sum, coarse_inverse)
    energy = 2.0 * (summed[:, corners + nrhs : corners + 2 * nrhs] + dots(corner_sum, solved))
    alpha = gram_solve(energy, gram_old)
    image_part = live * (image_local - image_beside)
    image = image_part + live * (
        spread(solved, onehot, faces) - spread(solved, onehot_beside, faces_beside)
    )
    multipliers = combine(alpha, precond)
    residual = residual - combine(alpha, image)
    direction, image_dir_part = precond, image_part
    energy_local = summed[:, corners + nrhs : corners + 2 * nrhs]

    product = block_product(residual, prec_ops)
    precond = live * (product - beside(product))
    new_local = block_product(precond, dual_ops)
    grams = jnp.concatenate(
        [
            dots(residual, precond),
            dots(precond, new_local),
            dots(direction, new_local) + dots(image_local, precond),
        ],
        axis=1,
    )
    payload = jnp.concatenate([corner_part(precond), grams], axis=1)
    payload = jnp.pad(payload, ((0, 0), (0, -payload.shape[1] % 128)))
    summed, low, up = region(payload, new_local[:, :half], new_local[:, half:])
    gram_new = summed[:, corners : corners + nrhs]
    new_new = summed[:, corners + nrhs : corners + 2 * nrhs]
    old_new = summed[:, corners + 2 * nrhs : corners + 3 * nrhs]
    beta = gram_solve(gram_old, gram_new)
    corner_sum = summed[:, :corners] + combine(beta, corner_sum)
    solved = dots(corner_sum, coarse_inverse)
    energy = 2.0 * (
        new_new
        + combine(beta, old_new)
        + combine(beta, jnp.dot(energy_local, beta, precision=HIGHEST))
        + dots(corner_sum, solved)
    )
    alpha = gram_solve(energy, gram_new)
    direction = precond + combine(beta, direction)
    image = (
        live * (new_local - jnp.concatenate([low, up], axis=1))
        + combine(beta, image_dir_part)
        + live * (spread(solved, onehot, faces) - spread(solved, onehot_beside, faces_beside))
    )
    multipliers = multipliers + combine(alpha, direction)
    residual = residual - combine(alpha, image)
    return (sign * multipliers)[None], (sign * residual)[None]


def solution(mesh):
    in_specs = (
        P("grp", None, "blk"),
        P("grp", "blk", None),
        P("grp", "blk", None),
        P("grp", "blk", None),
        P("grp", "blk"),
        P("grp", "blk"),
        P(),
    )
    out_specs = (P("grp", None, "blk"), P("grp", None, "blk"))
    return jax.shard_map(
        functools.partial(local, mesh.shape["blk"], mesh.shape["grp"]),
        mesh=mesh,
        in_specs=in_specs,
        out_specs=out_specs,
        check_vma=False,
    )
```

time: 225 us -> 80.4 us (0.36)
  blocking collectives: 167 us -> 0 us
  starting transfers between devices: 11.4 us -> 24.2 us
  matrix products: 16.6 us -> 21.3 us
  waiting for transfers between devices: 14.8 us -> 18.2 us
    psum x4 -> x0, blocking collectives: 167 us -> none  [region(): return lax.psum(values, ('blk', 'grp'))]
    ppermute x8 -> x16, starting transfers between devices: 11.4 us -> 24.2 us  [permute(): return lax.ppermute(values, AXES, pairs)]
    dot_general x28 -> x42, matrix products: 15.6 us -> 20.3 us  [the longest x4 7.58 us: block_product(): lax.dot_general(values.astype(jnp.bfloat16), blocks[0], NT, preferred_ele...]
    ppermute x8 -> x16, waiting for transfers between devices: 14.8 us -> 18.2 us  [permute(): return lax.ppermute(values, AXES, pairs)]
  transfers between devices with their start and end apart: 8 -> 16, of which waited for: 4 -> 11; matrix products, arithmetic and copies ran while one was open for 1% -> 5% of each run, Pallas kernels for 0% -> 0%
where the time goes in v1:
time: 80.4 us; the launch traced here: 79.2 us
  starting transfers between devices  24.2 us (30%)
  matrix products  21.3 us (26%)
  waiting for transfers between devices  18.2 us (23%)
  other arithmetic  13.5 us (17%)
  between operations  1.02 us (1%)
  local copies, waits for them, and re-layouts  0.88 us (1%)
    ppermute x16, starting transfers between devices, permute(): return lax.ppermute(values, AXES, pairs)  24.2 us
    ppermute x16, waiting for transfers between devices, permute(): return lax.ppermute(values, AXES, pairs)  18.2 us
    dot_general x4, matrix products, block_product(): lax.dot_general(values.astype(jnp.bfloat16), blocks[0], NT, preferred_ele...  7.58 us
    dot_general x18, matrix products, dots(): return lax.dot_general(first, second, NT, precision=HIGHEST)  6.9 us
    another operation x9, other arithmetic, gram_solve(): factor = jnp.linalg.cholesky(balanced)  6.38 us
    another operation x6, other arithmetic, gram_solve(): lax.linalg.triangular_solve(factor, middle, left_side=True, lower=True, t...  5.63 us
    dot_general x9, matrix products, combine(): return lax.dot_general(weights, values, TN, precision=HIGHEST)  3.54 us
  transfers between devices with their start and end apart: 16, of which 11 were waited for; matrix products, arithmetic and copies ran while one was open for 5% of the time, Pallas kernels for 0%

profile of v1, /device:TPU:0, one launch (start us, length us, event | category | flops | bytes accessed | tf_op | source)
XLA Modules:
  0.0 79.2 jit_solution(3025204313616055757)
XLA Ops:
  0.7 0.8 %convert_multiply_fusion = f32[1,1024]{1,0:T(1,128)S(1)} fusion(f32[1,1024]{1,0:T(1,128)S(1)} %bitcast.135, s32[1,1024]{1,0:T(1,128)} %param.17), kind=kLoop, calls=%fused_computation.224 | loop fusion | flops 2048 | bytes 12288 | tf_op jit(solution)/shard_map/mul | solution.py:126
  1.6 2.4 %fusion.6 = f32[16,1024]{1,0:T(8,128)S(1)} fusion(bf16[1,1024,1024]{2,1,0:T(8,128)(2,1)} %param.14, f32[1,16,1024]{2,1,0:T(8,128)} %param.12, f32[1024]{0:T(1024)S(1)} %bitcast.136), kind=kOutput, calls=%fused_computation.6 | convolution fusion | flops 33587200 | bytes 2232320 | tf_op jit(solution)/shard_map/dot_general | solution.py:158
  4.0 3.0 %collective-permute-start = (f32[16,512]{1,0:T(8,128)S(1)}, f32[16,512]{1,0:T(8,128)S(1)}, u32[]{:S(2)}, u32[]{:S(2)}) collective-permute-start(f32[16,512]{1,0:T(8,128)S(1)} %get-tuple-element.21), channel_id=1, source_target_pairs={{0,1},{1,0},{2,4},{3,5},{4,2},{5,3},{6,8},{7,9},{8,6},{9,7},{10,12... | collective-permute-start | bytes 98312 | tf_op jit(solution)/shard_map/ppermute | solution.py:140
  7.3 1.6 %collective-permute-done = f32[16,512]{1,0:T(8,128)S(1)} collective-permute-done((f32[16,512]{1,0:T(8,128)S(1)}, f32[16,512]{1,0:T(8,128)S(1)}, u32[]{:S(2)}, u32[]{:S(2)}) %collective-permute-start) | collective-permute-done | bytes 32800 | tf_op jit(solution)/shard_map/ppermute | solution.py:140
  9.4 0.7 fusion.2
  10.9 1.2 %collective-permute-done.2 = f32[16,1920]{1,0:T(8,128)S(1)} collective-permute-done((f32[16,1920]{1,0:T(8,128)S(1)}, f32[16,1920]{1,0:T(8,128)S(1)}, u32[]{:S(2)}, u32[]{:S(2)}) %collective-permute-start.2) | collective-permute-done | bytes 122912 | tf_op jit(solution)/shard_map/ppermute | solution.py:140
  12.2 1.8 %collective-permute-start.3 = (f32[16,896]{1,0:T(8,128)S(1)}, f32[16,896]{1,0:T(8,128)S(1)}, u32[]{:S(2)}, u32[]{:S(2)}) collective-permute-start(f32[16,896]{1,0:T(8,128)S(1)} %slice_add_fusion.1), channel_id=1, source_target_pairs={{0,6},{1,7},{2,4},{3,5},{4,2},{5,3},{6,0},{7,1},{8,14},{9,15},{10,... | collective-permute-start | bytes 172040 | tf_op jit(solution)/shard_map/ppermute | solution.py:140
  14.0 1.5 %collective-permute-start.7 = (f32[16,1024]{1,0:T(8,128)S(1)}, f32[16,1024]{1,0:T(8,128)S(1)}, u32[]{:S(2)}, u32[]{:S(2)}) collective-permute-start(f32[16,1024]{1,0:T(8,128)S(1)} %get-tuple-element.7), channel_id=1, source_target_pairs={{0,1},{1,0},{2,4},{3,5},{4,2},{5,3},{6,8},{7,9},{8,6},{9,7},{10,12... | collective-permute-start | bytes 196616 | tf_op jit(solution)/shard_map/ppermute | solution.py:140
  15.5 0.8 %collective-permute-done.3 = f32[16,896]{1,0:T(8,128)S(1)} collective-permute-done((f32[16,896]{1,0:T(8,128)S(1)}, f32[16,896]{1,0:T(8,128)S(1)}, u32[]{:S(2)}, u32[]{:S(2)}) %collective-permute-start.3) | collective-permute-done | bytes 57376 | tf_op jit(solution)/shard_map/ppermute | solution.py:140
  16.3 1.6 %collective-permute-start.4 = (f32[16,896]{1,0:T(8,128)S(1)}, f32[16,896]{1,0:T(8,128)S(1)}, u32[]{:S(2)}, u32[]{:S(2)}) collective-permute-start(f32[16,896]{1,0:T(8,128)S(1)} %add.97), channel_id=1, source_target_pairs={{0,3},{1,2},{2,1},{3,0},{4,7},{5,6},{6,5},{7,4},{8,11},{9,10},{10,... | collective-permute-start | bytes 172040 | tf_op jit(solution)/shard_map/ppermute | solution.py:140
  17.9 2.3 %collective-permute-done.4 = f32[16,896]{1,0:T(8,128)S(1)} collective-permute-done((f32[16,896]{1,0:T(8,128)S(1)}, f32[16,896]{1,0:T(8,128)S(1)}, u32[]{:S(2)}, u32[]{:S(2)}) %collective-permute-start.4) | collective-permute-done | bytes 57376 | tf_op jit(solution)/shard_map/ppermute | solution.py:140
  20.2 2.0 %collective-permute-start.5 = (f32[16,896]{1,0:T(8,128)S(1)}, f32[16,896]{1,0:T(8,128)S(1)}, u32[]{:S(2)}, u32[]{:S(2)}) collective-permute-start(f32[16,896]{1,0:T(8,128)S(1)} %add.98), channel_id=1, source_target_pairs={{0,10},{1,11},{2,8},{3,9},{4,14},{5,15},{6,12},{7,13},{8,2},{9,3},... | collective-permute-start | bytes 172040 | tf_op jit(solution)/shard_map/ppermute | solution.py:140
  22.3 1.9 %collective-permute-done.5 = f32[16,896]{1,0:T(8,128)S(1)} collective-permute-done((f32[16,896]{1,0:T(8,128)S(1)}, f32[16,896]{1,0:T(8,128)S(1)}, u32[]{:S(2)}, u32[]{:S(2)}) %collective-permute-start.5) | collective-permute-done | bytes 57376 | tf_op jit(solution)/shard_map/ppermute | solution.py:140
  24.3 3.0 %collective-permute-start.6 = (f32[16,896]{1,0:T(8,128)S(1)}, f32[16,896]{1,0:T(8,128)S(1)}, u32[]{:S(2)}, u32[]{:S(2)}) collective-permute-start(f32[16,896]{1,0:T(8,128)S(1)} %add.99), channel_id=1, source_target_pairs={{0,18},{1,19},{2,16},{3,17},{4,22},{5,23},{6,20},{7,21},{8,26},{9,... | collective-permute-start | bytes 172040 | tf_op jit(solution)/shard_map/ppermute | solution.py:140
  27.3 1.9 %collective-permute-done.6 = f32[16,896]{1,0:T(8,128)S(1)} collective-permute-done((f32[16,896]{1,0:T(8,128)S(1)}, f32[16,896]{1,0:T(8,128)S(1)}, u32[]{:S(2)}, u32[]{:S(2)}) %collective-permute-start.6) | collective-permute-done | bytes 57376 | tf_op jit(solution)/shard_map/ppermute | solution.py:140
  29.3 2.0 %fusion.57 = f32[16,768]{1,0:T(8,128)S(1)} fusion(f32[768,768]{1,0:T(8,128)S(1)} %copy-done, f32[16,896]{1,0:T(8,128)S(1)} %add.100), kind=kOutput, calls=%fused_computation.89 | convolution fusion | flops 113246208 | bytes 2457600 | tf_op jit(solution)/shard_map/dot_general | solution.py:163
  33.0 1.5 %cholesky.59 = f32[16,16]{1,0:T(8,128)S(1)} custom-call(f32[16,16]{1,0:T(8,128)S(1)} %copy.12), custom_call_target="Cholesky" | custom-call | tf_op jit(solution)/shard_map/jit(cholesky)/cholesky | solution.py:106
  34.5 0.6 compare_reduce_fusion.2
  35.2 0.6 fusion.121
  35.8 1.2 %custom-call.13 = f32[1,16,16]{1,2,0:T(8,128)S(1)} custom-call(f32[1,16,16]{2,1,0:T(8,128)S(1)} %fusion.121), custom_call_target="InvertDiagBlocksLowerTriangular" | custom-call | tf_op jit(solution)/shard_map/triangular_solve/custom-call.2 | solution.py:108
  37.4 0.3 fusion.174
  37.9 2.2 %fusion.4 = f32[16,1024]{1,0:T(8,128)S(1)} fusion(bf16[1,1024,1024]{2,1,0:T(8,128)(2,1)} %param.14, f32[16,1024]{1,0:T(8,128)S(1)} %convolution_subtract_fusion.1), kind=kOutput, calls=%fused_computation.4 | convolution fusion | flops 33570816 | bytes 2228224 | tf_op jit(solution)/shard_map/dot_general | solution.py:158
  40.2 1.6 %collective-permute-start.8 = (f32[16,512]{1,0:T(8,128)S(1)}, f32[16,512]{1,0:T(8,128)S(1)}, u32[]{:S(2)}, u32[]{:S(2)}) collective-permute-start(f32[16,512]{1,0:T(8,128)S(1)} %get-tuple-element.15), channel_id=1, source_target_pairs={{0,1},{1,0},{2,4},{3,5},{4,2},{5,3},{6,8},{7,9},{8,6},{9,7},{10,12... | collective-permute-start | bytes 98312 | tf_op jit(solution)/shard_map/ppermute | solution.py:140
  41.9 2.3 %collective-permute-done.8 = f32[16,512]{1,0:T(8,128)S(1)} collective-permute-done((f32[16,512]{1,0:T(8,128)S(1)}, f32[16,512]{1,0:T(8,128)S(1)}, u32[]{:S(2)}, u32[]{:S(2)}) %collective-permute-start.8) | collective-permute-done | bytes 32800 | tf_op jit(solution)/shard_map/ppermute | solution.py:140
  44.7 2.3 %fusion = f32[16,1024]{1,0:T(8,128)S(1)} fusion(bf16[1,1024,1024]{2,1,0:T(8,128)(2,1)} %param.13, f32[16,1024]{1,0:T(8,128)S(1)} %fusion.37), kind=kOutput, calls=%fused_computation | convolution fusion | flops 33570816 | bytes 2228224 | tf_op jit(solution)/shard_map/dot_general | solution.py:158
  48.1 1.4 %cholesky.70 = f32[16,16]{1,0:T(8,128)S(1)} custom-call(f32[16,16]{1,0:T(8,128)S(1)} %fusion.152), custom_call_target="Cholesky" | custom-call | tf_op jit(solution)/shard_map/jit(cholesky)/cholesky | solution.py:106
  49.6 2.9 %collective-permute-start.11 = (f32[16,896]{1,0:T(8,128)S(1)}, f32[16,896]{1,0:T(8,128)S(1)}, u32[]{:S(2)}, u32[]{:S(2)}) collective-permute-start(f32[16,896]{1,0:T(8,128)S(1)} %slice_add_fusion), channel_id=1, source_target_pairs={{0,6},{1,7},{2,4},{3,5},{4,2},{5,3},{6,0},{7,1},{8,14},{9,15},{10,... | collective-permute-start | bytes 172040 | tf_op jit(solution)/shard_map/ppermute | solution.py:140
  52.5 2.1 %collective-permute-done.11 = f32[16,896]{1,0:T(8,128)S(1)} collective-permute-done((f32[16,896]{1,0:T(8,128)S(1)}, f32[16,896]{1,0:T(8,128)S(1)}, u32[]{:S(2)}, u32[]{:S(2)}) %collective-permute-start.11) | collective-permute-done | bytes 57376 | tf_op jit(solution)/shard_map/ppermute | solution.py:140
  54.6 1.1 %collective-permute-start.12 = (f32[16,896]{1,0:T(8,128)S(1)}, f32[16,896]{1,0:T(8,128)S(1)}, u32[]{:S(2)}, u32[]{:S(2)}) collective-permute-start(f32[16,896]{1,0:T(8,128)S(1)} %add.106), channel_id=1, source_target_pairs={{0,3},{1,2},{2,1},{3,0},{4,7},{5,6},{6,5},{7,4},{8,11},{9,10},{10,... | collective-permute-start | bytes 172040 | tf_op jit(solution)/shard_map/ppermute | solution.py:140
  55.7 0.6 compare_reduce_fusion.1
  56.4 0.8 collective-permute-start.15
  57.2 1.2 %collective-permute-done.12 = f32[16,896]{1,0:T(8,128)S(1)} collective-permute-done((f32[16,896]{1,0:T(8,128)S(1)}, f32[16,896]{1,0:T(8,128)S(1)}, u32[]{:S(2)}, u32[]{:S(2)}) %collective-permute-start.12) | collective-permute-done | bytes 57376 | tf_op jit(solution)/shard_map/ppermute | solution.py:140
  58.4 1.7 %collective-permute-start.13 = (f32[16,896]{1,0:T(8,128)S(1)}, f32[16,896]{1,0:T(8,128)S(1)}, u32[]{:S(2)}, u32[]{:S(2)}) collective-permute-start(f32[16,896]{1,0:T(8,128)S(1)} %add.107), channel_id=1, source_target_pairs={{0,10},{1,11},{2,8},{3,9},{4,14},{5,15},{6,12},{7,13},{8,2},{9,3},... | collective-permute-start | bytes 172040 | tf_op jit(solution)/shard_map/ppermute | solution.py:140
  60.1 0.6 fusion.122
  60.7 1.2 %custom-call.15 = f32[1,16,16]{1,2,0:T(8,128)S(1)} custom-call(f32[1,16,16]{2,1,0:T(8,128)S(1)} %fusion.122), custom_call_target="InvertDiagBlocksLowerTriangular" | custom-call | tf_op jit(solution)/shard_map/triangular_solve/custom-call.2 | solution.py:108
  61.9 0.7 collective-permute-done.13
  62.6 2.9 %collective-permute-start.14 = (f32[16,896]{1,0:T(8,128)S(1)}, f32[16,896]{1,0:T(8,128)S(1)}, u32[]{:S(2)}, u32[]{:S(2)}) collective-permute-start(f32[16,896]{1,0:T(8,128)S(1)} %add.108), channel_id=1, source_target_pairs={{0,18},{1,19},{2,16},{3,17},{4,22},{5,23},{6,20},{7,21},{8,26},{9,... | collective-permute-start | bytes 172040 | tf_op jit(solution)/shard_map/ppermute | solution.py:140
  65.5 2.0 %collective-permute-done.14 = f32[16,896]{1,0:T(8,128)S(1)} collective-permute-done((f32[16,896]{1,0:T(8,128)S(1)}, f32[16,896]{1,0:T(8,128)S(1)}, u32[]{:S(2)}, u32[]{:S(2)}) %collective-permute-start.14) | collective-permute-done | bytes 57376 | tf_op jit(solution)/shard_map/ppermute | solution.py:140
  67.9 0.3 slice_add_fusion.2
  68.1 2.0 %fusion.179 = f32[16,768]{1,0:T(8,128)S(1)} fusion(f32[16,768]{1,0:T(8,128)S(1)} %slice_add_fusion.2, f32[768,768]{1,0:T(8,128)S(1)} %copy-done), kind=kOutput, calls=%fused_computation.245 | convolution fusion | flops 113246208 | bytes 2457600 | tf_op jit(solution)/shard_map/dot_general | solution.py:163
  70.8 0.3 fusion.110
  72.0 0.3 convolution_add_fusion.1
  73.0 1.5 %cholesky.81 = f32[16,16]{1,0:T(8,128)S(1)} custom-call(f32[16,16]{1,0:T(8,128)S(1)} %fusion.147), custom_call_target="Cholesky" | custom-call | tf_op jit(solution)/shard_map/jit(cholesky)/cholesky | solution.py:106
  74.5 0.6 compare_reduce_fusion
  75.1 0.6 fusion.123
  75.8 1.2 %custom-call.17 = f32[1,16,16]{1,2,0:T(8,128)S(1)} custom-call(f32[1,16,16]{2,1,0:T(8,128)S(1)} %fusion.123), custom_call_target="InvertDiagBlocksLowerTriangular" | custom-call | tf_op jit(solution)/shard_map/triangular_solve/custom-call.2 | solution.py:108
  77.4 0.9 %fusion.11 = f32[1,16,1024]{2,1,0:T(8,128)} fusion(f32[16,1024]{1,0:T(8,128)S(1)} %fusion.174, f32[16,16]{1,0:T(8,128)S(1)} %fusion.145, f32[16,1024]{1,0:T(8,128)S(1)} %convolution_add_fusion.1, f32[1024]{0:T(1024)S(1)} %bitcast.139), kind=kOutput, calls=%fused_computation.13 | convolution fusion | flops 3178496 | bytes 201728 | tf_op jit(solution)/shard_map/dot_general | solution.py:166
  78.3 0.9 %fusion.9 = f32[1,16,1024]{2,1,0:T(8,128)} fusion(f32[16,1024]{1,0:T(8,128)S(1)} %convolution_subtract_fusion.1, f32[16,16]{1,0:T(8,128)S(1)} %fusion.145, f32[16,1024]{1,0:T(8,128)S(1)} %fusion.110, f32[16,1024]{1,0:T(8,128)S(1)} %fusion, f32[16,512]{1,0:T(8,128)S(1)} %get-tuple-element.10, f32[16,512]{1,0:T(8,128)S(1)} %get-tuple-element.9, ...), kind=kOutput, calls=%fused_computation.10 | convolution fusion | flops 3325952 | bytes 467968 | tf_op jit(solution)/shard_map/dot_general | solution.py:166
  (113 shorter events, 8.9 us)
Async XLA Ops:
  0.6 28.6 %copy-start = (f32[768,768]{1,0:T(8,128)S(1)}, f32[768,768]{1,0:T(8,128)}, u32[]{:S(2)}) copy-start(f32[768,768]{1,0:T(8,128)} %param.18) | copy-start | bytes 7077892
  0.6 8.6 %copy-start.3 = (f32[1,16,1024]{2,1,0:T(8,128)S(1)}, f32[1,16,1024]{2,1,0:T(8,128)}, u32[]{:S(2)}) copy-start(f32[1,16,1024]{2,1,0:T(8,128)} %param.12) | copy-start | bytes 196612
  0.7 6.5 %copy-start.4 = (s32[1,24]{1,0:T(1,128)S(1)}, s32[1,24]{1,0:T(1,128)}, u32[]{:S(2)}) copy-start(s32[1,24]{1,0:T(1,128)} %param.16) | copy-start | bytes 292
  0.7 6.6 %copy-start.2 = (bf16[1,24,512]{2,1,0:T(8,128)(2,1)S(1)}, bf16[1,24,512]{2,1,0:T(8,128)(2,1)}, u32[]{:S(2)}) copy-start(bf16[1,24,512]{2,1,0:T(8,128)(2,1)} %param.15) | copy-start | bytes 73732
  0.7 8.7 %copy-start.1 = (bf16[1,1024,1024]{2,1,0:T(8,128)(2,1)S(1)}, bf16[1,1024,1024]{2,1,0:T(8,128)(2,1)}, u32[]{:S(2)}) copy-start(bf16[1,1024,1024]{2,1,0:T(8,128)(2,1)} %param.13) | copy-start | bytes 6291460
  4.0 4.9 %collective-permute-start = (f32[16,512]{1,0:T(8,128)S(1)}, f32[16,512]{1,0:T(8,128)S(1)}, u32[]{:S(2)}, u32[]{:S(2)}) collective-permute-start(f32[16,512]{1,0:T(8,128)S(1)} %get-tuple-element.21), channel_id=1, source_target_pairs={{0,1},{1,0},{2,4},{3,5},{4,2},{5,3},{6,8},{7,9},{8,6},{9,7},{10,12... | collective-permute-start | bytes 98312 | tf_op jit(solution)/shard_map/ppermute | solution.py:140
  7.0 1.9 %collective-permute-start.1 = (f32[16,512]{1,0:T(8,128)S(1)}, f32[16,512]{1,0:T(8,128)S(1)}, u32[]{:S(2)}, u32[]{:S(2)}) collective-permute-start(f32[16,512]{1,0:T(8,128)S(1)} %get-tuple-element.22), channel_id=1, source_target_pairs={{0,2},{1,3},{2,0},{3,1},{4,6},{5,7},{6,4},{7,5},{8,10},{9,11},{10,... | collective-permute-start | bytes 98312 | tf_op jit(solution)/shard_map/ppermute | solution.py:140
  10.7 1.4 %collective-permute-start.2 = (f32[16,1920]{1,0:T(8,128)S(1)}, f32[16,1920]{1,0:T(8,128)S(1)}, u32[]{:S(2)}, u32[]{:S(2)}) collective-permute-start(f32[16,1920]{1,0:T(8,128)S(1)} %pad_maximum_fusion), channel_id=1, source_target_pairs={{0,2},{1,3},{2,0},{3,1},{4,6},{5,7},{6,4},{7,5},{8,10},{9,11},{10,... | collective-permute-start | bytes 368648 | tf_op jit(solution)/shard_map/ppermute | solution.py:140
  12.2 4.1 %collective-permute-start.3 = (f32[16,896]{1,0:T(8,128)S(1)}, f32[16,896]{1,0:T(8,128)S(1)}, u32[]{:S(2)}, u32[]{:S(2)}) collective-permute-start(f32[16,896]{1,0:T(8,128)S(1)} %slice_add_fusion.1), channel_id=1, source_target_pairs={{0,6},{1,7},{2,4},{3,5},{4,2},{5,3},{6,0},{7,1},{8,14},{9,15},{10,... | collective-permute-start | bytes 172040 | tf_op jit(solution)/shard_map/ppermute | solution.py:140
  14.0 8.3 %collective-permute-start.7 = (f32[16,1024]{1,0:T(8,128)S(1)}, f32[16,1024]{1,0:T(8,128)S(1)}, u32[]{:S(2)}, u32[]{:S(2)}) collective-permute-start(f32[16,1024]{1,0:T(8,128)S(1)} %get-tuple-element.7), channel_id=1, source_target_pairs={{0,1},{1,0},{2,4},{3,5},{4,2},{5,3},{6,8},{7,9},{8,6},{9,7},{10,12... | collective-permute-start | bytes 196616 | tf_op jit(solution)/shard_map/ppermute | solution.py:140
  16.3 3.9 %collective-permute-start.4 = (f32[16,896]{1,0:T(8,128)S(1)}, f32[16,896]{1,0:T(8,128)S(1)}, u32[]{:S(2)}, u32[]{:S(2)}) collective-permute-start(f32[16,896]{1,0:T(8,128)S(1)} %add.97), channel_id=1, source_target_pairs={{0,3},{1,2},{2,1},{3,0},{4,7},{5,6},{6,5},{7,4},{8,11},{9,10},{10,... | collective-permute-start | bytes 172040 | tf_op jit(solution)/shard_map/ppermute | solution.py:140
  20.2 4.0 %collective-permute-start.5 = (f32[16,896]{1,0:T(8,128)S(1)}, f32[16,896]{1,0:T(8,128)S(1)}, u32[]{:S(2)}, u32[]{:S(2)}) collective-permute-start(f32[16,896]{1,0:T(8,128)S(1)} %add.98), channel_id=1, source_target_pairs={{0,10},{1,11},{2,8},{3,9},{4,14},{5,15},{6,12},{7,13},{8,2},{9,3},... | collective-permute-start | bytes 172040 | tf_op jit(solution)/shard_map/ppermute | solution.py:140
  24.3 5.0 %collective-permute-start.6 = (f32[16,896]{1,0:T(8,128)S(1)}, f32[16,896]{1,0:T(8,128)S(1)}, u32[]{:S(2)}, u32[]{:S(2)}) collective-permute-start(f32[16,896]{1,0:T(8,128)S(1)} %add.99), channel_id=1, source_target_pairs={{0,18},{1,19},{2,16},{3,17},{4,22},{5,23},{6,20},{7,21},{8,26},{9,... | collective-permute-start | bytes 172040 | tf_op jit(solution)/shard_map/ppermute | solution.py:140
  40.2 4.0 %collective-permute-start.8 = (f32[16,512]{1,0:T(8,128)S(1)}, f32[16,512]{1,0:T(8,128)S(1)}, u32[]{:S(2)}, u32[]{:S(2)}) collective-permute-start(f32[16,512]{1,0:T(8,128)S(1)} %get-tuple-element.15), channel_id=1, source_target_pairs={{0,1},{1,0},{2,4},{3,5},{4,2},{5,3},{6,8},{7,9},{8,6},{9,7},{10,12... | collective-permute-start | bytes 98312 | tf_op jit(solution)/shard_map/ppermute | solution.py:140
  41.8 2.4 %collective-permute-start.9 = (f32[16,512]{1,0:T(8,128)S(1)}, f32[16,512]{1,0:T(8,128)S(1)}, u32[]{:S(2)}, u32[]{:S(2)}) collective-permute-start(f32[16,512]{1,0:T(8,128)S(1)} %get-tuple-element.16), channel_id=1, source_target_pairs={{0,2},{1,3},{2,0},{3,1},{4,6},{5,7},{6,4},{7,5},{8,10},{9,11},{10,... | collective-permute-start | bytes 98312 | tf_op jit(solution)/shard_map/ppermute | solution.py:140
  48.0 1.5 %collective-permute-start.10 = (f32[16,1408]{1,0:T(8,128)S(1)}, f32[16,1408]{1,0:T(8,128)S(1)}, u32[]{:S(2)}, u32[]{:S(2)}) collective-permute-start(f32[16,1408]{1,0:T(8,128)S(1)} %pad_maximum_fusion.3), channel_id=1, source_target_pairs={{0,2},{1,3},{2,0},{3,1},{4,6},{5,7},{6,4},{7,5},{8,10},{9,11},{10,... | collective-permute-start | bytes 270344 | tf_op jit(solution)/shard_map/ppermute | solution.py:140
  49.6 5.0 %collective-permute-start.11 = (f32[16,896]{1,0:T(8,128)S(1)}, f32[16,896]{1,0:T(8,128)S(1)}, u32[]{:S(2)}, u32[]{:S(2)}) collective-permute-start(f32[16,896]{1,0:T(8,128)S(1)} %slice_add_fusion), channel_id=1, source_target_pairs={{0,6},{1,7},{2,4},{3,5},{4,2},{5,3},{6,0},{7,1},{8,14},{9,15},{10,... | collective-permute-start | bytes 172040 | tf_op jit(solution)/shard_map/ppermute | solution.py:140
  54.6 3.8 %collective-permute-start.12 = (f32[16,896]{1,0:T(8,128)S(1)}, f32[16,896]{1,0:T(8,128)S(1)}, u32[]{:S(2)}, u32[]{:S(2)}) collective-permute-start(f32[16,896]{1,0:T(8,128)S(1)} %add.106), channel_id=1, source_target_pairs={{0,3},{1,2},{2,1},{3,0},{4,7},{5,6},{6,5},{7,4},{8,11},{9,10},{10,... | collective-permute-start | bytes 172040 | tf_op jit(solution)/shard_map/ppermute | solution.py:140
  56.4 9.1 %collective-permute-start.15 = (f32[16,512]{1,0:T(8,128)S(1)}, f32[16,512]{1,0:T(8,128)S(1)}, u32[]{:S(2)}, u32[]{:S(2)}) collective-permute-start(f32[16,512]{1,0:T(8,128)S(1)} %get-tuple-element.11), channel_id=1, source_target_pairs={{0,1},{1,0},{2,4},{3,5},{4,2},{5,3},{6,8},{7,9},{8,6},{9,7},{10,12... | collective-permute-start | bytes 98312 | tf_op jit(solution)/shard_map/ppermute | solution.py:140
  58.4 4.2 %collective-permute-start.13 = (f32[16,896]{1,0:T(8,128)S(1)}, f32[16,896]{1,0:T(8,128)S(1)}, u32[]{:S(2)}, u32[]{:S(2)}) collective-permute-start(f32[16,896]{1,0:T(8,128)S(1)} %add.107), channel_id=1, source_target_pairs={{0,10},{1,11},{2,8},{3,9},{4,14},{5,15},{6,12},{7,13},{8,2},{9,3},... | collective-permute-start | bytes 172040 | tf_op jit(solution)/shard_map/ppermute | solution.py:140
  62.6 4.9 %collective-permute-start.14 = (f32[16,896]{1,0:T(8,128)S(1)}, f32[16,896]{1,0:T(8,128)S(1)}, u32[]{:S(2)}, u32[]{:S(2)}) collective-permute-start(f32[16,896]{1,0:T(8,128)S(1)} %add.108), channel_id=1, source_target_pairs={{0,18},{1,19},{2,16},{3,17},{4,22},{5,23},{6,20},{7,21},{8,26},{9,... | collective-permute-start | bytes 172040 | tf_op jit(solution)/shard_map/ppermute | solution.py:140

commit v2 on v1

v2 whole, which is shorter than its diff:
```python
import functools

import jax
import jax.numpy as jnp
from jax import lax
from jax.experimental import pallas as pl
from jax.experimental.pallas import tpu as pltpu
from jax.sharding import PartitionSpec as P

AXES = ("blk", "grp")
NN = (((1,), (0,)), ((), ()))
NT = (((1,), (1,)), ((), ()))
TN = (((0,), (0,)), ((), ()))
F32 = jnp.float32
BF16 = jnp.bfloat16


def radices(count):
    found = []
    factor = 2
    while count > 1:
        while count % factor == 0:
            found.append(factor)
            count //= factor
        factor += 1
    return found


def swap(count, groups, partner):
    pairs = []
    for blk in range(count):
        for grp in range(groups):
            other = partner(blk)
            if 0 <= other < count:
                target = other * groups + grp
            elif grp ^ 1 < groups:
                target = blk * groups + (grp ^ 1)
            else:
                target = blk * groups + grp
            pairs.append((blk * groups + grp, target))
    return pairs


def inner_pairs(count, groups):
    return swap(count, groups, lambda blk: blk ^ 1)


def outer_pairs(count, groups):
    return swap(count, groups, lambda blk: blk + 1 if blk % 2 == 1 else blk - 1)


def rotations(count, groups):
    core = 2 if count % 2 == 0 else 1
    steps = []

    def flipped(blk, turn):
        return (blk ^ 1) if (core == 2 and turn) else blk

    def add_axis(step_target, factor):
        steps.append(
            [
                [
                    (blk * groups + grp, step_target(blk, grp, turn))
                    for blk in range(count)
                    for grp in range(groups)
                ]
                for turn in range(1, factor)
            ]
        )

    stride = 1
    blk_steps = []
    for factor in radices(count // core):
        blk_steps.append((stride, factor))
        stride *= factor
    grp_steps = []
    stride = 1
    for factor in radices(groups):
        grp_steps.append((stride, factor))
        stride *= factor

    def blk_target(stride, factor):
        def target(blk, grp, turn):
            chip = blk // core
            digit = (chip // stride) % factor
            moved = chip + ((digit + turn) % factor - digit) * stride
            return flipped(moved * core + blk % core, turn) * groups + grp

        return target

    def grp_target(stride, factor):
        def target(blk, grp, turn):
            digit = (grp // stride) % factor
            moved = grp + ((digit + turn) % factor - digit) * stride
            return flipped(blk, turn) * groups + moved

        return target

    for stride, factor in blk_steps[:1]:
        add_axis(blk_target(stride, factor), factor)
    for stride, factor in grp_steps:
        add_axis(grp_target(stride, factor), factor)
    for stride, factor in blk_steps[1:]:
        add_axis(blk_target(stride, factor), factor)
    return steps


def mm(first, second, dims):
    return lax.dot_general(first, second, dims, preferred_element_type=F32)


def halves(values):
    high = values.astype(BF16)
    return high, (values - high.astype(F32)).astype(BF16)


def stacked(values):
    return jnp.concatenate(halves(values), axis=0)


def folded(rows):
    count = rows.shape[0] // 2
    return rows[:count] + rows[count:]


def dots(first, second):
    product = folded(mm(stacked(first), stacked(second), NT))
    count = second.shape[0]
    return product[:, :count] + product[:, count:]


def combine(weights, values):
    weight_high, weight_low = halves(weights)
    high, low = halves(values)
    left = jnp.concatenate([weight_high, weight_high, weight_low, weight_low], axis=0)
    right = jnp.concatenate([high, low, high, low], axis=0)
    return mm(left, right, TN)


def against(values, exact):
    return folded(mm(stacked(values), exact, NN))


def lanes_of(shape):
    return lax.broadcasted_iota(jnp.int32, shape, len(shape) - 1)


def chosen(row, corners):
    shape = (corners, row.shape[1])
    return (lax.broadcasted_iota(jnp.int32, shape, 0) == row).astype(BF16)


def live_mask(blk, count, width):
    lane = lanes_of((1, width))
    low = (blk > 0).astype(F32)
    up = (blk < count - 1).astype(F32)
    return jnp.where(lane < width // 2, low, up)


def split(even, low, up):
    return jnp.where(even, up, low), jnp.where(even, low, up)


def joined(even, from_inner, from_outer):
    low = jnp.where(even, from_outer, from_inner)
    up = jnp.where(even, from_inner, from_outer)
    return jnp.concatenate([low, up], axis=1)


def transposed(matrix):
    return matrix.T


def eliminate(matrix, target):
    count = matrix.shape[0]
    work = jnp.concatenate([matrix, target], axis=1)
    row_index = lax.broadcasted_iota(jnp.int32, (count, 1), 0)
    for step in range(count):
        row = work[step : step + 1, :]
        scaled = row * (1.0 / work[step : step + 1, step : step + 1])
        column = work[:, step : step + 1]
        work = jnp.where(row_index == step, scaled, work - column * scaled)
    return work[:, count:]


def symmetric(matrix):
    return 0.5 * (matrix + transposed(matrix))


def corner_values(values, couple, own_choice):
    half = values.shape[1] // 2
    both = stacked(values)
    low = folded(mm(both[:, :half], couple, NT))
    up = folded(mm(both[:, half:], couple, NT))
    mine = jnp.where(lanes_of(low.shape) < couple.shape[0] // 2, low, up)
    return folded(mm(stacked(mine), own_choice, NT))


def coarse_spread(solved, couple, own_row, beside):
    corners = solved.shape[1]
    slots = couple.shape[0] // 2
    half = couple.shape[1]
    both = stacked(solved)
    picked = folded(mm(both, chosen(own_row, corners), NN))
    lane = lanes_of(picked.shape)
    low = jnp.where(lane < slots, picked, 0.0)
    up = jnp.where(lane < slots, 0.0, picked)
    own_low = against(low, couple)
    own_up = against(up, couple)
    others = []
    for face in (beside[:, :half], beside[:, half:]):
        row = face[slots : slots + 1, : face.shape[0]]
        valid = lanes_of(row.shape) < slots
        choice = chosen(jnp.where(valid, row, -1.0).astype(jnp.int32), corners)
        others.append(against(folded(mm(both, choice, NN)), face.astype(BF16)))
    return jnp.concatenate([own_low - others[0], own_up - others[1]], axis=1)


def coarse_solve(corner_sum, parts):
    high, low = parts
    first = folded(mm(stacked(corner_sum), high, NN))
    return first + mm(corner_sum.astype(BF16), low, NN)


def start_kernel(count, rhs, signs, blocks, product, to_inner, to_outer, held, sems):
    rows = held.shape[1]
    copies = [
        pltpu.make_async_copy(blocks.at[0, pl.ds(part * rows, rows)], held.at[part], sems.at[part])
        for part in range(held.shape[0])
    ]
    for copy in copies:
        copy.start()
    blk = lax.axis_index("blk")
    width = rhs.shape[2]
    sign = signs[...].astype(F32) * live_mask(blk, count, width)
    rounded = (sign * rhs[0]).astype(BF16)
    total = jnp.zeros((rhs.shape[1], width), F32)
    for part, copy in enumerate(copies):
        copy.wait()
        total = total + mm(rounded[:, part * rows : (part + 1) * rows], held[part], NN)
    product[...] = total
    inner, outer = split(blk % 2 == 0, total[:, : width // 2], total[:, width // 2 :])
    to_inner[...] = inner
    to_outer[...] = outer


def first_kernel(
    count, corners, product, from_inner, from_outer, rhs, signs, blocks, coupling, corner_map,
    precond_out, image_out, to_inner, to_outer,
):
    blk = lax.axis_index("blk")
    even = blk % 2 == 0
    nrhs, width = product.shape
    half = width // 2
    live = live_mask(blk, count, width)
    residual = signs[...].astype(F32) * live * rhs[0]
    precond = live * (product[...] - joined(even, from_inner[...], from_outer[...]))
    image = mm(precond.astype(BF16), blocks[0], NN)
    precond_out[...] = precond
    image_out[...] = image
    couple = coupling[0]
    slots = couple.shape[0] // 2
    lanes = to_inner.shape[1] - width
    to_inner[:, :corners] = corner_values(precond, couple, chosen(corner_map[...], corners))
    grams = dots(jnp.concatenate([residual, precond], axis=0), jnp.concatenate([precond, image], axis=0))
    to_inner[:, corners:lanes] = jnp.concatenate(
        [grams[:nrhs, :nrhs], grams[nrhs:, nrhs:], jnp.zeros((nrhs, lanes - corners - 2 * nrhs), F32)], axis=1
    )
    inner, outer = split(even, image[:, :half], image[:, half:])
    to_inner[:, lanes : lanes + half] = inner
    to_outer[:, :half] = outer
    wide = couple.astype(F32)
    row = jnp.concatenate([corner_map[...].astype(F32), jnp.zeros((1, half - 2 * slots), F32)], axis=1)
    low, up = wide[:slots], wide[slots:]
    low_row, up_row = row, pltpu.roll(row, half - slots, 1)
    fill = jnp.zeros((nrhs - slots - 1, half), F32)
    inner, outer = split(
        even,
        jnp.concatenate([low, low_row, fill], axis=0),
        jnp.concatenate([up, up_row, fill], axis=0),
    )
    to_inner[:, lanes + half :] = inner
    to_outer[:, half:] = outer


def prepare_kernel(coarse, high, low):
    top, rest = halves(coarse[...])
    high[...] = top
    low[...] = rest


def middle_kernel(
    count, corners, summed_a, summed_b, got, from_outer, precond, image, rhs, signs, blocks, coupling, corner_map,
    coarse_high, coarse_low,
    sums_out, solved_out, residual_out, image_out, product_out, small_out, beside_out, to_inner, to_outer,
):
    blk = lax.axis_index("blk")
    even = blk % 2 == 0
    nrhs, width = precond.shape
    half = width // 2
    live = live_mask(blk, count, width)
    lanes = summed_a.shape[1]
    summed = summed_a[...] + summed_b[...]
    corner_sum = summed[:, :corners]
    gram = summed[:, corners : corners + nrhs]
    local_energy = summed[:, corners + nrhs : corners + 2 * nrhs]
    solved = coarse_solve(corner_sum, (coarse_high[...], coarse_low[...]))
    energy = local_energy + dots(corner_sum, solved)
    alpha = eliminate(symmetric(2.0 * energy), gram)
    inner_got = got[:, lanes:]
    outer_got = from_outer[...]
    image_beside = joined(even, inner_got[:, :half], outer_got[:, :half])
    beside = joined(even, inner_got[:, half:], outer_got[:, half:])
    whole = live * (
        image[...] - image_beside + coarse_spread(solved, coupling[0], corner_map[...], beside)
    )
    residual = signs[...].astype(F32) * live * rhs[0] - combine(alpha, whole)
    product = mm(residual.astype(BF16), blocks[0], NN)
    inner, outer = split(even, product[:, :half], product[:, half:])
    to_inner[...] = inner
    to_outer[...] = outer
    sums_out[...] = corner_sum
    solved_out[...] = solved
    residual_out[...] = residual
    image_out[...] = whole
    product_out[...] = product
    small_out[...] = jnp.concatenate([gram, energy, alpha, jnp.zeros((nrhs, 128 - 3 * nrhs), F32)], axis=1)
    beside_out[...] = beside


def invert_kernel(small, inverse):
    nrhs = small.shape[0]
    row = lax.broadcasted_iota(jnp.int32, (nrhs, nrhs), 0)
    unit = (row == lanes_of((nrhs, nrhs))).astype(F32)
    inverse[...] = eliminate(symmetric(small[:, :nrhs]), unit)


def second_kernel(
    count, corners, product, from_inner, from_outer, residual, old_precond, old_image, blocks, coupling, corner_map,
    precond_out, image_out, to_inner, to_outer,
):
    blk = lax.axis_index("blk")
    even = blk % 2 == 0
    nrhs, width = product.shape
    half = width // 2
    live = live_mask(blk, count, width)
    precond = live * (product[...] - joined(even, from_inner[...], from_outer[...]))
    image = mm(precond.astype(BF16), blocks[0], NN)
    precond_out[...] = precond
    image_out[...] = image
    inner, outer = split(even, image[:, :half], image[:, half:])
    lanes = to_inner.shape[1] - half
    to_inner[:, lanes:] = inner
    to_outer[...] = outer
    to_inner[:, :corners] = corner_values(precond, coupling[0], chosen(corner_map[...], corners))
    left = jnp.concatenate([residual[...], precond, old_precond[...], old_image[...]], axis=0)
    grams = dots(left, jnp.concatenate([precond, image], axis=0))
    to_inner[:, corners:lanes] = jnp.concatenate(
        [
            grams[:nrhs, :nrhs],
            grams[nrhs : 2 * nrhs, nrhs:],
            grams[2 * nrhs : 3 * nrhs, nrhs:] + grams[3 * nrhs :, :nrhs],
            jnp.zeros((nrhs, lanes - corners - 3 * nrhs), F32),
        ],
        axis=1,
    )


def final_kernel(
    count, corners, summed_a, summed_b, got, from_outer, precond, image, residual, old_precond, old_image, old_sums,
    old_solved, small, inverse, beside, signs, coupling, corner_map, coarse_high, coarse_low,
    multipliers_out, residual_out,
):
    blk = lax.axis_index("blk")
    even = blk % 2 == 0
    nrhs, width = precond.shape
    live = live_mask(blk, count, width)
    lanes = summed_a.shape[1]
    summed = summed_a[...] + summed_b[...]
    corner_sum = summed[:, :corners]
    gram = summed[:, corners : corners + nrhs]
    new_new = summed[:, corners + nrhs : corners + 2 * nrhs]
    old_new = summed[:, corners + 2 * nrhs : corners + 3 * nrhs]
    beta = combine(inverse[...], gram)
    solved = coarse_solve(corner_sum, (coarse_high[...], coarse_low[...]))
    cross = dots(
        jnp.concatenate([corner_sum, old_sums[...]], axis=0),
        jnp.concatenate([solved, old_solved[...]], axis=0),
    )
    new_new = new_new + cross[:nrhs, :nrhs]
    old_new = old_new + cross[nrhs:, :nrhs] + transposed(cross[:nrhs, nrhs:])
    old_old = symmetric(small[:, nrhs : 2 * nrhs])
    energy = new_new + combine(beta, old_new + combine(old_old, beta))
    alpha = eliminate(symmetric(2.0 * energy), gram)
    image_beside = joined(even, got[:, lanes:], from_outer[...])
    whole = live * (
        image[...] - image_beside + coarse_spread(solved, coupling[0], corner_map[...], beside[...])
    )
    carried = combine(transposed(beta), alpha)
    sign = signs[...].astype(F32) * live
    first = small[:, 2 * nrhs : 3 * nrhs]
    weights = jnp.concatenate([alpha, carried + first], axis=0)
    multipliers_out[0] = sign * combine(weights, jnp.concatenate([precond[...], old_precond[...]], axis=0))
    weights = jnp.concatenate([alpha, carried], axis=0)
    change = combine(weights, jnp.concatenate([whole, old_image[...]], axis=0))
    residual_out[0] = sign * (residual[...] - change)


VMEM = pl.BlockSpec(memory_space=pltpu.VMEM)
ANY = pl.BlockSpec(memory_space=pl.ANY)


def call(body, shapes, *args, specs=None, scratch=(), flops=0):
    shapes = [jax.ShapeDtypeStruct(shape, dtype) for shape, dtype in shapes]
    moved = sum(arg.size * arg.dtype.itemsize for arg in args)
    return pl.pallas_call(
        body,
        out_shape=shapes,
        in_specs=specs or [VMEM] * len(args),
        out_specs=[VMEM] * len(shapes),
        scratch_shapes=list(scratch),
        compiler_params=pltpu.CompilerParams(vmem_limit_bytes=16 << 20),
        cost_estimate=pl.CostEstimate(flops=flops, bytes_accessed=moved, transcendentals=0),
    )(*args)


def local(count, groups, dual_rhs, dual_ops, prec_ops, corner_coupling, corner_map, signs, coarse_inverse):
    nrhs, width = dual_rhs.shape[1:]
    half = width // 2
    corners = coarse_inverse.shape[0]
    inner, outer = inner_pairs(count, groups), outer_pairs(count, groups)
    steps = rotations(count, groups)
    lanes = corners + 128 * ((3 * nrhs + 127) // 128)
    flops = 2 * nrhs * width * width

    def permute(values, pairs):
        return lax.ppermute(values, AXES, pairs)

    def region(to_inner):
        got = permute(to_inner, inner)
        values = to_inner[:, :lanes] + got[:, :lanes]
        parts = [values]
        for turns in steps:
            values = sum(parts[1:], parts[0])
            parts = [values] + [permute(values, pairs) for pairs in turns]
        return sum(parts[1:-1], parts[0]), parts[-1], got

    wide = ((nrhs, width), F32)
    face = ((nrhs, half), F32)
    pieces = 4
    product, to_inner, to_outer = call(
        functools.partial(start_kernel, count),
        [wide, face, face],
        dual_rhs, signs, prec_ops,
        specs=[VMEM, VMEM, ANY],
        scratch=[pltpu.VMEM((pieces, width // pieces, width), BF16), pltpu.SemaphoreType.DMA((pieces,))],
        flops=flops,
    )
    from_outer = permute(to_outer, outer)
    from_inner = permute(to_inner, inner)
    precond0, image0, to_inner, to_outer = call(
        functools.partial(first_kernel, count, corners),
        [wide, wide, ((nrhs, lanes + width), F32), wide],
        product, from_inner, from_outer, dual_rhs, signs, dual_ops, corner_coupling, corner_map,
        flops=flops,
    )
    square = ((corners, corners), BF16)
    coarse_parts = call(prepare_kernel, [square, square], coarse_inverse, flops=corners * corners)
    from_outer = permute(to_outer, outer)
    left, right, got = region(to_inner)
    sums0, solved0, residual1, whole0, product, small, beside, to_inner, to_outer = call(
        functools.partial(middle_kernel, count, corners),
        [
            ((nrhs, corners), F32), ((nrhs, corners), F32), wide, wide, wide, ((nrhs, 128), F32), wide, face, face,
        ],
        left, right, got, from_outer, precond0, image0, dual_rhs, signs, prec_ops, corner_coupling, corner_map,
        *coarse_parts,
        flops=flops,
    )
    from_outer = permute(to_outer, outer)
    from_inner = permute(to_inner, inner)
    (inverse,) = call(invert_kernel, [((nrhs, nrhs), F32)], small, flops=nrhs**3)
    precond1, image1, to_inner, to_outer = call(
        functools.partial(second_kernel, count, corners),
        [wide, wide, ((nrhs, lanes + half), F32), face],
        product, from_inner, from_outer, residual1, precond0, image0, dual_ops, corner_coupling, corner_map,
        flops=flops,
    )
    from_outer = permute(to_outer, outer)
    left, right, got = region(to_inner)
    whole_out = ((1, nrhs, width), F32)
    return tuple(
        call(
            functools.partial(final_kernel, count, corners),
            [whole_out, whole_out],
            left, right, got, from_outer, precond1, image1, residual1, precond0, whole0, sums0, solved0, small,
            inverse, beside, signs, corner_coupling, corner_map, *coarse_parts,
            flops=flops,
        )
    )


def solution(mesh):
    in_specs = (
        P("grp", None, "blk"),
        P("grp", "blk", None),
        P("grp", "blk", None),
        P("grp", "blk", None),
        P("grp", "blk"),
        P("grp", "blk"),
        P(),
    )
    out_specs = (P("grp", None, "blk"), P("grp", None, "blk"))
    return jax.shard_map(
        functools.partial(local, mesh.shape["blk"], mesh.shape["grp"]),
        mesh=mesh,
        in_specs=in_specs,
        out_specs=out_specs,
        check_vma=False,
    )
```

time: 80.4 us -> 63.7 us (0.79); the launches traced: 79.2 us -> 63.4 us
  matrix products: 21.3 us -> 0 us
  other arithmetic: 13.5 us -> 0.07 us
  Pallas kernels: 0 us -> 10.9 us
  waiting for transfers between devices: 18.2 us -> 22 us
  local copies, waits for them, and re-layouts: 0.88 us -> 4.52 us
  starting transfers between devices: 24.2 us -> 25.2 us
    dot_general x42 -> x0, matrix products: 20.3 us -> none  [the longest x4 7.58 us: block_product(): lax.dot_general(values.astype(jnp.bfloat16), blocks[0], NT, preferred_ele...]
    another operation x16 -> x0, other arithmetic: 12 us -> none  [the longest x9 6.38 us: gram_solve(): factor = jnp.linalg.cholesky(balanced)]
    pallas_call x0 -> x7, Pallas kernels: none -> 10.9 us  [call(): pl.pallas_call(body, out_shape=shapes, in_specs=specs or [VMEM] * len(arg...]
    unnamed x10 -> x20, local copies, waits for them, and re-layouts: 0.05 us -> 4.52 us
    ppermute x16, waiting for transfers between devices: 18.2 us -> 22 us  [permute(): return lax.ppermute(values, AXES, pairs)]
    ppermute x16, starting transfers between devices: 24.2 us -> 25.2 us  [permute(): return lax.ppermute(values, AXES, pairs)]
    another operation x6 -> x0, matrix products: 1.02 us -> none  [the longest x3 0.6 us: gram_solve(): lax.linalg.triangular_solve(factor, target, left_side=True, lower=True)]
    mul x6 -> x0, other arithmetic: 0.89 us -> none  [the longest x1 0.85 us: local(): sign = signs.astype(jnp.float32) * live]
  transfers between devices with their start and end apart: 16 -> 16, of which waited for: 11 -> 12; matrix products, arithmetic and copies ran while one was open for 5% -> 0% of each run, Pallas kernels for 0% -> 3%
where the time goes in v2:
time: 63.7 us; the launch traced here: 63.4 us
  starting transfers between devices  25.2 us (40%)
  waiting for transfers between devices  22 us (35%)
  Pallas kernels  10.9 us (17%)
  local copies, waits for them, and re-layouts  4.52 us (7%)
  between operations  0.71 us (1%)
    ppermute x16, starting transfers between devices, permute(): return lax.ppermute(values, AXES, pairs)  25.2 us
    ppermute x16, waiting for transfers between devices, permute(): return lax.ppermute(values, AXES, pairs)  22 us
    pallas_call x7, Pallas kernels, call(): pl.pallas_call(body, out_shape=shapes, in_specs=specs or [VMEM] * len(arg...  10.9 us
    unnamed x20, local copies, waits for them, and re-layouts  4.52 us
  transfers between devices with their start and end apart: 16, of which 12 were waited for; matrix products, arithmetic and copies ran while one was open for 0% of the time, Pallas kernels for 3%

profile of v2, /device:TPU:0, one launch (start us, length us, event | category | flops | bytes accessed | tf_op | source)
XLA Modules:
  0.0 63.4 jit_solution(17159825013219215134)
XLA Ops:
  0.6 0.0 copy-start
  0.6 1.6 %copy-done = bf16[1,1024,1024]{2,1,0:T(8,128)(2,1)S(1)} copy-done((bf16[1,1024,1024]{2,1,0:T(8,128)(2,1)S(1)}, bf16[1,1024,1024]{2,1,0:T(8,128)(2,1)}, u32[]{:S(2)}) %copy-start) | copy-done | bytes 2097176
  2.2 0.8 %copy-done.4 = f32[1,16,1024]{2,1,0:T(8,128)S(1)} copy-done((f32[1,16,1024]{2,1,0:T(8,128)S(1)}, f32[1,16,1024]{2,1,0:T(8,128)}, u32[]{:S(2)}) %copy-start.4) | copy-done | bytes 65560
  3.1 0.7 %copy-done.7 = s32[1,1024]{1,0:T(1,128)S(1)} copy-done((s32[1,1024]{1,0:T(1,128)S(1)}, s32[1,1024]{1,0:T(1,128)}, u32[]{:S(2)}) %copy-start.7) | copy-done | bytes 4120
  3.8 0.6 shard_map.86
  4.4 0.5 collective-permute-start
  4.9 2.6 %collective-permute-start.1 = (f32[16,512]{1,0:T(8,128)S(1)}, f32[16,512]{1,0:T(8,128)S(1)}, u32[]{:S(2)}, u32[]{:S(2)}) collective-permute-start(f32[16,512]{1,0:T(8,128)S(1)} %get-tuple-element.26), channel_id=1, source_target_pairs={{0,1},{1,0},{2,4},{3,5},{4,2},{5,3},{6,8},{7,9},{8,6},{9,7},{10,12... | collective-permute-start | bytes 98312 | tf_op jit(solution)/shard_map/ppermute | solution.py:437
  7.5 0.0 collective-permute-done.from_inner
  7.5 1.9 %collective-permute-done.1.from_outer = f32[16,512]{1,0:T(8,128)S(1)} collective-permute-done((f32[16,512]{1,0:T(8,128)S(1)}, f32[16,512]{1,0:T(8,128)S(1)}, u32[]{:S(2)}, u32[]{:S(2)}) %collective-permute-start.1) | collective-permute-done | bytes 32800 | tf_op jit(solution)/shard_map/ppermute | solution.py:437
  9.4 0.0 copy-done.2
  9.4 0.7 %copy-done.5 = bf16[1,24,512]{2,1,0:T(8,128)(2,1)S(1)} copy-done((bf16[1,24,512]{2,1,0:T(8,128)(2,1)S(1)}, bf16[1,24,512]{2,1,0:T(8,128)(2,1)}, u32[]{:S(2)}) %copy-start.5) | copy-done | bytes 24600
  10.1 0.7 %copy-done.8 = s32[1,24]{1,0:T(1,128)S(1)} copy-done((s32[1,24]{1,0:T(1,128)S(1)}, s32[1,24]{1,0:T(1,128)}, u32[]{:S(2)}) %copy-start.8) | copy-done | bytes 120
  10.8 0.7 %shard_map.87 = (f32[16,1024]{1,0:T(8,128)S(1)}, f32[16,1024]{1,0:T(8,128)S(1)}, f32[16,1920]{1,0:T(8,128)S(1)}, f32[16,1024]{1,0:T(8,128)S(1)}) custom-call(f32[16,1024]{1,0:T(8,128)S(1)} %get-tuple-element.24.product, f32[16,512]{1,0:T(8,128)S(1)} %collective-permute-done.from_inner, f32[16,512]{1,0:T(8,128)S(1)} %collective-permute-done.1.from_outer, ...), custom_call_target="tpu_custom_call" | custom-call | flops 33554432 | bytes 2322528 | tf_op jit(solution)/shard_map/pallas_call | solution.py:416
  11.5 0.0 copy-start.9
  11.5 0.2 collective-permute-start.2
  11.6 1.2 %collective-permute-done.2.got = f32[16,1920]{1,0:T(8,128)S(1)} collective-permute-done((f32[16,1920]{1,0:T(8,128)S(1)}, f32[16,1920]{1,0:T(8,128)S(1)}, u32[]{:S(2)}, u32[]{:S(2)}) %collective-permute-start.2) | collective-permute-done | bytes 122912 | tf_op jit(solution)/shard_map/ppermute | solution.py:437
  12.9 2.5 %collective-permute-start.3 = (f32[16,896]{1,0:T(8,128)S(1)}, f32[16,896]{1,0:T(8,128)S(1)}, u32[]{:S(2)}, u32[]{:S(2)}) collective-permute-start(f32[16,896]{1,0:T(8,128)S(1)} %slice_add_fusion.1), channel_id=1, source_target_pairs={{0,6},{1,7},{2,4},{3,5},{4,2},{5,3},{6,0},{7,1},{8,14},{9,15},{10,... | collective-permute-start | bytes 172040 | tf_op jit(solution)/shard_map/ppermute | solution.py:437
  15.4 2.2 %collective-permute-done.3 = f32[16,896]{1,0:T(8,128)S(1)} collective-permute-done((f32[16,896]{1,0:T(8,128)S(1)}, f32[16,896]{1,0:T(8,128)S(1)}, u32[]{:S(2)}, u32[]{:S(2)}) %collective-permute-start.3) | collective-permute-done | bytes 57376 | tf_op jit(solution)/shard_map/ppermute | solution.py:437
  17.6 1.3 %collective-permute-start.4 = (f32[16,896]{1,0:T(8,128)S(1)}, f32[16,896]{1,0:T(8,128)S(1)}, u32[]{:S(2)}, u32[]{:S(2)}) collective-permute-start(f32[16,896]{1,0:T(8,128)S(1)} %add.25), channel_id=1, source_target_pairs={{0,3},{1,2},{2,1},{3,0},{4,7},{5,6},{6,5},{7,4},{8,11},{9,10},{10,... | collective-permute-start | bytes 172040 | tf_op jit(solution)/shard_map/ppermute | solution.py:437
  18.8 2.7 %collective-permute-done.4 = f32[16,896]{1,0:T(8,128)S(1)} collective-permute-done((f32[16,896]{1,0:T(8,128)S(1)}, f32[16,896]{1,0:T(8,128)S(1)}, u32[]{:S(2)}, u32[]{:S(2)}) %collective-permute-start.4) | collective-permute-done | bytes 57376 | tf_op jit(solution)/shard_map/ppermute | solution.py:437
  21.6 1.6 %collective-permute-start.5 = (f32[16,896]{1,0:T(8,128)S(1)}, f32[16,896]{1,0:T(8,128)S(1)}, u32[]{:S(2)}, u32[]{:S(2)}) collective-permute-start(f32[16,896]{1,0:T(8,128)S(1)} %add.26), channel_id=1, source_target_pairs={{0,10},{1,11},{2,8},{3,9},{4,14},{5,15},{6,12},{7,13},{8,2},{9,3},... | collective-permute-start | bytes 172040 | tf_op jit(solution)/shard_map/ppermute | solution.py:437
  23.2 1.5 %collective-permute-start.7 = (f32[16,1024]{1,0:T(8,128)S(1)}, f32[16,1024]{1,0:T(8,128)S(1)}, u32[]{:S(2)}, u32[]{:S(2)}) collective-permute-start(f32[16,1024]{1,0:T(8,128)S(1)} %get-tuple-element.28), channel_id=1, source_target_pairs={{0,1},{1,0},{2,4},{3,5},{4,2},{5,3},{6,8},{7,9},{8,6},{9,7},{10,12... | collective-permute-start | bytes 196616 | tf_op jit(solution)/shard_map/ppermute | solution.py:437
  24.7 0.9 %collective-permute-done.5 = f32[16,896]{1,0:T(8,128)S(1)} collective-permute-done((f32[16,896]{1,0:T(8,128)S(1)}, f32[16,896]{1,0:T(8,128)S(1)}, u32[]{:S(2)}, u32[]{:S(2)}) %collective-permute-start.5) | collective-permute-done | bytes 57376 | tf_op jit(solution)/shard_map/ppermute | solution.py:437
  25.6 2.6 %collective-permute-start.6 = (f32[16,896]{1,0:T(8,128)S(1)}, f32[16,896]{1,0:T(8,128)S(1)}, u32[]{:S(2)}, u32[]{:S(2)}) collective-permute-start(f32[16,896]{1,0:T(8,128)S(1)} %add.27.summed_a), channel_id=1, source_target_pairs={{0,18},{1,19},{2,16},{3,17},{4,22},{5,23},{6,20},{7,21},{8,26},{9,... | collective-permute-start | bytes 172040 | tf_op jit(solution)/shard_map/ppermute | solution.py:437
  28.2 0.0 copy-done.3
  28.2 0.3 shard_map.88
  28.5 0.0 collective-permute-done.7.from_outer
  28.5 1.8 %collective-permute-done.6.summed_b = f32[16,896]{1,0:T(8,128)S(1)} collective-permute-done((f32[16,896]{1,0:T(8,128)S(1)}, f32[16,896]{1,0:T(8,128)S(1)}, u32[]{:S(2)}, u32[]{:S(2)}) %collective-permute-start.6) | collective-permute-done | bytes 57376 | tf_op jit(solution)/shard_map/ppermute | solution.py:437
  30.3 3.0 %shard_map.89 = (f32[16,768]{1,0:T(8,128)S(1)}, f32[16,768]{1,0:T(8,128)S(1)}, f32[16,1024]{1,0:T(8,128)S(1)}, f32[16,1024]{1,0:T(8,128)S(1)}, f32[16,1024]{1,0:...) custom-call(f32[16,896]{1,0:T(8,128)S(1)} %add.27.summed_a, ...), custom_call_target="tpu_custom_call" | custom-call | flops 33554432 | bytes 4984928 | tf_op jit(solution)/shard_map/pallas_call | solution.py:416
  33.3 0.2 collective-permute-start.8
  33.6 1.5 %collective-permute-start.9 = (f32[16,512]{1,0:T(8,128)S(1)}, f32[16,512]{1,0:T(8,128)S(1)}, u32[]{:S(2)}, u32[]{:S(2)}) collective-permute-start(f32[16,512]{1,0:T(8,128)S(1)} %get-tuple-element.35), channel_id=1, source_target_pairs={{0,1},{1,0},{2,4},{3,5},{4,2},{5,3},{6,8},{7,9},{8,6},{9,7},{10,12... | collective-permute-start | bytes 98312 | tf_op jit(solution)/shard_map/ppermute | solution.py:437
  35.0 0.0 collective-permute-done.8.from_inner
  35.1 2.4 %collective-permute-done.9.from_outer = f32[16,512]{1,0:T(8,128)S(1)} collective-permute-done((f32[16,512]{1,0:T(8,128)S(1)}, f32[16,512]{1,0:T(8,128)S(1)}, u32[]{:S(2)}, u32[]{:S(2)}) %collective-permute-start.9) | collective-permute-done | bytes 32800 | tf_op jit(solution)/shard_map/ppermute | solution.py:437
  37.5 0.9 %shard_map.90 = (f32[16,1024]{1,0:T(8,128)S(1)}, f32[16,1024]{1,0:T(8,128)S(1)}, f32[16,1408]{1,0:T(8,128)S(1)}, f32[16,512]{1,0:T(8,128)S(1)}) custom-call(f32[16,1024]{1,0:T(8,128)S(1)} %get-tuple-element.33.product, f32[16,512]{1,0:T(8,128)S(1)} %collective-permute-done.8.from_inner, f32[16,512]{1,0:T(8,128)S(1)} %collective-permute-done.9.from_outer, ...), custom_call_target="tpu_custom_call" | custom-call | flops 33554432 | bytes 2449504 | tf_op jit(solution)/shard_map/pallas_call | solution.py:416
  38.4 0.3 collective-permute-start.10
  38.7 1.0 %collective-permute-done.10.got = f32[16,1408]{1,0:T(8,128)S(1)} collective-permute-done((f32[16,1408]{1,0:T(8,128)S(1)}, f32[16,1408]{1,0:T(8,128)S(1)}, u32[]{:S(2)}, u32[]{:S(2)}) %collective-permute-start.10) | collective-permute-done | bytes 90144 | tf_op jit(solution)/shard_map/ppermute | solution.py:437
  39.7 2.6 %collective-permute-start.11 = (f32[16,896]{1,0:T(8,128)S(1)}, f32[16,896]{1,0:T(8,128)S(1)}, u32[]{:S(2)}, u32[]{:S(2)}) collective-permute-start(f32[16,896]{1,0:T(8,128)S(1)} %slice_add_fusion), channel_id=1, source_target_pairs={{0,6},{1,7},{2,4},{3,5},{4,2},{5,3},{6,0},{7,1},{8,14},{9,15},{10,... | collective-permute-start | bytes 172040 | tf_op jit(solution)/shard_map/ppermute | solution.py:437
  42.3 2.2 %collective-permute-done.11 = f32[16,896]{1,0:T(8,128)S(1)} collective-permute-done((f32[16,896]{1,0:T(8,128)S(1)}, f32[16,896]{1,0:T(8,128)S(1)}, u32[]{:S(2)}, u32[]{:S(2)}) %collective-permute-start.11) | collective-permute-done | bytes 57376 | tf_op jit(solution)/shard_map/ppermute | solution.py:437
  44.5 1.3 %collective-permute-start.12 = (f32[16,896]{1,0:T(8,128)S(1)}, f32[16,896]{1,0:T(8,128)S(1)}, u32[]{:S(2)}, u32[]{:S(2)}) collective-permute-start(f32[16,896]{1,0:T(8,128)S(1)} %add.29), channel_id=1, source_target_pairs={{0,3},{1,2},{2,1},{3,0},{4,7},{5,6},{6,5},{7,4},{8,11},{9,10},{10,... | collective-permute-start | bytes 172040 | tf_op jit(solution)/shard_map/ppermute | solution.py:437
  45.7 2.7 %collective-permute-done.12 = f32[16,896]{1,0:T(8,128)S(1)} collective-permute-done((f32[16,896]{1,0:T(8,128)S(1)}, f32[16,896]{1,0:T(8,128)S(1)}, u32[]{:S(2)}, u32[]{:S(2)}) %collective-permute-start.12) | collective-permute-done | bytes 57376 | tf_op jit(solution)/shard_map/ppermute | solution.py:437
  48.5 1.8 %collective-permute-start.13 = (f32[16,896]{1,0:T(8,128)S(1)}, f32[16,896]{1,0:T(8,128)S(1)}, u32[]{:S(2)}, u32[]{:S(2)}) collective-permute-start(f32[16,896]{1,0:T(8,128)S(1)} %add.30), channel_id=1, source_target_pairs={{0,10},{1,11},{2,8},{3,9},{4,14},{5,15},{6,12},{7,13},{8,2},{9,3},... | collective-permute-start | bytes 172040 | tf_op jit(solution)/shard_map/ppermute | solution.py:437
  50.3 2.0 %collective-permute-done.13 = f32[16,896]{1,0:T(8,128)S(1)} collective-permute-done((f32[16,896]{1,0:T(8,128)S(1)}, f32[16,896]{1,0:T(8,128)S(1)}, u32[]{:S(2)}, u32[]{:S(2)}) %collective-permute-start.13) | collective-permute-done | bytes 57376 | tf_op jit(solution)/shard_map/ppermute | solution.py:437
  52.3 3.3 %collective-permute-start.14 = (f32[16,896]{1,0:T(8,128)S(1)}, f32[16,896]{1,0:T(8,128)S(1)}, u32[]{:S(2)}, u32[]{:S(2)}) collective-permute-start(f32[16,896]{1,0:T(8,128)S(1)} %add.31.summed_a), channel_id=1, source_target_pairs={{0,18},{1,19},{2,16},{3,17},{4,22},{5,23},{6,20},{7,21},{8,26},{9,... | collective-permute-start | bytes 172040 | tf_op jit(solution)/shard_map/ppermute | solution.py:437
  55.6 1.5 %collective-permute-start.15 = (f32[16,512]{1,0:T(8,128)S(1)}, f32[16,512]{1,0:T(8,128)S(1)}, u32[]{:S(2)}, u32[]{:S(2)}) collective-permute-start(f32[16,512]{1,0:T(8,128)S(1)} %get-tuple-element.38), channel_id=1, source_target_pairs={{0,1},{1,0},{2,4},{3,5},{4,2},{5,3},{6,8},{7,9},{8,6},{9,7},{10,12... | collective-permute-start | bytes 98312 | tf_op jit(solution)/shard_map/ppermute | solution.py:437
  57.1 1.4 %shard_map.91.inverse = f32[16,16]{1,0:T(8,128)S(1)} custom-call(f32[16,128]{1,0:T(8,128)S(1)} %get-tuple-element.44.small), custom_call_target="tpu_custom_call" | custom-call | flops 4096 | bytes 8192 | tf_op jit(solution)/shard_map/pallas_call | solution.py:416
  58.4 1.0 %collective-permute-done.15.from_outer = f32[16,512]{1,0:T(8,128)S(1)} collective-permute-done((f32[16,512]{1,0:T(8,128)S(1)}, f32[16,512]{1,0:T(8,128)S(1)}, u32[]{:S(2)}, u32[]{:S(2)}) %collective-permute-start.15) | collective-permute-done | bytes 32800 | tf_op jit(solution)/shard_map/ppermute | solution.py:437
  59.5 0.0 collective-permute-done.14.summed_b
  59.5 4.0 %shard_map.92 = (f32[1,16,1024]{2,1,0:T(8,128)}, f32[1,16,1024]{2,1,0:T(8,128)}) custom-call(f32[16,896]{1,0:T(8,128)S(1)} %add.31.summed_a, f32[16,896]{1,0:T(8,128)S(1)} %collective-permute-done.14.summed_b, f32[16,1408]{1,0:T(8,128)S(1)} %collective-permute-done.10.got, f32[16,512]{1,0:T(8,128)S(1)} %collective-permute-done.15.from_outer, ...), custom_call_target="tpu_custom_call" | custom-call | flops 33554432 | bytes 3126368 | tf_op jit(solution)/shard_map/pallas_call | solution.py:416
  (19 shorter events, 0.1 us)
Async XLA Ops:
  0.6 1.6 %copy-start = (bf16[1,1024,1024]{2,1,0:T(8,128)(2,1)S(1)}, bf16[1,1024,1024]{2,1,0:T(8,128)(2,1)}, u32[]{:S(2)}) copy-start(bf16[1,1024,1024]{2,1,0:T(8,128)(2,1)} %blocks.6) | copy-start | bytes 6291460
  2.2 0.8 %copy-start.4 = (f32[1,16,1024]{2,1,0:T(8,128)S(1)}, f32[1,16,1024]{2,1,0:T(8,128)}, u32[]{:S(2)}) copy-start(f32[1,16,1024]{2,1,0:T(8,128)} %rhs.5) | copy-start | bytes 196612
  3.1 0.7 %copy-start.7 = (s32[1,1024]{1,0:T(1,128)S(1)}, s32[1,1024]{1,0:T(1,128)}, u32[]{:S(2)}) copy-start(s32[1,1024]{1,0:T(1,128)} %signs.7) | copy-start | bytes 12292
  3.8 5.6 %copy-start.2 = (bf16[1,1024,1024]{2,1,0:T(8,128)(2,1)S(1)}, bf16[1,1024,1024]{2,1,0:T(8,128)(2,1)}, u32[]{:S(2)}) copy-start(bf16[1,1024,1024]{2,1,0:T(8,128)(2,1)} %blocks.7) | copy-start | bytes 6291460
  3.8 24.4 %copy-start.3 = (f32[768,768]{1,0:T(8,128)S(1)}, f32[768,768]{1,0:T(8,128)}, u32[]{:S(2)}) copy-start(f32[768,768]{1,0:T(8,128)} %coarse.1) | copy-start | bytes 7077892
  4.4 3.1 %collective-permute-start = (f32[16,512]{1,0:T(8,128)S(1)}, f32[16,512]{1,0:T(8,128)S(1)}, u32[]{:S(2)}, u32[]{:S(2)}) collective-permute-start(f32[16,512]{1,0:T(8,128)S(1)} %get-tuple-element.25), channel_id=1, source_target_pairs={{0,2},{1,3},{2,0},{3,1},{4,6},{5,7},{6,4},{7,5},{8,10},{9,11},{10,... | collective-permute-start | bytes 98312 | tf_op jit(solution)/shard_map/ppermute | solution.py:437
  4.9 4.5 %collective-permute-start.1 = (f32[16,512]{1,0:T(8,128)S(1)}, f32[16,512]{1,0:T(8,128)S(1)}, u32[]{:S(2)}, u32[]{:S(2)}) collective-permute-start(f32[16,512]{1,0:T(8,128)S(1)} %get-tuple-element.26), channel_id=1, source_target_pairs={{0,1},{1,0},{2,4},{3,5},{4,2},{5,3},{6,8},{7,9},{8,6},{9,7},{10,12... | collective-permute-start | bytes 98312 | tf_op jit(solution)/shard_map/ppermute | solution.py:437
  9.4 0.7 %copy-start.5 = (bf16[1,24,512]{2,1,0:T(8,128)(2,1)S(1)}, bf16[1,24,512]{2,1,0:T(8,128)(2,1)}, u32[]{:S(2)}) copy-start(bf16[1,24,512]{2,1,0:T(8,128)(2,1)} %coupling.7) | copy-start | bytes 73732
  10.1 0.7 %copy-start.8 = (s32[1,24]{1,0:T(1,128)S(1)}, s32[1,24]{1,0:T(1,128)}, u32[]{:S(2)}) copy-start(s32[1,24]{1,0:T(1,128)} %corner_map.7) | copy-start | bytes 292
  11.5 18.9 %copy-start.1 = (bf16[1,1024,1024]{2,1,0:T(8,128)(2,1)S(1)}, bf16[1,1024,1024]{2,1,0:T(8,128)(2,1)}, u32[]{:S(2)}) copy-start(bf16[1,1024,1024]{2,1,0:T(8,128)(2,1)} %blocks.6) | copy-start | bytes 6291460
  11.5 18.9 %copy-start.9 = (s32[1,24]{1,0:T(1,128)S(1)}, s32[1,24]{1,0:T(1,128)}, u32[]{:S(2)}) copy-start(s32[1,24]{1,0:T(1,128)} %corner_map.7) | copy-start | bytes 292
  11.5 1.4 %collective-permute-start.2 = (f32[16,1920]{1,0:T(8,128)S(1)}, f32[16,1920]{1,0:T(8,128)S(1)}, u32[]{:S(2)}, u32[]{:S(2)}) collective-permute-start(f32[16,1920]{1,0:T(8,128)S(1)} %get-tuple-element.27), channel_id=1, source_target_pairs={{0,2},{1,3},{2,0},{3,1},{4,6},{5,7},{6,4},{7,5},{8,10},{9,11},{10,... | collective-permute-start | bytes 368648 | tf_op jit(solution)/shard_map/ppermute | solution.py:437
  12.9 4.7 %collective-permute-start.3 = (f32[16,896]{1,0:T(8,128)S(1)}, f32[16,896]{1,0:T(8,128)S(1)}, u32[]{:S(2)}, u32[]{:S(2)}) collective-permute-start(f32[16,896]{1,0:T(8,128)S(1)} %slice_add_fusion.1), channel_id=1, source_target_pairs={{0,6},{1,7},{2,4},{3,5},{4,2},{5,3},{6,0},{7,1},{8,14},{9,15},{10,... | collective-permute-start | bytes 172040 | tf_op jit(solution)/shard_map/ppermute | solution.py:437
  17.6 4.0 %collective-permute-start.4 = (f32[16,896]{1,0:T(8,128)S(1)}, f32[16,896]{1,0:T(8,128)S(1)}, u32[]{:S(2)}, u32[]{:S(2)}) collective-permute-start(f32[16,896]{1,0:T(8,128)S(1)} %add.25), channel_id=1, source_target_pairs={{0,3},{1,2},{2,1},{3,0},{4,7},{5,6},{6,5},{7,4},{8,11},{9,10},{10,... | collective-permute-start | bytes 172040 | tf_op jit(solution)/shard_map/ppermute | solution.py:437
  21.6 4.0 %collective-permute-start.5 = (f32[16,896]{1,0:T(8,128)S(1)}, f32[16,896]{1,0:T(8,128)S(1)}, u32[]{:S(2)}, u32[]{:S(2)}) collective-permute-start(f32[16,896]{1,0:T(8,128)S(1)} %add.26), channel_id=1, source_target_pairs={{0,10},{1,11},{2,8},{3,9},{4,14},{5,15},{6,12},{7,13},{8,2},{9,3},... | collective-permute-start | bytes 172040 | tf_op jit(solution)/shard_map/ppermute | solution.py:437
  23.2 5.4 %collective-permute-start.7 = (f32[16,1024]{1,0:T(8,128)S(1)}, f32[16,1024]{1,0:T(8,128)S(1)}, u32[]{:S(2)}, u32[]{:S(2)}) collective-permute-start(f32[16,1024]{1,0:T(8,128)S(1)} %get-tuple-element.28), channel_id=1, source_target_pairs={{0,1},{1,0},{2,4},{3,5},{4,2},{5,3},{6,8},{7,9},{8,6},{9,7},{10,12... | collective-permute-start | bytes 196616 | tf_op jit(solution)/shard_map/ppermute | solution.py:437
  25.6 4.8 %collective-permute-start.6 = (f32[16,896]{1,0:T(8,128)S(1)}, f32[16,896]{1,0:T(8,128)S(1)}, u32[]{:S(2)}, u32[]{:S(2)}) collective-permute-start(f32[16,896]{1,0:T(8,128)S(1)} %add.27.summed_a), channel_id=1, source_target_pairs={{0,18},{1,19},{2,16},{3,17},{4,22},{5,23},{6,20},{7,21},{8,26},{9,... | collective-permute-start | bytes 172040 | tf_op jit(solution)/shard_map/ppermute | solution.py:437
  30.3 7.1 %copy-start.6 = (bf16[1,24,512]{2,1,0:T(8,128)(2,1)S(1)}, bf16[1,24,512]{2,1,0:T(8,128)(2,1)}, u32[]{:S(2)}) copy-start(bf16[1,24,512]{2,1,0:T(8,128)(2,1)} %coupling.7) | copy-start | bytes 73732
  33.3 1.7 %collective-permute-start.8 = (f32[16,512]{1,0:T(8,128)S(1)}, f32[16,512]{1,0:T(8,128)S(1)}, u32[]{:S(2)}, u32[]{:S(2)}) collective-permute-start(f32[16,512]{1,0:T(8,128)S(1)} %get-tuple-element.34), channel_id=1, source_target_pairs={{0,2},{1,3},{2,0},{3,1},{4,6},{5,7},{6,4},{7,5},{8,10},{9,11},{10,... | collective-permute-start | bytes 98312 | tf_op jit(solution)/shard_map/ppermute | solution.py:437
  33.6 3.9 %collective-permute-start.9 = (f32[16,512]{1,0:T(8,128)S(1)}, f32[16,512]{1,0:T(8,128)S(1)}, u32[]{:S(2)}, u32[]{:S(2)}) collective-permute-start(f32[16,512]{1,0:T(8,128)S(1)} %get-tuple-element.35), channel_id=1, source_target_pairs={{0,1},{1,0},{2,4},{3,5},{4,2},{5,3},{6,8},{7,9},{8,6},{9,7},{10,12... | collective-permute-start | bytes 98312 | tf_op jit(solution)/shard_map/ppermute | solution.py:437
  38.4 1.3 %collective-permute-start.10 = (f32[16,1408]{1,0:T(8,128)S(1)}, f32[16,1408]{1,0:T(8,128)S(1)}, u32[]{:S(2)}, u32[]{:S(2)}) collective-permute-start(f32[16,1408]{1,0:T(8,128)S(1)} %get-tuple-element.37), channel_id=1, source_target_pairs={{0,2},{1,3},{2,0},{3,1},{4,6},{5,7},{6,4},{7,5},{8,10},{9,11},{10,... | collective-permute-start | bytes 270344 | tf_op jit(solution)/shard_map/ppermute | solution.py:437
  39.7 4.7 %collective-permute-start.11 = (f32[16,896]{1,0:T(8,128)S(1)}, f32[16,896]{1,0:T(8,128)S(1)}, u32[]{:S(2)}, u32[]{:S(2)}) collective-permute-start(f32[16,896]{1,0:T(8,128)S(1)} %slice_add_fusion), channel_id=1, source_target_pairs={{0,6},{1,7},{2,4},{3,5},{4,2},{5,3},{6,0},{7,1},{8,14},{9,15},{10,... | collective-permute-start | bytes 172040 | tf_op jit(solution)/shard_map/ppermute | solution.py:437
  44.5 4.0 %collective-permute-start.12 = (f32[16,896]{1,0:T(8,128)S(1)}, f32[16,896]{1,0:T(8,128)S(1)}, u32[]{:S(2)}, u32[]{:S(2)}) collective-permute-start(f32[16,896]{1,0:T(8,128)S(1)} %add.29), channel_id=1, source_target_pairs={{0,3},{1,2},{2,1},{3,0},{4,7},{5,6},{6,5},{7,4},{8,11},{9,10},{10,... | collective-permute-start | bytes 172040 | tf_op jit(solution)/shard_map/ppermute | solution.py:437
  48.5 3.8 %collective-permute-start.13 = (f32[16,896]{1,0:T(8,128)S(1)}, f32[16,896]{1,0:T(8,128)S(1)}, u32[]{:S(2)}, u32[]{:S(2)}) collective-permute-start(f32[16,896]{1,0:T(8,128)S(1)} %add.30), channel_id=1, source_target_pairs={{0,10},{1,11},{2,8},{3,9},{4,14},{5,15},{6,12},{7,13},{8,2},{9,3},... | collective-permute-start | bytes 172040 | tf_op jit(solution)/shard_map/ppermute | solution.py:437
  52.3 7.2 %collective-permute-start.14 = (f32[16,896]{1,0:T(8,128)S(1)}, f32[16,896]{1,0:T(8,128)S(1)}, u32[]{:S(2)}, u32[]{:S(2)}) collective-permute-start(f32[16,896]{1,0:T(8,128)S(1)} %add.31.summed_a), channel_id=1, source_target_pairs={{0,18},{1,19},{2,16},{3,17},{4,22},{5,23},{6,20},{7,21},{8,26},{9,... | collective-permute-start | bytes 172040 | tf_op jit(solution)/shard_map/ppermute | solution.py:437
  55.6 3.9 %collective-permute-start.15 = (f32[16,512]{1,0:T(8,128)S(1)}, f32[16,512]{1,0:T(8,128)S(1)}, u32[]{:S(2)}, u32[]{:S(2)}) collective-permute-start(f32[16,512]{1,0:T(8,128)S(1)} %get-tuple-element.38), channel_id=1, source_target_pairs={{0,1},{1,0},{2,4},{3,5},{4,2},{5,3},{6,8},{7,9},{8,6},{9,7},{10,12... | collective-permute-start | bytes 98312 | tf_op jit(solution)/shard_map/ppermute | solution.py:437

commit v3 on v2

v3 whole, which is shorter than its diff:
```python
import functools

import jax
import jax.numpy as jnp
from jax import lax
from jax.experimental import pallas as pl
from jax.experimental.pallas import tpu as pltpu
from jax.sharding import PartitionSpec as P

AXES = ("blk", "grp")
NN = (((1,), (0,)), ((), ()))
NT = (((1,), (1,)), ((), ()))
TN = (((0,), (0,)), ((), ()))
F32 = jnp.float32
BF16 = jnp.bfloat16


def radices(count):
    found = []
    factor = 2
    while count > 1:
        while count % factor == 0:
            found.append(factor)
            count //= factor
        factor += 1
    return found


def swap(count, groups, partner):
    pairs = []
    for blk in range(count):
        for grp in range(groups):
            other = partner(blk)
            if 0 <= other < count:
                target = other * groups + grp
            elif grp ^ 1 < groups:
                target = blk * groups + (grp ^ 1)
            else:
                target = blk * groups + grp
            pairs.append((blk * groups + grp, target))
    return pairs


def inner_pairs(count, groups):
    return swap(count, groups, lambda blk: blk ^ 1)


def outer_pairs(count, groups):
    return swap(count, groups, lambda blk: blk + 1 if blk % 2 == 1 else blk - 1)


def rotations(count, groups):
    core = 2 if count % 2 == 0 else 1
    steps = []

    def flipped(blk, turn):
        return (blk ^ 1) if (core == 2 and turn) else blk

    def add_axis(step_target, factor):
        steps.append(
            [
                [
                    (blk * groups + grp, step_target(blk, grp, turn))
                    for blk in range(count)
                    for grp in range(groups)
                ]
                for turn in range(1, factor)
            ]
        )

    stride = 1
    blk_steps = []
    for factor in radices(count // core):
        blk_steps.append((stride, factor))
        stride *= factor
    grp_steps = []
    stride = 1
    for factor in radices(groups):
        grp_steps.append((stride, factor))
        stride *= factor

    def blk_target(stride, factor):
        def target(blk, grp, turn):
            chip = blk // core
            digit = (chip // stride) % factor
            moved = chip + ((digit + turn) % factor - digit) * stride
            return flipped(moved * core + blk % core, turn) * groups + grp

        return target

    def grp_target(stride, factor):
        def target(blk, grp, turn):
            digit = (grp // stride) % factor
            moved = grp + ((digit + turn) % factor - digit) * stride
            return flipped(blk, turn) * groups + moved

        return target

    for stride, factor in blk_steps[1:]:
        add_axis(blk_target(stride, factor), factor)
    for stride, factor in grp_steps:
        add_axis(grp_target(stride, factor), factor)
    for stride, factor in blk_steps[:1]:
        add_axis(blk_target(stride, factor), factor)
    return steps


def mm(first, second, dims):
    return lax.dot_general(first, second, dims, preferred_element_type=F32)


def halves(values):
    high = values.astype(BF16)
    return high, (values - high.astype(F32)).astype(BF16)


def stacked(values):
    return jnp.concatenate(halves(values), axis=0)


def folded(rows):
    count = rows.shape[0] // 2
    return rows[:count] + rows[count:]


def dots(first, second):
    product = folded(mm(stacked(first), stacked(second), NT))
    count = second.shape[0]
    return product[:, :count] + product[:, count:]


def combine(weights, values):
    weight_high, weight_low = halves(weights)
    high, low = halves(values)
    left = jnp.concatenate([weight_high, weight_high, weight_low, weight_low], axis=0)
    right = jnp.concatenate([high, low, high, low], axis=0)
    return mm(left, right, TN)


def against(values, exact):
    return folded(mm(stacked(values), exact, NN))


def lanes_of(shape):
    return lax.broadcasted_iota(jnp.int32, shape, len(shape) - 1)


def chosen(row, corners):
    shape = (corners, row.shape[1])
    return (lax.broadcasted_iota(jnp.int32, shape, 0) == row).astype(BF16)


def live_mask(blk, count, width):
    lane = lanes_of((1, width))
    low = (blk > 0).astype(F32)
    up = (blk < count - 1).astype(F32)
    return jnp.where(lane < width // 2, low, up)


def split(even, low, up):
    return jnp.where(even, up, low), jnp.where(even, low, up)


def joined(even, from_inner, from_outer):
    low = jnp.where(even, from_outer, from_inner)
    up = jnp.where(even, from_inner, from_outer)
    return jnp.concatenate([low, up], axis=1)


def transposed(matrix):
    return matrix.T


def eliminate(matrix, target):
    count = matrix.shape[1]
    row_index = lax.broadcasted_iota(jnp.int32, (1, count, 1), 1)
    column_index = lax.broadcasted_iota(jnp.int32, (1, count, count), 2)
    diagonal = jnp.where(row_index == column_index, matrix, 0.0)
    scale = lax.rsqrt(jnp.sum(diagonal, axis=2, keepdims=True))
    matrix = matrix * lax.rsqrt(jnp.sum(diagonal, axis=1, keepdims=True))
    work = jnp.concatenate([matrix, target], axis=2) * scale
    size = 4
    for start in range(0, count, size):
        at = [start + index for index in range(size)]
        columns = [jnp.broadcast_to(work[:, :, k : k + 1], work.shape) for k in at]
        pivot = [[column[:, k : k + 1] for column in columns] for k in at]
        rows = [work[:, k : k + 1] for k in at]
        for one in range(0, size, 2):
            two = one + 1
            a, b, c, d = pivot[one][one], pivot[one][two], pivot[two][one], pivot[two][two]
            inverse = 1.0 / (a * d - b * c)
            for j in range(two + 1, size):
                p, q = pivot[one][j], pivot[two][j]
                pivot[one][j], pivot[two][j] = (d * p - b * q) * inverse, (a * q - c * p) * inverse
            p, q = rows[one], rows[two]
            rows[one], rows[two] = (d * p - b * q) * inverse, (a * q - c * p) * inverse
            for i in range(size):
                if i not in (one, two):
                    left, right = pivot[i][one], pivot[i][two]
                    for j in range(two + 1, size):
                        pivot[i][j] = pivot[i][j] - left * pivot[one][j] - right * pivot[two][j]
                    rows[i] = rows[i] - left * rows[one] - right * rows[two]
        products = [column * row for column, row in zip(columns, rows)]
        work = work - ((products[0] + products[1]) + (products[2] + products[3]))
        for k, row in zip(at, rows):
            work = jnp.where(row_index == k, row, work)
    return work[:, :, count:] * scale


def symmetric(matrix):
    return 0.5 * (matrix + transposed(matrix))


def corner_values(values, couple):
    half = values.shape[1] // 2
    both = stacked(values)
    low = folded(mm(both[:, :half], couple, NT))
    up = folded(mm(both[:, half:], couple, NT))
    return jnp.where(lanes_of(low.shape) < couple.shape[0] // 2, low, up)


TILE = 128
GROUP = 32
MOST = 32


def abreast(rows):
    half = rows.shape[0] // 2
    return [rows[:half], rows[half:]]


def tile_of(corner, middle, first, second):
    shared = jnp.concatenate(abreast(corner) + middle + abreast(first), axis=1)
    return jnp.concatenate([jnp.concatenate([shared, part], axis=1) for part in abreast(second)], axis=0)


def merged(own, got, even, lane):
    rows = lax.broadcasted_iota(jnp.int32, own.shape, 0)
    mine = (rows < own.shape[0] // 2) == even
    taken, other = jnp.where(mine, own, got), jnp.where(mine, got, own)
    return taken + jnp.where(lanes_of(own.shape) < lane, 0.0, other)


def untile(tiles, slots):
    half = tiles.shape[0] // 2
    count = 2 * half
    even, odd = tiles[:half], tiles[half:]
    both = even + odd
    start = 2 * slots
    last = start + 4 * count
    squares = [
        jnp.concatenate([both[:, at : at + count], both[:, at + count : at + 2 * count]], axis=0)
        for at in (start, start + 2 * count)
    ]
    return *squares, jnp.concatenate([even[:, last : last + count], odd[:, last : last + count]], axis=0)


def dense(tiles, maps, slots, corners):
    count = tiles.shape[0] // 8
    lane = lanes_of((1, TILE))
    low, up, index = [], [], []
    totals = [jnp.zeros((8, TILE), F32)] * 2
    for start in range(0, count, TILE // GROUP):
        parts = [jnp.zeros((8, TILE), F32), jnp.zeros((8, TILE), F32), jnp.full((1, TILE), -1.0, F32)]
        for turn, at in enumerate(range(start, min(start + TILE // GROUP, count))):
            tile, name = tiles[8 * at : 8 * at + 8], maps[8 * at : 8 * at + 1]
            totals[at % 2] = totals[at % 2] + tile
            here = (lane // GROUP == turn) & (lane % GROUP < slots)
            shift = GROUP * turn
            moved = [
                pltpu.roll(tile, shift, 1) if shift else tile,
                pltpu.roll(tile, (shift - slots) % TILE, 1),
                pltpu.roll(name, (shift - 2 * slots) % TILE, 1),
            ]
            parts = [jnp.where(here, new, old) for new, old in zip(moved, parts)]
        low.append(parts[0])
        up.append(parts[1])
        index.append(parts[2])
    values = jnp.concatenate([jnp.concatenate(low, axis=1), jnp.concatenate(up, axis=1)], axis=0)
    choice = chosen(jnp.concatenate(index, axis=1).astype(jnp.int32), corners)
    corner_sum = folded(mm(stacked(values), choice, NT))
    return jnp.concatenate([corner_sum, jnp.concatenate(totals, axis=0)], axis=1)


def dense_kernel(slots, corners, tiles, maps, out):
    out[...] = dense(tiles[...], maps[...], slots, corners)


def total_of(left, right, maps, slots, corners):
    if right.shape[1] == TILE:
        return left[...] + dense(right[...], maps[...], slots, corners)
    return left[...] + right[...]


def face_rows(rows):
    low = lax.broadcasted_iota(jnp.int32, rows.shape, 0) < rows.shape[0] // 2
    return jnp.concatenate([jnp.where(low, rows, 0.0), jnp.where(low, 0.0, rows)], axis=1)


def picked(solved, row):
    return folded(mm(stacked(solved), chosen(row.astype(jnp.int32), solved.shape[1]), NN))


def product_of(first, second):
    high, low = halves(second)
    return folded(mm(stacked(first), high, NN)) + mm(first.astype(BF16), low, NN)


def coarse_solve(corner_sum, parts):
    high, low = parts
    first = folded(mm(stacked(corner_sum), high, NN))
    return first + mm(corner_sum.astype(BF16), low, NN)


def start_kernel(
    count, rhs, signs, blocks, coupling, corner_map,
    product, to_inner, to_outer, residual_out, sign_out, couple_out, map_out, inner_extra, outer_extra, held,
    rhs_held, signs_held, coupling_held, map_held, sems,
):
    rows = held.shape[1]
    pieces = [(rhs, rhs_held), (signs, signs_held)]
    pieces += [(blocks.at[0, pl.ds(part * rows, rows)], held.at[part]) for part in range(held.shape[0])]
    pieces += [(corner_map, map_held), (coupling, coupling_held)]
    copies = [pltpu.make_async_copy(*piece, sems.at[index]) for index, piece in enumerate(pieces)]
    for copy in copies:
        copy.start()
    blk = lax.axis_index("blk")
    even = blk % 2 == 0
    nrhs, width = product.shape
    half = width // 2
    live = live_mask(blk, count, width)
    copies[0].wait()
    copies[1].wait()
    sign = signs_held[...].astype(F32) * live
    residual = sign * rhs_held[0]
    rounded = residual.astype(BF16)
    sign_out[...] = sign
    residual_out[...] = residual
    total = jnp.zeros((nrhs, width), F32)
    for part, copy in enumerate(copies[2:-2]):
        copy.wait()
        total = total + mm(rounded[:, part * rows : (part + 1) * rows], held[part], NN)
    product[...] = total
    inner, outer = split(even, total[:, :half], total[:, half:])
    to_inner[...] = inner
    to_outer[...] = outer
    copies[-2].wait()
    copies[-1].wait()
    couple = coupling_held[0]
    couple_out[...] = couple
    slots = couple.shape[0] // 2
    wide = couple.astype(F32)
    row = jnp.concatenate([map_held[...].astype(F32), jnp.zeros((1, half - 2 * slots), F32)], axis=1)
    map_out[...] = row[:, : map_out.shape[1]]
    fill = jnp.zeros((nrhs - slots - 1, half), F32)
    inner, outer = split(
        even,
        jnp.concatenate([wide[:slots], row, fill], axis=0),
        jnp.concatenate([wide[slots:], pltpu.roll(row, half - slots, 1), fill], axis=0),
    )
    inner_extra[...] = inner
    outer_extra[...] = outer


def first_kernel(
    count, product, from_inner, from_outer, residual, blocks, couple, map_row, inner_extra, outer_extra,
    precond_out, image_out, tile_out, to_inner, to_outer,
):
    blk = lax.axis_index("blk")
    even = blk % 2 == 0
    nrhs, width = product.shape
    half = width // 2
    live = live_mask(blk, count, width)
    precond = live * (product[...] - joined(even, from_inner[...], from_outer[...]))
    image = mm(precond.astype(BF16), blocks[...], NN)
    precond_out[...] = precond
    image_out[...] = image
    grams = dots(
        jnp.concatenate([residual[...], precond], axis=0), jnp.concatenate([precond, image], axis=0)
    )
    slots = couple.shape[0]
    middle = jnp.concatenate([map_row[:, :slots], jnp.zeros((1, 2 * nrhs - slots), F32)], axis=1)
    middle = jnp.broadcast_to(middle, (nrhs // 2, 2 * nrhs))
    tile = tile_of(corner_values(precond, couple[...]), [middle], grams[:nrhs, :nrhs], grams[nrhs:, nrhs:])
    tile_out[...] = tile
    inner, outer = split(even, image[:, :half], image[:, half:])
    to_inner[:, :half] = inner
    to_outer[:, :half] = outer
    to_inner[:, half:width] = inner_extra[...]
    to_outer[:, half:] = outer_extra[...]
    to_inner[:, width:] = tile


def load_kernel(blocks, after, out, sems):
    del after
    rows = out.shape[0] // sems.shape[0]
    copies = [
        pltpu.make_async_copy(
            blocks.at[0, pl.ds(part * rows, rows)], out.at[pl.ds(part * rows, rows)], sems.at[part]
        )
        for part in range(sems.shape[0])
    ]
    for copy in copies:
        copy.start()
    for copy in copies:
        copy.wait()


def prepare_kernel(coarse, high, low):
    top, rest = halves(coarse[...])
    high[...] = top
    low[...] = rest


def follow_kernel(
    count, image, got, from_outer, couple, map_row, blocks,
    part_out, product_out, spread_out, columns_out, map_out, to_inner, to_outer,
):
    blk = lax.axis_index("blk")
    even = blk % 2 == 0
    nrhs, width = image.shape
    half = width // 2
    live = live_mask(blk, count, width)
    inner_got = got[...]
    outer_got = from_outer[...]
    part = live * (image[...] - joined(even, inner_got[:, :half], outer_got[:, :half]))
    beside = joined(even, inner_got[:, half:width], outer_got[:, half:])
    wide = couple[...].astype(F32)
    slots = wide.shape[0] // 2
    other = jnp.concatenate([beside[:slots, :half], beside[:slots, half:]], axis=0)
    columns = (live * jnp.concatenate([face_rows(wide), -face_rows(other)], axis=0)).astype(BF16)
    products = mm(jnp.concatenate([stacked(part), columns], axis=0), blocks[...].reshape(width, width), NN)
    product = products[:nrhs] + products[nrhs : 2 * nrhs]
    spread = products[2 * nrhs :]
    row = jnp.concatenate(
        [
            map_row[:, : 2 * slots],
            beside[slots : slots + 1, :slots],
            beside[slots : slots + 1, half : half + slots],
            jnp.full((1, map_row.shape[1] - 4 * slots), -1.0, F32),
        ],
        axis=1,
    )
    part_out[...] = part
    product_out[...] = product
    spread_out[...] = spread
    columns_out[...] = columns
    map_out[...] = row
    count_rows = nrhs + 4 * slots
    rows = jnp.concatenate([product, spread], axis=0)
    to_inner[:count_rows, :], to_outer[:count_rows, :] = split(even, rows[:, :half], rows[:, half:])
    last = jnp.concatenate([row, jnp.zeros((1, half - row.shape[1]), F32)], axis=1)
    last = jnp.broadcast_to(last, (to_inner.shape[0] - count_rows, half))
    to_inner[count_rows:, :] = last
    to_outer[count_rows:, :] = last


def middle_kernel(
    count, corners, left, right, maps, from_inner, from_outer, part, product, spread, columns, map_row,
    precond_in, image_in, residual_in, blocks, couple, coarse_high, coarse_low,
    sums_out, solved_out, residual_out, whole_out, precond_out, image_out, small_out, tile_out, to_inner, to_outer,
):
    blk = lax.axis_index("blk")
    even = blk % 2 == 0
    nrhs, width = part.shape
    half = width // 2
    live = live_mask(blk, count, width)
    slots = couple.shape[0]
    summed = total_of(left, right, maps, slots, corners)
    corner_sum = summed[:, :corners]
    _, gram, energy = untile(summed[:, corners:], slots)
    solved = coarse_solve(corner_sum, (coarse_high[...], coarse_low[...]))
    energy = energy + dots(corner_sum, solved)
    unit = (lax.broadcasted_iota(jnp.int32, (nrhs, nrhs), 0) == lanes_of((nrhs, nrhs))).astype(F32)
    both = eliminate(jnp.stack([symmetric(2.0 * energy), symmetric(gram)]), jnp.stack([gram, unit]))
    alpha, inverse = both[0], both[1]

    rows = spread.shape[0]
    wide = map_row.shape[1]
    inner_got, outer_got = from_inner[...], from_outer[...]
    sides = [jnp.where(even, outer_got, inner_got), jnp.where(even, inner_got, outer_got)]
    index = jnp.concatenate([map_row[...]] + [side[nrhs + rows : nrhs + rows + 1, :wide] for side in sides], axis=1)
    at = picked(solved, index)
    whole = part[...] + against(at[:, :rows], columns[...])
    own = product[...] + product_of(at[:, :rows], spread[...])
    others = [
        side[:nrhs] + product_of(at[:, wide * turn : wide * turn + rows], side[nrhs : nrhs + rows])
        for turn, side in enumerate(sides, 1)
    ]
    change = live * (own - jnp.concatenate(others, axis=1))
    residual = residual_in[...] - combine(alpha, whole)
    precond = precond_in[...] - combine(alpha, change)

    image = mm(precond.astype(BF16), blocks[...], NN)
    left = jnp.concatenate([residual, precond, precond_in[...], image_in[...]], axis=0)
    grams = dots(left, jnp.concatenate([precond, image], axis=0))
    middle = abreast(grams[2 * nrhs : 3 * nrhs, nrhs:] + grams[3 * nrhs :, :nrhs])
    tile = tile_of(
        corner_values(precond, couple[...]), middle, grams[:nrhs, :nrhs], grams[nrhs : 2 * nrhs, nrhs:]
    )
    tile_out[...] = tile
    inner, outer = split(even, image[:, :half], image[:, half:])
    to_inner[:, :half] = inner
    to_inner[:, half:] = tile
    to_outer[...] = outer
    sums_out[...] = corner_sum
    solved_out[...] = solved
    residual_out[...] = residual
    whole_out[...] = whole
    precond_out[...] = precond
    image_out[...] = image
    small_out[...] = jnp.concatenate([inverse, energy, alpha, jnp.zeros((nrhs, 128 - 3 * nrhs), F32)], axis=1)


def final_kernel(
    count, corners, left, right, maps, got, from_outer, precond, image, residual, old_precond, old_image, old_sums,
    old_solved, small, columns, map_row, sign, coarse_high, coarse_low,
    multipliers_out, residual_out,
):
    blk = lax.axis_index("blk")
    even = blk % 2 == 0
    nrhs, width = precond.shape
    live = live_mask(blk, count, width)
    slots = columns.shape[0] // 2
    summed = total_of(left, right, maps, slots, corners)
    corner_sum = summed[:, :corners]
    old_new, gram, new_new = untile(summed[:, corners:], slots)
    beta = combine(small[:, :nrhs], gram)
    solved = coarse_solve(corner_sum, (coarse_high[...], coarse_low[...]))
    cross = dots(
        jnp.concatenate([corner_sum, old_sums[...]], axis=0),
        jnp.concatenate([solved, old_solved[...]], axis=0),
    )
    new_new = new_new + cross[:nrhs, :nrhs]
    old_new = old_new + cross[nrhs:, :nrhs] + transposed(cross[:nrhs, nrhs:])
    old_old = symmetric(small[:, nrhs : 2 * nrhs])
    energy = new_new + combine(beta, old_new + combine(old_old, beta))
    alpha = eliminate(symmetric(2.0 * energy)[None], gram[None])[0]
    image_beside = joined(even, got[:, : width // 2], from_outer[...])
    at = picked(solved, map_row[...])
    whole = live * (image[...] - image_beside) + against(at[:, : columns.shape[0]], columns[...])
    carried = combine(transposed(beta), alpha)
    first = small[:, 2 * nrhs : 3 * nrhs]
    weights = jnp.concatenate([alpha, carried + first], axis=0)
    multipliers_out[0] = sign[...] * combine(
        weights, jnp.concatenate([precond[...], old_precond[...]], axis=0)
    )
    weights = jnp.concatenate([alpha, carried], axis=0)
    change = combine(weights, jnp.concatenate([whole, old_image[...]], axis=0))
    residual_out[0] = sign[...] * (residual[...] - change)


VMEM = pl.BlockSpec(memory_space=pltpu.VMEM)
HBM = pl.BlockSpec(memory_space=pltpu.HBM)


def call(body, shapes, *args, specs=None, scratch=(), flops=0):
    shapes = [jax.ShapeDtypeStruct(shape, dtype) for shape, dtype in shapes]
    moved = sum(arg.size * arg.dtype.itemsize for arg in args)
    return pl.pallas_call(
        body,
        out_shape=shapes,
        in_specs=specs or [VMEM] * len(args),
        out_specs=[VMEM] * len(shapes),
        scratch_shapes=list(scratch),
        compiler_params=pltpu.CompilerParams(vmem_limit_bytes=16 << 20),
        cost_estimate=pl.CostEstimate(flops=flops, bytes_accessed=moved, transcendentals=0),
    )(*args)


def local(count, groups, dual_rhs, dual_ops, prec_ops, corner_coupling, corner_map, signs, coarse_inverse):
    nrhs, width = dual_rhs.shape[1:]
    half = width // 2
    corners = coarse_inverse.shape[0]
    inner, outer = inner_pairs(count, groups), outer_pairs(count, groups)
    steps = rotations(count, groups)
    dense_shape = ((nrhs, corners + TILE), F32)
    slots = corner_map.shape[1]
    flops = 2 * nrhs * width * width

    def permute(values, pairs):
        return lax.ppermute(values, AXES, pairs)

    def exchange(to_inner, to_outer):
        from_outer = permute(to_outer, outer)
        return permute(to_inner, inner), from_outer

    def densify(tiles, maps):
        body = functools.partial(dense_kernel, slots, corners)
        return call(body, [dense_shape], tiles, maps, flops=flops)[0]

    def region(tile, to_inner, to_outer, maps=None, follow=None):
        from_outer = permute(to_outer, outer)
        got = permute(to_inner, inner)
        even = lax.axis_index("blk") % 2 == 0
        values = merged(tile, got[:, got.shape[1] - TILE :], even, 2 * slots + 4 * nrhs)
        known = maps
        left, right = None, None
        for index, turns in enumerate(steps):
            if index > 0:
                if left.shape[1] == TILE and 8 * MOST < 2 * left.shape[0] * (1 + len(turns)):
                    known = known or (left, right)
                    left, right = densify(left, known[0]), densify(right, known[1])
                if left.shape[1] == TILE:
                    values = jnp.concatenate([left, right], axis=0)
                else:
                    values = left + right
            if follow is None and index == len(steps) - 1:
                values, from_outer = lax.optimization_barrier((values, from_outer))
                result = (got, from_outer)
            if follow is not None and index == max(len(steps) - 2, 0):
                *kept, to_inner, to_outer = follow(got, from_outer)
                values, to_inner, to_outer = lax.optimization_barrier((values, to_inner, to_outer))
                result = (*exchange(to_inner, to_outer), *kept)
            left = values
            terms = [permute(values, pairs) for pairs in turns]
            right = jnp.concatenate(terms, axis=0) if left.shape[1] == TILE else sum(terms[1:], terms[0])
        known = known or (left, right)
        if left.shape[1] == TILE:
            left = densify(left, known[0])
        return known, (left, right, known[1], *result)

    wide = ((nrhs, width), F32)
    face = ((nrhs, half), F32)
    pieces = 4
    product, to_inner, to_outer, residual0, sign, couple, map_row, *extras, held = call(
        functools.partial(start_kernel, count),
        [
            wide, face, face, wide, ((1, width), F32), (corner_coupling.shape[1:], BF16),
            ((1, 128), F32), face, face,
            ((pieces, width // pieces, width), BF16),
        ],
        *[pltpu.with_memory_space_constraint(arg, pltpu.HBM) for arg in (dual_rhs, signs, prec_ops, corner_coupling, corner_map)],
        specs=[HBM] * 5,
        scratch=[
            pltpu.VMEM(dual_rhs.shape, F32),
            pltpu.VMEM(signs.shape, jnp.int32),
            pltpu.VMEM(corner_coupling.shape, BF16),
            pltpu.VMEM(corner_map.shape, jnp.int32),
            pltpu.SemaphoreType.DMA((pieces + 4,)),
        ],
        flops=flops,
    )
    (loaded,) = call(
        load_kernel,
        [((width, width), BF16)],
        pltpu.with_memory_space_constraint(dual_ops, pltpu.HBM), sign,
        specs=[HBM, VMEM],
        scratch=[pltpu.SemaphoreType.DMA((pieces,))],
    )
    tile_shape = ((nrhs, TILE), F32)
    precond0, image0, tile, to_inner, to_outer = call(
        functools.partial(first_kernel, count),
        [wide, wide, tile_shape, ((nrhs, width + TILE), F32), wide],
        product, *exchange(to_inner, to_outer), residual0, loaded, couple, map_row, *extras,
        flops=flops,
    )
    square = ((corners, corners), BF16)
    coarse_parts = call(prepare_kernel, [square, square], coarse_inverse, flops=corners * corners)
    rows = nrhs + 2 * slots + 8

    def follow(got, from_outer):
        return call(
            functools.partial(follow_kernel, count),
            [
                wide, wide, ((2 * slots, width), F32), ((2 * slots, width), BF16), ((1, 128), F32),
                ((rows, half), F32), ((rows, half), F32),
            ],
            image0, got, from_outer, couple, map_row, held,
            flops=5 * flops,
        )

    maps, gathered = region(tile, to_inner, to_outer, follow=follow)
    columns, index = gathered[-2:]
    sums = ((nrhs, corners), F32)
    sums0, solved0, residual1, whole0, precond1, image1, small, tile, to_inner, to_outer = call(
        functools.partial(middle_kernel, count, corners),
        [sums, sums, wide, wide, wide, wide, ((nrhs, 128), F32), tile_shape, ((nrhs, half + TILE), F32), face],
        *gathered, precond0, image0, residual0, loaded, couple, *coarse_parts,
        flops=flops,
    )
    _, gathered = region(tile, to_inner, to_outer, maps=maps)
    whole_out = ((1, nrhs, width), F32)
    return tuple(
        call(
            functools.partial(final_kernel, count, corners),
            [whole_out, whole_out],
            *gathered, precond1, image1, residual1, precond0, whole0, sums0, solved0, small,
            columns, index, sign, *coarse_parts,
            flops=flops,
        )
    )


def solution(mesh):
    in_specs = (
        P("grp", None, "blk"),
        P("grp", "blk", None),
        P("grp", "blk", None),
        P("grp", "blk", None),
        P("grp", "blk"),
        P("grp", "blk"),
        P(),
    )
    out_specs = (P("grp", None, "blk"), P("grp", None, "blk"))
    return jax.shard_map(
        functools.partial(local, mesh.shape["blk"], mesh.shape["grp"]),
        mesh=mesh,
        in_specs=in_specs,
        out_specs=out_specs,
        check_vma=False,
    )
```

time: 63.7 us -> 51.1 us (0.80)
  waiting for transfers between devices: 22 us -> 14.5 us
  local copies, waits for them, and re-layouts: 4.52 us -> 0.01 us
  starting transfers between devices: 25.2 us -> 22.6 us
  Pallas kernels: 10.9 us -> 12.9 us
    ppermute x16, waiting for transfers between devices: 22 us -> 14.5 us  [permute(): return lax.ppermute(values, AXES, pairs)]
    unnamed x20 -> x3, local copies, waits for them, and re-layouts: 4.52 us -> 0.01 us
    ppermute x16, starting transfers between devices: 25.2 us -> 22.6 us  [permute(): return lax.ppermute(values, AXES, pairs)]
    pallas_call x7 -> x9, Pallas kernels: 10.9 us -> 12.9 us  [call(): pl.pallas_call(body, out_shape=shapes, in_specs=specs or [VMEM] * len(arg...]
  transfers between devices with their start and end apart: 16 -> 16, of which waited for: 12 -> 12; matrix products, arithmetic and copies ran while one was open for 0% -> 0% of each run, Pallas kernels for 3% -> 7%
where the time goes in v3:
time: 51.1 us; the launch traced here: 50.9 us
  starting transfers between devices  22.6 us (44%)
  waiting for transfers between devices  14.5 us (28%)
  Pallas kernels  12.9 us (25%)
  between operations  0.69 us (1%)
    ppermute x16, starting transfers between devices, permute(): return lax.ppermute(values, AXES, pairs)  22.6 us
    ppermute x16, waiting for transfers between devices, permute(): return lax.ppermute(values, AXES, pairs)  14.5 us
    pallas_call x9, Pallas kernels, call(): pl.pallas_call(body, out_shape=shapes, in_specs=specs or [VMEM] * len(arg...  12.9 us
  transfers between devices with their start and end apart: 16, of which 12 were waited for; matrix products, arithmetic and copies ran while one was open for 0% of the time, Pallas kernels for 7%

profile of v3, /device:TPU:0, one launch (start us, length us, event | category | flops | bytes accessed | tf_op | source)
XLA Modules:
  0.0 50.9 jit_solution(2128589505110723558)
XLA Ops:
  0.6 1.9 %shard_map.86 = (f32[16,1024]{1,0:T(8,128)S(1)}, f32[16,512]{1,0:T(8,128)S(1)}, f32[16,512]{1,0:T(8,128)S(1)}, f32[16,1024]{1,0:T(8,128)S(1)}, f32[1,1024]{1,0:T...) custom-call(f32[1,16,1024]{2,1,0:T(8,128)} %rhs.1, ...), custom_call_target="tpu_custom_call" | custom-call | flops 33554432 | bytes 2191456 | tf_op jit(solution)/shard_map/pallas_call | solution.py:560
  2.5 0.5 %collective-permute-start = (f32[16,512]{1,0:T(8,128)S(1)}, f32[16,512]{1,0:T(8,128)S(1)}, u32[]{:S(2)}, u32[]{:S(2)}) collective-permute-start(f32[16,512]{1,0:T(8,128)S(1)} %get-tuple-element.42), channel_id=1, source_target_pairs={{0,2},{1,3},{2,0},{3,1},{4,6},{5,7},{6,4},{7,5},{8,10},{9,11},{10,... | collective-permute-start | bytes 98312 | tf_op jit(solution)/shard_map/ppermute | solution.py:582
  3.1 2.6 %collective-permute-start.1 = (f32[16,512]{1,0:T(8,128)S(1)}, f32[16,512]{1,0:T(8,128)S(1)}, u32[]{:S(2)}, u32[]{:S(2)}) collective-permute-start(f32[16,512]{1,0:T(8,128)S(1)} %get-tuple-element.43), channel_id=1, source_target_pairs={{0,1},{1,0},{2,4},{3,5},{4,2},{5,3},{6,8},{7,9},{8,6},{9,7},{10,12... | collective-permute-start | bytes 98312 | tf_op jit(solution)/shard_map/ppermute | solution.py:582
  5.6 1.5 %shard_map.87.blocks = bf16[1024,1024]{1,0:T(8,128)(2,1)S(1)} custom-call(bf16[1,1024,1024]{2,1,0:T(8,128)(2,1)} %blocks.3, f32[1,1024]{1,0:T(1,128)S(1)} %get-tuple-element.45.after.sign), custom_call_target="tpu_custom_call" | custom-call | bytes 2101248 | tf_op jit(solution)/shard_map/pallas_call | solution.py:560
  7.2 0.0 collective-permute-done.from_inner
  7.2 0.3 collective-permute-done.1.from_outer
  7.5 0.0 copy-start
  7.5 0.7 %shard_map.88 = (f32[16,1024]{1,0:T(8,128)S(1)}, f32[16,1024]{1,0:T(8,128)S(1)}, f32[16,128]{1,0:T(8,128)S(1)}, f32[16,1152]{1,0:T(8,128)S(1)}, f32[16,1024]{1,0:T(8,128)S(1)}) custom-call(f32[16,1024]{1,0:T(8,128)S(1)} %get-tuple-element.41.product, f32[16,512]{1,0:T(8,128)S(1)} %collective-permute-done.from_inner, ...), custom_call_target="tpu_custom_call" | custom-call | flops 33554432 | bytes 2384384 | tf_op jit(solution)/shard_map/pallas_call | solution.py:560
  8.2 0.1 collective-permute-start.2
  8.4 1.1 %collective-permute-done.2.got = f32[16,1152]{1,0:T(8,128)S(1)} collective-permute-done((f32[16,1152]{1,0:T(8,128)S(1)}, f32[16,1152]{1,0:T(8,128)S(1)}, u32[]{:S(2)}, u32[]{:S(2)}) %collective-permute-start.2) | collective-permute-done | bytes 73760 | tf_op jit(solution)/shard_map/ppermute | solution.py:582
  9.5 0.1 select_add_fusion.1
  9.6 2.3 %collective-permute-start.3 = (f32[16,128]{1,0:T(8,128)S(1)}, f32[16,128]{1,0:T(8,128)S(1)}, u32[]{:S(2)}, u32[]{:S(2)}) collective-permute-start(f32[16,128]{1,0:T(8,128)S(1)} %select_add_fusion.1), channel_id=1, source_target_pairs={{0,10},{1,11},{2,8},{3,9},{4,14},{5,15},{6,12},{7,13},{8,2},{9,3},... | collective-permute-start | bytes 24584 | tf_op jit(solution)/shard_map/ppermute | solution.py:582
  11.8 1.5 %collective-permute-start.5 = (f32[16,1024]{1,0:T(8,128)S(1)}, f32[16,1024]{1,0:T(8,128)S(1)}, u32[]{:S(2)}, u32[]{:S(2)}) collective-permute-start(f32[16,1024]{1,0:T(8,128)S(1)} %get-tuple-element.53), channel_id=1, source_target_pairs={{0,1},{1,0},{2,4},{3,5},{4,2},{5,3},{6,8},{7,9},{8,6},{9,7},{10,12... | collective-permute-start | bytes 196616 | tf_op jit(solution)/shard_map/ppermute | solution.py:582
  13.3 0.0 collective-permute-done.3
  13.3 2.6 %collective-permute-start.4 = (f32[32,128]{1,0:T(8,128)S(1)}, f32[32,128]{1,0:T(8,128)S(1)}, u32[]{:S(2)}, u32[]{:S(2)}) collective-permute-start(f32[32,128]{1,0:T(8,128)S(1)} %pad_maximum_fusion.3), channel_id=1, source_target_pairs={{0,18},{1,19},{2,16},{3,17},{4,22},{5,23},{6,20},{7,21},{8,26},{9,... | collective-permute-start | bytes 49160 | tf_op jit(solution)/shard_map/ppermute | solution.py:582
  15.9 0.2 collective-permute-done.5.from_outer
  16.1 0.5 shard_map.89
  16.6 0.8 %collective-permute-done.4 = f32[32,128]{1,0:T(8,128)S(1)} collective-permute-done((f32[32,128]{1,0:T(8,128)S(1)}, f32[32,128]{1,0:T(8,128)S(1)}, u32[]{:S(2)}, u32[]{:S(2)}) %collective-permute-start.4) | collective-permute-done | bytes 16416 | tf_op jit(solution)/shard_map/ppermute | solution.py:582
  17.4 1.4 %collective-permute-start.6 = (f32[64,128]{1,0:T(8,128)S(1)}, f32[64,128]{1,0:T(8,128)S(1)}, u32[]{:S(2)}, u32[]{:S(2)}) collective-permute-start(f32[64,128]{1,0:T(8,128)S(1)} %pad_maximum_fusion.1), channel_id=1, source_target_pairs={{0,3},{1,2},{2,1},{3,0},{4,7},{5,6},{6,5},{7,4},{8,11},{9,10},{10,... | collective-permute-start | bytes 98312 | tf_op jit(solution)/shard_map/ppermute | solution.py:582
  18.9 0.1 collective-permute-start.8
  19.0 0.6 %collective-permute-start.9 = (f32[72,512]{1,0:T(8,128)S(1)}, f32[72,512]{1,0:T(8,128)S(1)}, u32[]{:S(2)}, u32[]{:S(2)}) collective-permute-start(f32[72,512]{1,0:T(8,128)S(1)} %get-tuple-element.59), channel_id=1, source_target_pairs={{0,1},{1,0},{2,4},{3,5},{4,2},{5,3},{6,8},{7,9},{8,6},{9,7},{10,12... | collective-permute-start | bytes 442376 | tf_op jit(solution)/shard_map/ppermute | solution.py:582
  19.6 1.2 %collective-permute-done.6 = f32[64,128]{1,0:T(8,128)S(1)} collective-permute-done((f32[64,128]{1,0:T(8,128)S(1)}, f32[64,128]{1,0:T(8,128)S(1)}, u32[]{:S(2)}, u32[]{:S(2)}) %collective-permute-start.6) | collective-permute-done | bytes 32800 | tf_op jit(solution)/shard_map/ppermute | solution.py:582
  20.8 1.8 %collective-permute-start.7 = (f32[128,128]{1,0:T(8,128)S(1)}, f32[128,128]{1,0:T(8,128)S(1)}, u32[]{:S(2)}, u32[]{:S(2)}) collective-permute-start(f32[128,128]{1,0:T(8,128)S(1)} %constant_dynamic-update-slice_fusion.tiles.maps), channel_id=1, source_target_pairs={{0,6},{1,7},{2,4},{3,5},{4,2},{5,3},{6,0},{7,1},{8,14},{9,15},{10,... | collective-permute-start | bytes 196616 | tf_op jit(solution)/shard_map/ppermute | solution.py:582
  22.5 0.0 copy-done
  22.5 0.4 shard_map.91
  22.9 0.5 shard_map.90.left
  23.4 2.5 %collective-permute-done.7.right.maps = f32[128,128]{1,0:T(8,128)S(1)} collective-permute-done((f32[128,128]{1,0:T(8,128)S(1)}, f32[128,128]{1,0:T(8,128)S(1)}, u32[]{:S(2)}, u32[]{:S(2)}) %collective-permute-start.7) | collective-permute-done | bytes 65568 | tf_op jit(solution)/shard_map/ppermute | solution.py:582
  25.9 0.0 collective-permute-done.8.from_inner
  25.9 0.0 collective-permute-done.9.from_outer
  25.9 3.3 %shard_map.92 = (f32[16,768]{1,0:T(8,128)S(1)}, f32[16,768]{1,0:T(8,128)S(1)}, f32[16,1024]{1,0:T(8,128)S(1)}, f32[16,1024]{1,0:T(8,128)S(1)}, f32[16,1024]{1,0:...) custom-call(f32[16,896]{1,0:T(8,128)S(1)} %shard_map.90.left, ...), custom_call_target="tpu_custom_call" | custom-call | flops 33554432 | bytes 5587456 | tf_op jit(solution)/shard_map/pallas_call | solution.py:560
  29.1 0.4 collective-permute-start.10
  29.5 0.9 %collective-permute-done.10.got = f32[16,640]{1,0:T(8,128)S(1)} collective-permute-done((f32[16,640]{1,0:T(8,128)S(1)}, f32[16,640]{1,0:T(8,128)S(1)}, u32[]{:S(2)}, u32[]{:S(2)}) %collective-permute-start.10) | collective-permute-done | bytes 40992 | tf_op jit(solution)/shard_map/ppermute | solution.py:582
  30.4 0.1 select_add_fusion
  30.5 2.3 %collective-permute-start.11 = (f32[16,128]{1,0:T(8,128)S(1)}, f32[16,128]{1,0:T(8,128)S(1)}, u32[]{:S(2)}, u32[]{:S(2)}) collective-permute-start(f32[16,128]{1,0:T(8,128)S(1)} %select_add_fusion), channel_id=1, source_target_pairs={{0,10},{1,11},{2,8},{3,9},{4,14},{5,15},{6,12},{7,13},{8,2},{9,3},... | collective-permute-start | bytes 24584 | tf_op jit(solution)/shard_map/ppermute | solution.py:582
  32.8 1.4 %collective-permute-done.11 = f32[16,128]{1,0:T(8,128)S(1)} collective-permute-done((f32[16,128]{1,0:T(8,128)S(1)}, f32[16,128]{1,0:T(8,128)S(1)}, u32[]{:S(2)}, u32[]{:S(2)}) %collective-permute-start.11) | collective-permute-done | bytes 8224 | tf_op jit(solution)/shard_map/ppermute | solution.py:582
  34.1 2.7 %collective-permute-start.12 = (f32[32,128]{1,0:T(8,128)S(1)}, f32[32,128]{1,0:T(8,128)S(1)}, u32[]{:S(2)}, u32[]{:S(2)}) collective-permute-start(f32[32,128]{1,0:T(8,128)S(1)} %pad_maximum_fusion.4), channel_id=1, source_target_pairs={{0,18},{1,19},{2,16},{3,17},{4,22},{5,23},{6,20},{7,21},{8,26},{9,... | collective-permute-start | bytes 49160 | tf_op jit(solution)/shard_map/ppermute | solution.py:582
  36.9 1.4 %collective-permute-done.12 = f32[32,128]{1,0:T(8,128)S(1)} collective-permute-done((f32[32,128]{1,0:T(8,128)S(1)}, f32[32,128]{1,0:T(8,128)S(1)}, u32[]{:S(2)}, u32[]{:S(2)}) %collective-permute-start.12) | collective-permute-done | bytes 16416 | tf_op jit(solution)/shard_map/ppermute | solution.py:582
  38.3 0.4 collective-permute-start.13
  38.7 1.4 %collective-permute-start.14 = (f32[16,512]{1,0:T(8,128)S(1)}, f32[16,512]{1,0:T(8,128)S(1)}, u32[]{:S(2)}, u32[]{:S(2)}) collective-permute-start(f32[16,512]{1,0:T(8,128)S(1)} %get-tuple-element.70), channel_id=1, source_target_pairs={{0,1},{1,0},{2,4},{3,5},{4,2},{5,3},{6,8},{7,9},{8,6},{9,7},{10,12... | collective-permute-start | bytes 98312 | tf_op jit(solution)/shard_map/ppermute | solution.py:582
  40.1 1.6 %collective-permute-done.13 = f32[64,128]{1,0:T(8,128)S(1)} collective-permute-done((f32[64,128]{1,0:T(8,128)S(1)}, f32[64,128]{1,0:T(8,128)S(1)}, u32[]{:S(2)}, u32[]{:S(2)}) %collective-permute-start.13) | collective-permute-done | bytes 32800 | tf_op jit(solution)/shard_map/ppermute | solution.py:582
  41.7 1.0 %collective-permute-done.14.from_outer = f32[16,512]{1,0:T(8,128)S(1)} collective-permute-done((f32[16,512]{1,0:T(8,128)S(1)}, f32[16,512]{1,0:T(8,128)S(1)}, u32[]{:S(2)}, u32[]{:S(2)}) %collective-permute-start.14) | collective-permute-done | bytes 32800 | tf_op jit(solution)/shard_map/ppermute | solution.py:582
  42.6 1.9 %collective-permute-start.15 = (f32[128,128]{1,0:T(8,128)S(1)}, f32[128,128]{1,0:T(8,128)S(1)}, u32[]{:S(2)}, u32[]{:S(2)}) collective-permute-start(f32[128,128]{1,0:T(8,128)S(1)} %pad_maximum_fusion.tiles), channel_id=1, source_target_pairs={{0,6},{1,7},{2,4},{3,5},{4,2},{5,3},{6,0},{7,1},{8,14},{9,15},{10,... | collective-permute-start | bytes 196616 | tf_op jit(solution)/shard_map/ppermute | solution.py:582
  44.6 0.5 shard_map.93.left
  45.0 2.1 %collective-permute-done.15.right = f32[128,128]{1,0:T(8,128)S(1)} collective-permute-done((f32[128,128]{1,0:T(8,128)S(1)}, f32[128,128]{1,0:T(8,128)S(1)}, u32[]{:S(2)}, u32[]{:S(2)}) %collective-permute-start.15) | collective-permute-done | bytes 65568 | tf_op jit(solution)/shard_map/ppermute | solution.py:582
  47.2 3.7 %shard_map.94 = (f32[1,16,1024]{2,1,0:T(8,128)}, f32[1,16,1024]{2,1,0:T(8,128)}) custom-call(f32[16,896]{1,0:T(8,128)S(1)} %shard_map.93.left, f32[128,128]{1,0:T(8,128)S(1)} %collective-permute-done.15.right, f32[128,128]{1,0:T(8,128)S(1)} %collective-permute-done.7.right.maps, f32[16,640]{1,0:T(8,128)S(1)} %collective-permute-done.10.got, ...), custom_call_target="tpu_custom_call" | custom-call | flops 33554432 | bytes 3158528 | tf_op jit(solution)/shard_map/pallas_call | solution.py:560
  (9 shorter events, 0.0 us)
Async XLA Ops:
  2.5 4.6 %collective-permute-start = (f32[16,512]{1,0:T(8,128)S(1)}, f32[16,512]{1,0:T(8,128)S(1)}, u32[]{:S(2)}, u32[]{:S(2)}) collective-permute-start(f32[16,512]{1,0:T(8,128)S(1)} %get-tuple-element.42), channel_id=1, source_target_pairs={{0,2},{1,3},{2,0},{3,1},{4,6},{5,7},{6,4},{7,5},{8,10},{9,11},{10,... | collective-permute-start | bytes 98312 | tf_op jit(solution)/shard_map/ppermute | solution.py:582
  3.1 4.5 %collective-permute-start.1 = (f32[16,512]{1,0:T(8,128)S(1)}, f32[16,512]{1,0:T(8,128)S(1)}, u32[]{:S(2)}, u32[]{:S(2)}) collective-permute-start(f32[16,512]{1,0:T(8,128)S(1)} %get-tuple-element.43), channel_id=1, source_target_pairs={{0,1},{1,0},{2,4},{3,5},{4,2},{5,3},{6,8},{7,9},{8,6},{9,7},{10,12... | collective-permute-start | bytes 98312 | tf_op jit(solution)/shard_map/ppermute | solution.py:582
  7.5 15.0 %copy-start = (f32[768,768]{1,0:T(8,128)S(1)}, f32[768,768]{1,0:T(8,128)}, u32[]{:S(2)}) copy-start(f32[768,768]{1,0:T(8,128)} %coarse.1) | copy-start | bytes 7077892
  8.2 1.3 %collective-permute-start.2 = (f32[16,1152]{1,0:T(8,128)S(1)}, f32[16,1152]{1,0:T(8,128)S(1)}, u32[]{:S(2)}, u32[]{:S(2)}) collective-permute-start(f32[16,1152]{1,0:T(8,128)S(1)} %get-tuple-element.51), channel_id=1, source_target_pairs={{0,2},{1,3},{2,0},{3,1},{4,6},{5,7},{6,4},{7,5},{8,10},{9,11},{10,... | collective-permute-start | bytes 221192 | tf_op jit(solution)/shard_map/ppermute | solution.py:582
  9.6 3.8 %collective-permute-start.3 = (f32[16,128]{1,0:T(8,128)S(1)}, f32[16,128]{1,0:T(8,128)S(1)}, u32[]{:S(2)}, u32[]{:S(2)}) collective-permute-start(f32[16,128]{1,0:T(8,128)S(1)} %select_add_fusion.1), channel_id=1, source_target_pairs={{0,10},{1,11},{2,8},{3,9},{4,14},{5,15},{6,12},{7,13},{8,2},{9,3},... | collective-permute-start | bytes 24584 | tf_op jit(solution)/shard_map/ppermute | solution.py:582
  11.8 4.3 %collective-permute-start.5 = (f32[16,1024]{1,0:T(8,128)S(1)}, f32[16,1024]{1,0:T(8,128)S(1)}, u32[]{:S(2)}, u32[]{:S(2)}) collective-permute-start(f32[16,1024]{1,0:T(8,128)S(1)} %get-tuple-element.53), channel_id=1, source_target_pairs={{0,1},{1,0},{2,4},{3,5},{4,2},{5,3},{6,8},{7,9},{8,6},{9,7},{10,12... | collective-permute-start | bytes 196616 | tf_op jit(solution)/shard_map/ppermute | solution.py:582
  13.3 4.1 %collective-permute-start.4 = (f32[32,128]{1,0:T(8,128)S(1)}, f32[32,128]{1,0:T(8,128)S(1)}, u32[]{:S(2)}, u32[]{:S(2)}) collective-permute-start(f32[32,128]{1,0:T(8,128)S(1)} %pad_maximum_fusion.3), channel_id=1, source_target_pairs={{0,18},{1,19},{2,16},{3,17},{4,22},{5,23},{6,20},{7,21},{8,26},{9,... | collective-permute-start | bytes 49160 | tf_op jit(solution)/shard_map/ppermute | solution.py:582
  17.4 3.3 %collective-permute-start.6 = (f32[64,128]{1,0:T(8,128)S(1)}, f32[64,128]{1,0:T(8,128)S(1)}, u32[]{:S(2)}, u32[]{:S(2)}) collective-permute-start(f32[64,128]{1,0:T(8,128)S(1)} %pad_maximum_fusion.1), channel_id=1, source_target_pairs={{0,3},{1,2},{2,1},{3,0},{4,7},{5,6},{6,5},{7,4},{8,11},{9,10},{10,... | collective-permute-start | bytes 98312 | tf_op jit(solution)/shard_map/ppermute | solution.py:582
  18.9 7.0 %collective-permute-start.8 = (f32[72,512]{1,0:T(8,128)S(1)}, f32[72,512]{1,0:T(8,128)S(1)}, u32[]{:S(2)}, u32[]{:S(2)}) collective-permute-start(f32[72,512]{1,0:T(8,128)S(1)} %get-tuple-element.58), channel_id=1, source_target_pairs={{0,2},{1,3},{2,0},{3,1},{4,6},{5,7},{6,4},{7,5},{8,10},{9,11},{10,... | collective-permute-start | bytes 442376 | tf_op jit(solution)/shard_map/ppermute | solution.py:582
  19.0 6.9 %collective-permute-start.9 = (f32[72,512]{1,0:T(8,128)S(1)}, f32[72,512]{1,0:T(8,128)S(1)}, u32[]{:S(2)}, u32[]{:S(2)}) collective-permute-start(f32[72,512]{1,0:T(8,128)S(1)} %get-tuple-element.59), channel_id=1, source_target_pairs={{0,1},{1,0},{2,4},{3,5},{4,2},{5,3},{6,8},{7,9},{8,6},{9,7},{10,12... | collective-permute-start | bytes 442376 | tf_op jit(solution)/shard_map/ppermute | solution.py:582
  20.8 5.1 %collective-permute-start.7 = (f32[128,128]{1,0:T(8,128)S(1)}, f32[128,128]{1,0:T(8,128)S(1)}, u32[]{:S(2)}, u32[]{:S(2)}) collective-permute-start(f32[128,128]{1,0:T(8,128)S(1)} %constant_dynamic-update-slice_fusion.tiles.maps), channel_id=1, source_target_pairs={{0,6},{1,7},{2,4},{3,5},{4,2},{5,3},{6,0},{7,1},{8,14},{9,15},{10,... | collective-permute-start | bytes 196616 | tf_op jit(solution)/shard_map/ppermute | solution.py:582
  29.1 1.3 %collective-permute-start.10 = (f32[16,640]{1,0:T(8,128)S(1)}, f32[16,640]{1,0:T(8,128)S(1)}, u32[]{:S(2)}, u32[]{:S(2)}) collective-permute-start(f32[16,640]{1,0:T(8,128)S(1)} %get-tuple-element.69), channel_id=1, source_target_pairs={{0,2},{1,3},{2,0},{3,1},{4,6},{5,7},{6,4},{7,5},{8,10},{9,11},{10,... | collective-permute-start | bytes 122888 | tf_op jit(solution)/shard_map/ppermute | solution.py:582
  30.5 3.6 %collective-permute-start.11 = (f32[16,128]{1,0:T(8,128)S(1)}, f32[16,128]{1,0:T(8,128)S(1)}, u32[]{:S(2)}, u32[]{:S(2)}) collective-permute-start(f32[16,128]{1,0:T(8,128)S(1)} %select_add_fusion), channel_id=1, source_target_pairs={{0,10},{1,11},{2,8},{3,9},{4,14},{5,15},{6,12},{7,13},{8,2},{9,3},... | collective-permute-start | bytes 24584 | tf_op jit(solution)/shard_map/ppermute | solution.py:582
  34.1 4.2 %collective-permute-start.12 = (f32[32,128]{1,0:T(8,128)S(1)}, f32[32,128]{1,0:T(8,128)S(1)}, u32[]{:S(2)}, u32[]{:S(2)}) collective-permute-start(f32[32,128]{1,0:T(8,128)S(1)} %pad_maximum_fusion.4), channel_id=1, source_target_pairs={{0,18},{1,19},{2,16},{3,17},{4,22},{5,23},{6,20},{7,21},{8,26},{9,... | collective-permute-start | bytes 49160 | tf_op jit(solution)/shard_map/ppermute | solution.py:582
  38.3 3.3 %collective-permute-start.13 = (f32[64,128]{1,0:T(8,128)S(1)}, f32[64,128]{1,0:T(8,128)S(1)}, u32[]{:S(2)}, u32[]{:S(2)}) collective-permute-start(f32[64,128]{1,0:T(8,128)S(1)} %pad_maximum_fusion.2), channel_id=1, source_target_pairs={{0,3},{1,2},{2,1},{3,0},{4,7},{5,6},{6,5},{7,4},{8,11},{9,10},{10,... | collective-permute-start | bytes 98312 | tf_op jit(solution)/shard_map/ppermute | solution.py:582
  38.7 3.9 %collective-permute-start.14 = (f32[16,512]{1,0:T(8,128)S(1)}, f32[16,512]{1,0:T(8,128)S(1)}, u32[]{:S(2)}, u32[]{:S(2)}) collective-permute-start(f32[16,512]{1,0:T(8,128)S(1)} %get-tuple-element.70), channel_id=1, source_target_pairs={{0,1},{1,0},{2,4},{3,5},{4,2},{5,3},{6,8},{7,9},{8,6},{9,7},{10,12... | collective-permute-start | bytes 98312 | tf_op jit(solution)/shard_map/ppermute | solution.py:582
  42.6 4.5 %collective-permute-start.15 = (f32[128,128]{1,0:T(8,128)S(1)}, f32[128,128]{1,0:T(8,128)S(1)}, u32[]{:S(2)}, u32[]{:S(2)}) collective-permute-start(f32[128,128]{1,0:T(8,128)S(1)} %pad_maximum_fusion.tiles), channel_id=1, source_target_pairs={{0,6},{1,7},{2,4},{3,5},{4,2},{5,3},{6,0},{7,1},{8,14},{9,15},{10,... | collective-permute-start | bytes 196616 | tf_op jit(solution)/shard_map/ppermute | solution.py:582

commit v4 on v3

--- a/solution.py
+++ b/solution.py
@@ -229,67 +229,70 @@
     return [rows[:half], rows[half:]]
 
 
-def tile_of(corner, middle, first, second):
-    shared = jnp.concatenate(abreast(corner) + middle + abreast(first), axis=1)
-    return jnp.concatenate([jnp.concatenate([shared, part], axis=1) for part in abreast(second)], axis=0)
-
-
-def merged(own, got, even, lane):
-    rows = lax.broadcasted_iota(jnp.int32, own.shape, 0)
-    mine = (rows < own.shape[0] // 2) == even
-    taken, other = jnp.where(mine, own, got), jnp.where(mine, got, own)
-    return taken + jnp.where(lanes_of(own.shape) < lane, 0.0, other)
-
-
-def untile(tiles, slots):
-    half = tiles.shape[0] // 2
-    count = 2 * half
-    even, odd = tiles[:half], tiles[half:]
-    both = even + odd
-    start = 2 * slots
-    last = start + 4 * count
-    squares = [
-        jnp.concatenate([both[:, at : at + count], both[:, at + count : at + 2 * count]], axis=0)
-        for at in (start, start + 2 * count)
+def tiles_of(even, corner, index, first, second, third):
+    half = first.shape[0] // 2
+    squares = abreast(first) + abreast(second) + abreast(third)
+    used = sum(part.shape[1] for part in squares)
+    squares = jnp.concatenate(squares + [jnp.zeros((half, TILE - used), F32)], axis=1)
+    values = abreast(corner)
+    gap = jnp.zeros((half, 2 * corner.shape[1]), F32)
+    left, right = jnp.concatenate(values + [gap], axis=1), jnp.concatenate([gap] + values, axis=1)
+    row = lax.broadcasted_iota(jnp.int32, (half, index.shape[1]), 0)
+    index = jnp.where(row == jnp.where(even, 0, 1), index, 0.0)
+    rest = jnp.zeros((half, TILE - left.shape[1] - index.shape[1]), F32)
+    return jnp.concatenate(
+        [squares, jnp.concatenate([jnp.where(even, left, right), index, rest], axis=1)], axis=0
+    )
+
+
+def untile(tile):
+    count = 2 * tile.shape[0]
+    return [
+        jnp.concatenate([tile[:, at : at + count], tile[:, at + count : at + 2 * count]], axis=0)
+        for at in (0, 2 * count, 4 * count)
     ]
-    return *squares, jnp.concatenate([even[:, last : last + count], odd[:, last : last + count]], axis=0)
 
 
 def dense(tiles, maps, slots, corners):
     count = tiles.shape[0] // 8
     lane = lanes_of((1, TILE))
     low, up, index = [], [], []
-    totals = [jnp.zeros((8, TILE), F32)] * 2
-    for start in range(0, count, TILE // GROUP):
+
+    def moved(rows, at, to):
+        shift = (to - at) % TILE
+        return pltpu.roll(rows, shift, 1) if shift else rows
+
+    for start in range(0, count, TILE // GROUP // 2):
         parts = [jnp.zeros((8, TILE), F32), jnp.zeros((8, TILE), F32), jnp.full((1, TILE), -1.0, F32)]
-        for turn, at in enumerate(range(start, min(start + TILE // GROUP, count))):
-            tile, name = tiles[8 * at : 8 * at + 8], maps[8 * at : 8 * at + 1]
-            totals[at % 2] = totals[at % 2] + tile
-            here = (lane // GROUP == turn) & (lane % GROUP < slots)
-            shift = GROUP * turn
-            moved = [
-                pltpu.roll(tile, shift, 1) if shift else tile,
-                pltpu.roll(tile, (shift - slots) % TILE, 1),
-                pltpu.roll(name, (shift - 2 * slots) % TILE, 1),
-            ]
-            parts = [jnp.where(here, new, old) for new, old in zip(moved, parts)]
+        for turn in range(TILE // GROUP):
+            at, core = start + turn // 2, turn % 2
+            if at < count:
+                here = (lane // GROUP == turn) & (lane % GROUP < slots)
+                tile = tiles[8 * at : 8 * at + 8]
+                name = maps[8 * at + core : 8 * at + core + 1]
+                new = [
+                    moved(tile, 2 * slots * core, GROUP * turn),
+                    moved(tile, 2 * slots * core + slots, GROUP * turn),
+                    moved(name, 4 * slots, GROUP * turn),
+                ]
+                parts = [jnp.where(here, one, old) for one, old in zip(new, parts)]
         low.append(parts[0])
         up.append(parts[1])
         index.append(parts[2])
     values = jnp.concatenate([jnp.concatenate(low, axis=1), jnp.concatenate(up, axis=1)], axis=0)
     choice = chosen(jnp.concatenate(index, axis=1).astype(jnp.int32), corners)
-    corner_sum = folded(mm(stacked(values), choice, NT))
-    return jnp.concatenate([corner_sum, jnp.concatenate(totals, axis=0)], axis=1)
+    return folded(mm(stacked(values), choice, NT))
 
 
 def dense_kernel(slots, corners, tiles, maps, out):
-    out[...] = dense(tiles[...], maps[...], slots, corners)
+    out[:, :corners] = dense(tiles[8:], maps[8:], slots, corners)
+    out[:, corners:] = jnp.concatenate([tiles[:8], jnp.zeros((out.shape[0] - 8, TILE), F32)], axis=0)
 
 
 def total_of(left, right, maps, slots, corners):
     if right.shape[1] == TILE:
-        return left[...] + dense(right[...], maps[...], slots, corners)
-    return left[...] + right[...]
+        return left[:, :corners] + dense(right[8:], maps[8:], slots, corners), left[:8, corners:] + right[:8]
+    return left[:, :corners] + right[:, :corners], left[:8, corners:] + right[:8, corners:]
 
 
 def face_rows(rows):
@@ -379,9 +382,10 @@
         jnp.concatenate([residual[...], precond], axis=0), jnp.concatenate([precond, image], axis=0)
     )
     slots = couple.shape[0]
-    middle = jnp.concatenate([map_row[:, :slots], jnp.zeros((1, 2 * nrhs - slots), F32)], axis=1)
-    middle = jnp.broadcast_to(middle, (nrhs // 2, 2 * nrhs))
-    tile = tile_of(corner_values(precond, couple[...]), [middle], grams[:nrhs, :nrhs], grams[nrhs:, nrhs:])
+    first, second = grams[:nrhs, :nrhs], grams[nrhs:, nrhs:]
+    tile = tiles_of(
+        even, corner_values(precond, couple[...]), map_row[:, :slots], first, second, jnp.zeros_like(first)
+    )
     tile_out[...] = tile
     inner, outer = split(even, image[:, :half], image[:, half:])
     to_inner[:, :half] = inner
@@ -458,7 +462,7 @@
 def middle_kernel(
     count, corners, left, right, maps, from_inner, from_outer, part, product, spread, columns, map_row,
     precond_in, image_in, residual_in, blocks, couple, coarse_high, coarse_low,
-    sums_out, solved_out, residual_out, whole_out, precond_out, image_out, small_out, tile_out, to_inner, to_outer,
+    solved_out, residual_out, whole_out, precond_out, image_out, small_out, tile_out, to_inner, to_outer,
 ):
     blk = lax.axis_index("blk")
     even = blk % 2 == 0
@@ -466,9 +470,8 @@
     half = width // 2
     live = live_mask(blk, count, width)
     slots = couple.shape[0]
-    summed = total_of(left, right, maps, slots, corners)
-    corner_sum = summed[:, :corners]
-    _, gram, energy = untile(summed[:, corners:], slots)
+    corner_sum, squares = total_of(left, right, maps, slots, corners)
+    gram, energy, _ = untile(squares)
     solved = coarse_solve(corner_sum, (coarse_high[...], coarse_low[...]))
     energy = energy + dots(corner_sum, solved)
     unit = (lax.broadcasted_iota(jnp.int32, (nrhs, nrhs), 0) == lanes_of((nrhs, nrhs))).astype(F32)
@@ -488,22 +491,26 @@
         for turn, side in enumerate(sides, 1)
     ]
     change = live * (own - jnp.concatenate(others, axis=1))
-    residual = residual_in[...] - combine(alpha, whole)
-    precond = precond_in[...] - combine(alpha, change)
+    change = combine(alpha, jnp.concatenate([whole, change], axis=1))
+    residual = residual_in[...] - change[:, :width]
+    precond = precond_in[...] - change[:, width:]
 
     image = mm(precond.astype(BF16), blocks[...], NN)
     left = jnp.concatenate([residual, precond, precond_in[...], image_in[...]], axis=0)
     grams = dots(left, jnp.concatenate([precond, image], axis=0))
-    middle = abreast(grams[2 * nrhs : 3 * nrhs, nrhs:] + grams[3 * nrhs :, :nrhs])
-    tile = tile_of(
-        corner_values(precond, couple[...]), middle, grams[:nrhs, :nrhs], grams[nrhs : 2 * nrhs, nrhs:]
+    tile = tiles_of(
+        even,
+        corner_values(precond, couple[...]),
+        jnp.zeros((1, slots), F32),
+        grams[:nrhs, :nrhs],
+        grams[nrhs : 2 * nrhs, nrhs:],
+        grams[2 * nrhs : 3 * nrhs, nrhs:] + grams[3 * nrhs :, :nrhs],
     )
     tile_out[...] = tile
     inner, outer = split(even, image[:, :half], image[:, half:])
     to_inner[:, :half] = inner
     to_inner[:, half:] = tile
     to_outer[...] = outer
-    sums_out[...] = corner_sum
     solved_out[...] = solved
     residual_out[...] = residual
     whole_out[...] = whole
@@ -513,7 +520,7 @@
 
 
 def final_kernel(
-    count, corners, left, right, maps, got, from_outer, precond, image, residual, old_precond, old_image, old_sums,
+    count, corners, left, right, maps, got, from_outer, precond, image, residual, old_precond, old_image,
     old_solved, small, columns, map_row, sign, coarse_high, coarse_low,
     multipliers_out, residual_out,
 ):
@@ -522,32 +529,22 @@
     nrhs, width = precond.shape
     live = live_mask(blk, count, width)
     slots = columns.shape[0] // 2
-    summed = total_of(left, right, maps, slots, corners)
-    corner_sum = summed[:, :corners]
-    old_new, gram, new_new = untile(summed[:, corners:], slots)
+    corner_sum, squares = total_of(left, right, maps, slots, corners)
+    gram, new_new, old_new = untile(squares)
     beta = combine(small[:, :nrhs], gram)
     solved = coarse_solve(corner_sum, (coarse_high[...], coarse_low[...]))
-    cross = dots(
-        jnp.concatenate([corner_sum, old_sums[...]], axis=0),
-        jnp.concatenate([solved, old_solved[...]], axis=0),
-    )
-    new_new = new_new + cross[:nrhs, :nrhs]
-    old_new = old_new + cross[nrhs:, :nrhs] + transposed(cross[:nrhs, nrhs:])
     old_old = symmetric(small[:, nrhs : 2 * nrhs])
-    energy = new_new + combine(beta, old_new + combine(old_old, beta))
+    old_new = old_new + 2.0 * dots(old_solved[...], corner_sum)
+    energy = new_new + combine(beta, old_new + combine(old_old, beta)) + dots(corner_sum, solved)
     alpha = eliminate(symmetric(2.0 * energy)[None], gram[None])[0]
     image_beside = joined(even, got[:, : width // 2], from_outer[...])
     at = picked(solved, map_row[...])
     whole = live * (image[...] - image_beside) + against(at[:, : columns.shape[0]], columns[...])
-    carried = combine(transposed(beta), alpha)
-    first = small[:, 2 * nrhs : 3 * nrhs]
-    weights = jnp.concatenate([alpha, carried + first], axis=0)
-    multipliers_out[0] = sign[...] * combine(
-        weights, jnp.concatenate([precond[...], old_precond[...]], axis=0)
-    )
-    weights = jnp.concatenate([alpha, carried], axis=0)
-    change = combine(weights, jnp.concatenate([whole, old_image[...]], axis=0))
-    residual_out[0] = sign[...] * (residual[...] - change)
+    first = combine(small[:, 2 * nrhs : 3 * nrhs], old_precond[...])
+    carried = combine(beta, jnp.concatenate([old_precond[...], old_image[...]], axis=1))
+    change = combine(alpha, jnp.concatenate([precond[...], whole], axis=1) + carried)
+    multipliers_out[0] = sign[...] * (first + change[:, :width])
+    residual_out[0] = sign[...] * (residual[...] - change[:, width:])
 
 
 VMEM = pl.BlockSpec(memory_space=pltpu.VMEM)
@@ -589,22 +586,25 @@
         body = functools.partial(dense_kernel, slots, corners)
         return call(body, [dense_shape], tiles, maps, flops=flops)[0]
 
+    def united(parts):
+        if parts[0].shape[1] != TILE:
+            return sum(parts[1:], parts[0])
+        squares = [part[:8] for part in parts]
+        return jnp.concatenate([sum(squares[1:], squares[0])] + [part[8:] for part in parts], axis=0)
+
     def region(tile, to_inner, to_outer, maps=None, follow=None):
         from_outer = permute(to_outer, outer)
         got = permute(to_inner, inner)
-        even = lax.axis_index("blk") % 2 == 0
-        values = merged(tile, got[:, got.shape[1] - TILE :], even, 2 * slots + 4 * nrhs)
+        values = tile + got[:, got.shape[1] - TILE :]
         known = maps
         left, right = None, None
         for index, turns in enumerate(steps):
             if index > 0:
-                if left.shape[1] == TILE and 8 * MOST < 2 * left.shape[0] * (1 + len(turns)):
+                held = left.shape[0] + right.shape[0] - 16
+                if left.shape[1] == TILE and 8 * MOST < 2 * held * (1 + len(turns)):
                     known = known or (left, right)
                     left, right = densify(left, known[0]), densify(right, known[1])
-                if left.shape[1] == TILE:
-                    values = jnp.concatenate([left, right], axis=0)
-                else:
-                    values = left + right
+                values = united([left, right])
             if follow is None and index == len(steps) - 1:
                 values, from_outer = lax.optimization_barrier((values, from_outer))
                 result = (got, from_outer)
@@ -613,8 +613,7 @@
                 values, to_inner, to_outer = lax.optimization_barrier((values, to_inner, to_outer))
                 result = (*exchange(to_inner, to_outer), *kept)
             left = values
-            terms = [permute(values, pairs) for pairs in turns]
-            right = jnp.concatenate(terms, axis=0) if left.shape[1] == TILE else sum(terms[1:], terms[0])
+            right = united([permute(values, pairs) for pairs in turns])
         known = known or (left, right)
         if left.shape[1] == TILE:
             left = densify(left, known[0])
@@ -672,10 +671,9 @@
 
     maps, gathered = region(tile, to_inner, to_outer, follow=follow)
     columns, index = gathered[-2:]
-    sums = ((nrhs, corners), F32)
-    sums0, solved0, residual1, whole0, precond1, image1, small, tile, to_inner, to_outer = call(
+    solved0, residual1, whole0, precond1, image1, small, tile, to_inner, to_outer = call(
         functools.partial(middle_kernel, count, corners),
-        [sums, sums, wide, wide, wide, wide, ((nrhs, 128), F32), tile_shape, ((nrhs, half + TILE), F32), face],
+        [((nrhs, corners), F32), wide, wide, wide, wide, ((nrhs, 128), F32), tile_shape, ((nrhs, half + TILE), F32), face],
         *gathered, precond0, image0, residual0, loaded, couple, *coarse_parts,
         flops=flops,
     )
@@ -685,7 +683,7 @@
         call(
             functools.partial(final_kernel, count, corners),
             [whole_out, whole_out],
-            *gathered, precond1, image1, residual1, precond0, whole0, sums0, solved0, small,
+            *gathered, precond1, image1, residual1, precond0, whole0, solved0, small,
             columns, index, sign, *coarse_parts,
             flops=flops,
         )

time: 51.1 us -> 49.1 us (0.961)
  waiting for transfers between devices: 14.5 us -> 13 us
  Pallas kernels: 12.9 us -> 12.2 us
    ppermute x16, waiting for transfers between devices: 14.5 us -> 13 us  [permute(): return lax.ppermute(values, AXES, pairs)]
    pallas_call x9, Pallas kernels: 12.9 us -> 12.2 us  [call(): pl.pallas_call(body, out_shape=shapes, in_specs=specs or [VMEM] * len(arg...]
where the time goes in v4:
time: 49.1 us; the launch traced here: 49 us
  starting transfers between devices  23 us (47%)
  waiting for transfers between devices  13 us (26%)
  Pallas kernels  12.2 us (25%)
  between operations  0.71 us (1%)
    ppermute x16, starting transfers between devices, permute(): return lax.ppermute(values, AXES, pairs)  23 us
    ppermute x16, waiting for transfers between devices, permute(): return lax.ppermute(values, AXES, pairs)  13 us
    pallas_call x9, Pallas kernels, call(): pl.pallas_call(body, out_shape=shapes, in_specs=specs or [VMEM] * len(arg...  12.2 us
  transfers between devices with their start and end apart: 16, of which 12 were waited for; matrix products, arithmetic and copies ran while one was open for 0% of the time, Pallas kernels for 7%

profile of v4, /device:TPU:0, one launch (start us, length us, event | category | flops | bytes accessed | tf_op | source)
XLA Modules:
  0.0 49.0 jit_solution(11539844760700331420)
XLA Ops:
  0.6 1.9 %shard_map.86 = (f32[16,1024]{1,0:T(8,128)S(1)}, f32[16,512]{1,0:T(8,128)S(1)}, f32[16,512]{1,0:T(8,128)S(1)}, f32[16,1024]{1,0:T(8,128)S(1)}, f32[1,1024]{1,0:T...) custom-call(f32[1,16,1024]{2,1,0:T(8,128)} %rhs.1, ...), custom_call_target="tpu_custom_call" | custom-call | flops 33554432 | bytes 2191456 | tf_op jit(solution)/shard_map/pallas_call | solution.py:557
  2.6 0.5 %collective-permute-start = (f32[16,512]{1,0:T(8,128)S(1)}, f32[16,512]{1,0:T(8,128)S(1)}, u32[]{:S(2)}, u32[]{:S(2)}) collective-permute-start(f32[16,512]{1,0:T(8,128)S(1)} %get-tuple-element.41), channel_id=1, source_target_pairs={{0,2},{1,3},{2,0},{3,1},{4,6},{5,7},{6,4},{7,5},{8,10},{9,11},{10,... | collective-permute-start | bytes 98312 | tf_op jit(solution)/shard_map/ppermute | solution.py:579
  3.1 2.6 %collective-permute-start.1 = (f32[16,512]{1,0:T(8,128)S(1)}, f32[16,512]{1,0:T(8,128)S(1)}, u32[]{:S(2)}, u32[]{:S(2)}) collective-permute-start(f32[16,512]{1,0:T(8,128)S(1)} %get-tuple-element.42), channel_id=1, source_target_pairs={{0,1},{1,0},{2,4},{3,5},{4,2},{5,3},{6,8},{7,9},{8,6},{9,7},{10,12... | collective-permute-start | bytes 98312 | tf_op jit(solution)/shard_map/ppermute | solution.py:579
  5.6 1.5 %shard_map.87.blocks = bf16[1024,1024]{1,0:T(8,128)(2,1)S(1)} custom-call(bf16[1,1024,1024]{2,1,0:T(8,128)(2,1)} %blocks.3, f32[1,1024]{1,0:T(1,128)S(1)} %get-tuple-element.44.after.sign), custom_call_target="tpu_custom_call" | custom-call | bytes 2101248 | tf_op jit(solution)/shard_map/pallas_call | solution.py:557
  7.2 0.0 collective-permute-done.from_inner
  7.2 0.3 collective-permute-done.1.from_outer
  7.5 0.0 copy-start
  7.5 0.7 %shard_map.88 = (f32[16,1024]{1,0:T(8,128)S(1)}, f32[16,1024]{1,0:T(8,128)S(1)}, f32[16,128]{1,0:T(8,128)S(1)}, f32[16,1152]{1,0:T(8,128)S(1)}, f32[16,1024]{1,0:T(8,128)S(1)}) custom-call(f32[16,1024]{1,0:T(8,128)S(1)} %get-tuple-element.40.product, f32[16,512]{1,0:T(8,128)S(1)} %collective-permute-done.from_inner, ...), custom_call_target="tpu_custom_call" | custom-call | flops 33554432 | bytes 2384384 | tf_op jit(solution)/shard_map/pallas_call | solution.py:557
  8.2 0.2 collective-permute-start.2
  8.4 1.2 %collective-permute-done.2.got = f32[16,1152]{1,0:T(8,128)S(1)} collective-permute-done((f32[16,1152]{1,0:T(8,128)S(1)}, f32[16,1152]{1,0:T(8,128)S(1)}, u32[]{:S(2)}, u32[]{:S(2)}) %collective-permute-start.2) | collective-permute-done | bytes 73760 | tf_op jit(solution)/shard_map/ppermute | solution.py:579
  9.5 2.3 %collective-permute-start.3 = (f32[16,128]{1,0:T(8,128)S(1)}, f32[16,128]{1,0:T(8,128)S(1)}, u32[]{:S(2)}, u32[]{:S(2)}) collective-permute-start(f32[16,128]{1,0:T(8,128)S(1)} %slice_add_fusion.1), channel_id=1, source_target_pairs={{0,10},{1,11},{2,8},{3,9},{4,14},{5,15},{6,12},{7,13},{8,2},{9,3},... | collective-permute-start | bytes 24584 | tf_op jit(solution)/shard_map/ppermute | solution.py:579
  11.8 1.5 %collective-permute-start.5 = (f32[16,1024]{1,0:T(8,128)S(1)}, f32[16,1024]{1,0:T(8,128)S(1)}, u32[]{:S(2)}, u32[]{:S(2)}) collective-permute-start(f32[16,1024]{1,0:T(8,128)S(1)} %get-tuple-element.52), channel_id=1, source_target_pairs={{0,1},{1,0},{2,4},{3,5},{4,2},{5,3},{6,8},{7,9},{8,6},{9,7},{10,12... | collective-permute-start | bytes 196616 | tf_op jit(solution)/shard_map/ppermute | solution.py:579
  13.3 0.0 collective-permute-done.3
  13.3 2.6 %collective-permute-start.4 = (f32[24,128]{1,0:T(8,128)S(1)}, f32[24,128]{1,0:T(8,128)S(1)}, u32[]{:S(2)}, u32[]{:S(2)}) collective-permute-start(f32[24,128]{1,0:T(8,128)S(1)} %pad_maximum_fusion.3), channel_id=1, source_target_pairs={{0,18},{1,19},{2,16},{3,17},{4,22},{5,23},{6,20},{7,21},{8,26},{9,... | collective-permute-start | bytes 36872 | tf_op jit(solution)/shard_map/ppermute | solution.py:579
  15.9 0.2 collective-permute-done.5.from_outer
  16.0 0.5 shard_map.89
  16.5 0.8 %collective-permute-done.4 = f32[24,128]{1,0:T(8,128)S(1)} collective-permute-done((f32[24,128]{1,0:T(8,128)S(1)}, f32[24,128]{1,0:T(8,128)S(1)}, u32[]{:S(2)}, u32[]{:S(2)}) %collective-permute-start.4) | collective-permute-done | bytes 12320 | tf_op jit(solution)/shard_map/ppermute | solution.py:579
  17.4 1.5 %collective-permute-start.6 = (f32[40,128]{1,0:T(8,128)S(1)}, f32[40,128]{1,0:T(8,128)S(1)}, u32[]{:S(2)}, u32[]{:S(2)}) collective-permute-start(f32[40,128]{1,0:T(8,128)S(1)} %pad_maximum_fusion.1), channel_id=1, source_target_pairs={{0,3},{1,2},{2,1},{3,0},{4,7},{5,6},{6,5},{7,4},{8,11},{9,10},{10,... | collective-permute-start | bytes 61448 | tf_op jit(solution)/shard_map/ppermute | solution.py:579
  18.9 0.1 collective-permute-start.8
  19.0 0.6 %collective-permute-start.9 = (f32[72,512]{1,0:T(8,128)S(1)}, f32[72,512]{1,0:T(8,128)S(1)}, u32[]{:S(2)}, u32[]{:S(2)}) collective-permute-start(f32[72,512]{1,0:T(8,128)S(1)} %get-tuple-element.58), channel_id=1, source_target_pairs={{0,1},{1,0},{2,4},{3,5},{4,2},{5,3},{6,8},{7,9},{8,6},{9,7},{10,12... | collective-permute-start | bytes 442376 | tf_op jit(solution)/shard_map/ppermute | solution.py:579
  19.6 1.1 %collective-permute-done.6 = f32[40,128]{1,0:T(8,128)S(1)} collective-permute-done((f32[40,128]{1,0:T(8,128)S(1)}, f32[40,128]{1,0:T(8,128)S(1)}, u32[]{:S(2)}, u32[]{:S(2)}) %collective-permute-start.6) | collective-permute-done | bytes 20512 | tf_op jit(solution)/shard_map/ppermute | solution.py:579
  20.7 1.7 %collective-permute-start.7 = (f32[72,128]{1,0:T(8,128)S(1)}, f32[72,128]{1,0:T(8,128)S(1)}, u32[]{:S(2)}, u32[]{:S(2)}) collective-permute-start(f32[72,128]{1,0:T(8,128)S(1)} %pad_maximum_fusion.tiles.maps), channel_id=1, source_target_pairs={{0,6},{1,7},{2,4},{3,5},{4,2},{5,3},{6,0},{7,1},{8,14},{9,15},{10,... | collective-permute-start | bytes 110600 | tf_op jit(solution)/shard_map/ppermute | solution.py:579
  22.4 0.0 copy-done
  22.4 0.3 shard_map.91
  22.7 0.5 shard_map.90.left
  23.2 2.0 %collective-permute-done.7.right.maps = f32[72,128]{1,0:T(8,128)S(1)} collective-permute-done((f32[72,128]{1,0:T(8,128)S(1)}, f32[72,128]{1,0:T(8,128)S(1)}, u32[]{:S(2)}, u32[]{:S(2)}) %collective-permute-start.7) | collective-permute-done | bytes 36896 | tf_op jit(solution)/shard_map/ppermute | solution.py:579
  25.2 0.0 collective-permute-done.8.from_inner
  25.2 0.0 collective-permute-done.9.from_outer
  25.2 3.2 %shard_map.92 = (f32[16,768]{1,0:T(8,128)S(1)}, f32[16,1024]{1,0:T(8,128)S(1)}, f32[16,1024]{1,0:T(8,128)S(1)}, f32[16,1024]{1,0:T(8,128)S(1)}, f32[16,1024]{1,0...) custom-call(f32[16,896]{1,0:T(8,128)S(1)} %shard_map.90.left, ...), custom_call_target="tpu_custom_call" | custom-call | flops 33554432 | bytes 5530112 | tf_op jit(solution)/shard_map/pallas_call | solution.py:557
  28.4 0.4 collective-permute-start.10
  28.8 0.9 %collective-permute-done.10.got = f32[16,640]{1,0:T(8,128)S(1)} collective-permute-done((f32[16,640]{1,0:T(8,128)S(1)}, f32[16,640]{1,0:T(8,128)S(1)}, u32[]{:S(2)}, u32[]{:S(2)}) %collective-permute-start.10) | collective-permute-done | bytes 40992 | tf_op jit(solution)/shard_map/ppermute | solution.py:579
  29.7 2.3 %collective-permute-start.11 = (f32[16,128]{1,0:T(8,128)S(1)}, f32[16,128]{1,0:T(8,128)S(1)}, u32[]{:S(2)}, u32[]{:S(2)}) collective-permute-start(f32[16,128]{1,0:T(8,128)S(1)} %slice_add_fusion), channel_id=1, source_target_pairs={{0,10},{1,11},{2,8},{3,9},{4,14},{5,15},{6,12},{7,13},{8,2},{9,3},... | collective-permute-start | bytes 24584 | tf_op jit(solution)/shard_map/ppermute | solution.py:579
  32.0 1.4 %collective-permute-done.11 = f32[16,128]{1,0:T(8,128)S(1)} collective-permute-done((f32[16,128]{1,0:T(8,128)S(1)}, f32[16,128]{1,0:T(8,128)S(1)}, u32[]{:S(2)}, u32[]{:S(2)}) %collective-permute-start.11) | collective-permute-done | bytes 8224 | tf_op jit(solution)/shard_map/ppermute | solution.py:579
  33.3 2.7 %collective-permute-start.12 = (f32[24,128]{1,0:T(8,128)S(1)}, f32[24,128]{1,0:T(8,128)S(1)}, u32[]{:S(2)}, u32[]{:S(2)}) collective-permute-start(f32[24,128]{1,0:T(8,128)S(1)} %pad_maximum_fusion.4), channel_id=1, source_target_pairs={{0,18},{1,19},{2,16},{3,17},{4,22},{5,23},{6,20},{7,21},{8,26},{9,... | collective-permute-start | bytes 36872 | tf_op jit(solution)/shard_map/ppermute | solution.py:579
  36.1 1.4 %collective-permute-done.12 = f32[24,128]{1,0:T(8,128)S(1)} collective-permute-done((f32[24,128]{1,0:T(8,128)S(1)}, f32[24,128]{1,0:T(8,128)S(1)}, u32[]{:S(2)}, u32[]{:S(2)}) %collective-permute-start.12) | collective-permute-done | bytes 12320 | tf_op jit(solution)/shard_map/ppermute | solution.py:579
  37.5 0.4 collective-permute-start.13
  37.9 1.4 %collective-permute-start.14 = (f32[16,512]{1,0:T(8,128)S(1)}, f32[16,512]{1,0:T(8,128)S(1)}, u32[]{:S(2)}, u32[]{:S(2)}) collective-permute-start(f32[16,512]{1,0:T(8,128)S(1)} %get-tuple-element.69), channel_id=1, source_target_pairs={{0,1},{1,0},{2,4},{3,5},{4,2},{5,3},{6,8},{7,9},{8,6},{9,7},{10,12... | collective-permute-start | bytes 98312 | tf_op jit(solution)/shard_map/ppermute | solution.py:579
  39.3 1.4 %collective-permute-done.13 = f32[40,128]{1,0:T(8,128)S(1)} collective-permute-done((f32[40,128]{1,0:T(8,128)S(1)}, f32[40,128]{1,0:T(8,128)S(1)}, u32[]{:S(2)}, u32[]{:S(2)}) %collective-permute-start.13) | collective-permute-done | bytes 20512 | tf_op jit(solution)/shard_map/ppermute | solution.py:579
  40.8 1.0 %collective-permute-done.14.from_outer = f32[16,512]{1,0:T(8,128)S(1)} collective-permute-done((f32[16,512]{1,0:T(8,128)S(1)}, f32[16,512]{1,0:T(8,128)S(1)}, u32[]{:S(2)}, u32[]{:S(2)}) %collective-permute-start.14) | collective-permute-done | bytes 32800 | tf_op jit(solution)/shard_map/ppermute | solution.py:579
  41.8 2.3 %collective-permute-start.15 = (f32[72,128]{1,0:T(8,128)S(1)}, f32[72,128]{1,0:T(8,128)S(1)}, u32[]{:S(2)}, u32[]{:S(2)}) collective-permute-start(f32[72,128]{1,0:T(8,128)S(1)} %slice_dynamic-update-slice_fusion.tiles), channel_id=1, source_target_pairs={{0,6},{1,7},{2,4},{3,5},{4,2},{5,3},{6,0},{7,1},{8,14},{9,15},{10,... | collective-permute-start | bytes 110600 | tf_op jit(solution)/shard_map/ppermute | solution.py:579
  44.1 0.5 shard_map.93.left
  44.5 1.3 %collective-permute-done.15.right = f32[72,128]{1,0:T(8,128)S(1)} collective-permute-done((f32[72,128]{1,0:T(8,128)S(1)}, f32[72,128]{1,0:T(8,128)S(1)}, u32[]{:S(2)}, u32[]{:S(2)}) %collective-permute-start.15) | collective-permute-done | bytes 36896 | tf_op jit(solution)/shard_map/ppermute | solution.py:579
  45.8 3.1 %shard_map.94 = (f32[1,16,1024]{2,1,0:T(8,128)}, f32[1,16,1024]{2,1,0:T(8,128)}) custom-call(f32[16,896]{1,0:T(8,128)S(1)} %shard_map.93.left, f32[72,128]{1,0:T(8,128)S(1)} %collective-permute-done.15.right, f32[72,128]{1,0:T(8,128)S(1)} %collective-permute-done.7.right.maps, f32[16,640]{1,0:T(8,128)S(1)} %collective-permute-done.10.got, ...), custom_call_target="tpu_custom_call" | custom-call | flops 33554432 | bytes 3052032 | tf_op jit(solution)/shard_map/pallas_call | solution.py:557
  (21 shorter events, 0.1 us)
Async XLA Ops:
  2.6 4.6 %collective-permute-start = (f32[16,512]{1,0:T(8,128)S(1)}, f32[16,512]{1,0:T(8,128)S(1)}, u32[]{:S(2)}, u32[]{:S(2)}) collective-permute-start(f32[16,512]{1,0:T(8,128)S(1)} %get-tuple-element.41), channel_id=1, source_target_pairs={{0,2},{1,3},{2,0},{3,1},{4,6},{5,7},{6,4},{7,5},{8,10},{9,11},{10,... | collective-permute-start | bytes 98312 | tf_op jit(solution)/shard_map/ppermute | solution.py:579
  3.1 4.5 %collective-permute-start.1 = (f32[16,512]{1,0:T(8,128)S(1)}, f32[16,512]{1,0:T(8,128)S(1)}, u32[]{:S(2)}, u32[]{:S(2)}) collective-permute-start(f32[16,512]{1,0:T(8,128)S(1)} %get-tuple-element.42), channel_id=1, source_target_pairs={{0,1},{1,0},{2,4},{3,5},{4,2},{5,3},{6,8},{7,9},{8,6},{9,7},{10,12... | collective-permute-start | bytes 98312 | tf_op jit(solution)/shard_map/ppermute | solution.py:579
  7.5 14.9 %copy-start = (f32[768,768]{1,0:T(8,128)S(1)}, f32[768,768]{1,0:T(8,128)}, u32[]{:S(2)}) copy-start(f32[768,768]{1,0:T(8,128)} %coarse.1) | copy-start | bytes 7077892
  8.2 1.3 %collective-permute-start.2 = (f32[16,1152]{1,0:T(8,128)S(1)}, f32[16,1152]{1,0:T(8,128)S(1)}, u32[]{:S(2)}, u32[]{:S(2)}) collective-permute-start(f32[16,1152]{1,0:T(8,128)S(1)} %get-tuple-element.50), channel_id=1, source_target_pairs={{0,2},{1,3},{2,0},{3,1},{4,6},{5,7},{6,4},{7,5},{8,10},{9,11},{10,... | collective-permute-start | bytes 221192 | tf_op jit(solution)/shard_map/ppermute | solution.py:579
  9.5 3.7 %collective-permute-start.3 = (f32[16,128]{1,0:T(8,128)S(1)}, f32[16,128]{1,0:T(8,128)S(1)}, u32[]{:S(2)}, u32[]{:S(2)}) collective-permute-start(f32[16,128]{1,0:T(8,128)S(1)} %slice_add_fusion.1), channel_id=1, source_target_pairs={{0,10},{1,11},{2,8},{3,9},{4,14},{5,15},{6,12},{7,13},{8,2},{9,3},... | collective-permute-start | bytes 24584 | tf_op jit(solution)/shard_map/ppermute | solution.py:579
  11.8 4.3 %collective-permute-start.5 = (f32[16,1024]{1,0:T(8,128)S(1)}, f32[16,1024]{1,0:T(8,128)S(1)}, u32[]{:S(2)}, u32[]{:S(2)}) collective-permute-start(f32[16,1024]{1,0:T(8,128)S(1)} %get-tuple-element.52), channel_id=1, source_target_pairs={{0,1},{1,0},{2,4},{3,5},{4,2},{5,3},{6,8},{7,9},{8,6},{9,7},{10,12... | collective-permute-start | bytes 196616 | tf_op jit(solution)/shard_map/ppermute | solution.py:579
  13.3 4.1 %collective-permute-start.4 = (f32[24,128]{1,0:T(8,128)S(1)}, f32[24,128]{1,0:T(8,128)S(1)}, u32[]{:S(2)}, u32[]{:S(2)}) collective-permute-start(f32[24,128]{1,0:T(8,128)S(1)} %pad_maximum_fusion.3), channel_id=1, source_target_pairs={{0,18},{1,19},{2,16},{3,17},{4,22},{5,23},{6,20},{7,21},{8,26},{9,... | collective-permute-start | bytes 36872 | tf_op jit(solution)/shard_map/ppermute | solution.py:579
  17.4 3.3 %collective-permute-start.6 = (f32[40,128]{1,0:T(8,128)S(1)}, f32[40,128]{1,0:T(8,128)S(1)}, u32[]{:S(2)}, u32[]{:S(2)}) collective-permute-start(f32[40,128]{1,0:T(8,128)S(1)} %pad_maximum_fusion.1), channel_id=1, source_target_pairs={{0,3},{1,2},{2,1},{3,0},{4,7},{5,6},{6,5},{7,4},{8,11},{9,10},{10,... | collective-permute-start | bytes 61448 | tf_op jit(solution)/shard_map/ppermute | solution.py:579
  18.9 6.3 %collective-permute-start.8 = (f32[72,512]{1,0:T(8,128)S(1)}, f32[72,512]{1,0:T(8,128)S(1)}, u32[]{:S(2)}, u32[]{:S(2)}) collective-permute-start(f32[72,512]{1,0:T(8,128)S(1)} %get-tuple-element.57), channel_id=1, source_target_pairs={{0,2},{1,3},{2,0},{3,1},{4,6},{5,7},{6,4},{7,5},{8,10},{9,11},{10,... | collective-permute-start | bytes 442376 | tf_op jit(solution)/shard_map/ppermute | solution.py:579
  19.0 6.3 %collective-permute-start.9 = (f32[72,512]{1,0:T(8,128)S(1)}, f32[72,512]{1,0:T(8,128)S(1)}, u32[]{:S(2)}, u32[]{:S(2)}) collective-permute-start(f32[72,512]{1,0:T(8,128)S(1)} %get-tuple-element.58), channel_id=1, source_target_pairs={{0,1},{1,0},{2,4},{3,5},{4,2},{5,3},{6,8},{7,9},{8,6},{9,7},{10,12... | collective-permute-start | bytes 442376 | tf_op jit(solution)/shard_map/ppermute | solution.py:579
  20.7 4.6 %collective-permute-start.7 = (f32[72,128]{1,0:T(8,128)S(1)}, f32[72,128]{1,0:T(8,128)S(1)}, u32[]{:S(2)}, u32[]{:S(2)}) collective-permute-start(f32[72,128]{1,0:T(8,128)S(1)} %pad_maximum_fusion.tiles.maps), channel_id=1, source_target_pairs={{0,6},{1,7},{2,4},{3,5},{4,2},{5,3},{6,0},{7,1},{8,14},{9,15},{10,... | collective-permute-start | bytes 110600 | tf_op jit(solution)/shard_map/ppermute | solution.py:579
  28.4 1.3 %collective-permute-start.10 = (f32[16,640]{1,0:T(8,128)S(1)}, f32[16,640]{1,0:T(8,128)S(1)}, u32[]{:S(2)}, u32[]{:S(2)}) collective-permute-start(f32[16,640]{1,0:T(8,128)S(1)} %get-tuple-element.68), channel_id=1, source_target_pairs={{0,2},{1,3},{2,0},{3,1},{4,6},{5,7},{6,4},{7,5},{8,10},{9,11},{10,... | collective-permute-start | bytes 122888 | tf_op jit(solution)/shard_map/ppermute | solution.py:579
  29.7 3.6 %collective-permute-start.11 = (f32[16,128]{1,0:T(8,128)S(1)}, f32[16,128]{1,0:T(8,128)S(1)}, u32[]{:S(2)}, u32[]{:S(2)}) collective-permute-start(f32[16,128]{1,0:T(8,128)S(1)} %slice_add_fusion), channel_id=1, source_target_pairs={{0,10},{1,11},{2,8},{3,9},{4,14},{5,15},{6,12},{7,13},{8,2},{9,3},... | collective-permute-start | bytes 24584 | tf_op jit(solution)/shard_map/ppermute | solution.py:579
  33.3 4.1 %collective-permute-start.12 = (f32[24,128]{1,0:T(8,128)S(1)}, f32[24,128]{1,0:T(8,128)S(1)}, u32[]{:S(2)}, u32[]{:S(2)}) collective-permute-start(f32[24,128]{1,0:T(8,128)S(1)} %pad_maximum_fusion.4), channel_id=1, source_target_pairs={{0,18},{1,19},{2,16},{3,17},{4,22},{5,23},{6,20},{7,21},{8,26},{9,... | collective-permute-start | bytes 36872 | tf_op jit(solution)/shard_map/ppermute | solution.py:579
  37.5 3.3 %collective-permute-start.13 = (f32[40,128]{1,0:T(8,128)S(1)}, f32[40,128]{1,0:T(8,128)S(1)}, u32[]{:S(2)}, u32[]{:S(2)}) collective-permute-start(f32[40,128]{1,0:T(8,128)S(1)} %pad_maximum_fusion.2), channel_id=1, source_target_pairs={{0,3},{1,2},{2,1},{3,0},{4,7},{5,6},{6,5},{7,4},{8,11},{9,10},{10,... | collective-permute-start | bytes 61448 | tf_op jit(solution)/shard_map/ppermute | solution.py:579
  37.9 3.9 %collective-permute-start.14 = (f32[16,512]{1,0:T(8,128)S(1)}, f32[16,512]{1,0:T(8,128)S(1)}, u32[]{:S(2)}, u32[]{:S(2)}) collective-permute-start(f32[16,512]{1,0:T(8,128)S(1)} %get-tuple-element.69), channel_id=1, source_target_pairs={{0,1},{1,0},{2,4},{3,5},{4,2},{5,3},{6,8},{7,9},{8,6},{9,7},{10,12... | collective-permute-start | bytes 98312 | tf_op jit(solution)/shard_map/ppermute | solution.py:579
  41.8 4.0 %collective-permute-start.15 = (f32[72,128]{1,0:T(8,128)S(1)}, f32[72,128]{1,0:T(8,128)S(1)}, u32[]{:S(2)}, u32[]{:S(2)}) collective-permute-start(f32[72,128]{1,0:T(8,128)S(1)} %slice_dynamic-update-slice_fusion.tiles), channel_id=1, source_target_pairs={{0,6},{1,7},{2,4},{3,5},{4,2},{5,3},{6,0},{7,1},{8,14},{9,15},{10,... | collective-permute-start | bytes 110600 | tf_op jit(solution)/shard_map/ppermute | solution.py:579

commit v5 on v4

--- a/solution.py
+++ b/solution.py
@@ -10,7 +10,6 @@
 AXES = ("blk", "grp")
 NN = (((1,), (0,)), ((), ()))
 NT = (((1,), (1,)), ((), ()))
-TN = (((0,), (0,)), ((), ()))
 F32 = jnp.float32
 BF16 = jnp.bfloat16
 
@@ -129,14 +128,6 @@
     return product[:, :count] + product[:, count:]
 
 
-def combine(weights, values):
-    weight_high, weight_low = halves(weights)
-    high, low = halves(values)
-    left = jnp.concatenate([weight_high, weight_high, weight_low, weight_low], axis=0)
-    right = jnp.concatenate([high, low, high, low], axis=0)
-    return mm(left, right, TN)
-
-
 def against(values, exact):
     return folded(mm(stacked(values), exact, NN))
 
@@ -179,7 +170,7 @@
     scale = lax.rsqrt(jnp.sum(diagonal, axis=2, keepdims=True))
     matrix = matrix * lax.rsqrt(jnp.sum(diagonal, axis=1, keepdims=True))
     work = jnp.concatenate([matrix, target], axis=2) * scale
-    size = 4
+    size = 8
     for start in range(0, count, size):
         at = [start + index for index in range(size)]
         columns = [jnp.broadcast_to(work[:, :, k : k + 1], work.shape) for k in at]
@@ -201,7 +192,9 @@
                         pivot[i][j] = pivot[i][j] - left * pivot[one][j] - right * pivot[two][j]
                     rows[i] = rows[i] - left * rows[one] - right * rows[two]
         products = [column * row for column, row in zip(columns, rows)]
-        work = work - ((products[0] + products[1]) + (products[2] + products[3]))
+        while len(products) > 1:
+            products = [one + two for one, two in zip(products[::2], products[1::2])]
+        work = work - products[0]
         for k, row in zip(at, rows):
             work = jnp.where(row_index == k, row, work)
     return work[:, :, count:] * scale
@@ -300,6 +293,12 @@
     return jnp.concatenate([jnp.where(low, rows, 0.0), jnp.where(low, 0.0, rows)], axis=1)
 
 
+def both_orders(first, second):
+    count = first.shape[0]
+    products = dots(jnp.concatenate([first, second], axis=0), jnp.concatenate([second, first], axis=0))
+    return 0.5 * (products[:count, :count] + products[count:, count:])
+
+
 def picked(solved, row):
     return folded(mm(stacked(solved), chosen(row.astype(jnp.int32), solved.shape[1]), NN))
 
@@ -316,14 +315,11 @@
 
 
 def start_kernel(
-    count, rhs, signs, blocks, coupling, corner_map,
-    product, to_inner, to_outer, residual_out, sign_out, couple_out, map_out, inner_extra, outer_extra, held,
-    rhs_held, signs_held, coupling_held, map_held, sems,
+    count, rhs, signs, blocks, product, to_inner, to_outer, residual_out, sign_out, held, rhs_held, signs_held, sems,
 ):
     rows = held.shape[1]
     pieces = [(rhs, rhs_held), (signs, signs_held)]
     pieces += [(blocks.at[0, pl.ds(part * rows, rows)], held.at[part]) for part in range(held.shape[0])]
-    pieces += [(corner_map, map_held), (coupling, coupling_held)]
     copies = [pltpu.make_async_copy(*piece, sems.at[index]) for index, piece in enumerate(pieces)]
     for copy in copies:
         copy.start()
@@ -340,15 +336,30 @@
     sign_out[...] = sign
     residual_out[...] = residual
     total = jnp.zeros((nrhs, width), F32)
-    for part, copy in enumerate(copies[2:-2]):
+    for part, copy in enumerate(copies[2:]):
         copy.wait()
         total = total + mm(rounded[:, part * rows : (part + 1) * rows], held[part], NN)
     product[...] = total
     inner, outer = split(even, total[:, :half], total[:, half:])
     to_inner[...] = inner
     to_outer[...] = outer
-    copies[-2].wait()
-    copies[-1].wait()
+
+
+def load_kernel(
+    blocks, coupling, corner_map, after, out, couple_out, map_out, inner_extra, outer_extra, coupling_held, map_held, sems
+):
+    del after
+    parts = sems.shape[0] - 2
+    rows = out.shape[0] // parts
+    pieces = [(corner_map, map_held), (coupling, coupling_held)]
+    pieces += [(blocks.at[0, pl.ds(part * rows, rows)], out.at[pl.ds(part * rows, rows)]) for part in range(parts)]
+    copies = [pltpu.make_async_copy(*piece, sems.at[index]) for index, piece in enumerate(pieces)]
+    for copy in copies:
+        copy.start()
+    copies[0].wait()
+    copies[1].wait()
+    even = lax.axis_index("blk") % 2 == 0
+    nrhs, half = inner_extra.shape
     couple = coupling_held[0]
     couple_out[...] = couple
     slots = couple.shape[0] // 2
@@ -363,6 +374,8 @@
     )
     inner_extra[...] = inner
     outer_extra[...] = outer
+    for copy in copies[2:]:
+        copy.wait()
 
 
 def first_kernel(
@@ -379,10 +392,11 @@
     precond_out[...] = precond
     image_out[...] = image
     grams = dots(
-        jnp.concatenate([residual[...], precond], axis=0), jnp.concatenate([precond, image], axis=0)
+        jnp.concatenate([residual[...], precond, image], axis=0), jnp.concatenate([precond, image], axis=0)
     )
     slots = couple.shape[0]
-    first, second = grams[:nrhs, :nrhs], grams[nrhs:, nrhs:]
+    first = grams[:nrhs, :nrhs]
+    second = 0.5 * (grams[nrhs : 2 * nrhs, nrhs:] + grams[2 * nrhs :, :nrhs])
     tile = tiles_of(
         even, corner_values(precond, couple[...]), map_row[:, :slots], first, second, jnp.zeros_like(first)
     )
@@ -393,21 +407,6 @@
     to_inner[:, half:width] = inner_extra[...]
     to_outer[:, half:] = outer_extra[...]
     to_inner[:, width:] = tile
-
-
-def load_kernel(blocks, after, out, sems):
-    del after
-    rows = out.shape[0] // sems.shape[0]
-    copies = [
-        pltpu.make_async_copy(
-            blocks.at[0, pl.ds(part * rows, rows)], out.at[pl.ds(part * rows, rows)], sems.at[part]
-        )
-        for part in range(sems.shape[0])
-    ]
-    for copy in copies:
-        copy.start()
-    for copy in copies:
-        copy.wait()
 
 
 def prepare_kernel(coarse, high, low):
@@ -473,10 +472,10 @@
     corner_sum, squares = total_of(left, right, maps, slots, corners)
     gram, energy, _ = untile(squares)
     solved = coarse_solve(corner_sum, (coarse_high[...], coarse_low[...]))
-    energy = energy + dots(corner_sum, solved)
+    energy = energy + both_orders(corner_sum, solved)
     unit = (lax.broadcasted_iota(jnp.int32, (nrhs, nrhs), 0) == lanes_of((nrhs, nrhs))).astype(F32)
-    both = eliminate(jnp.stack([symmetric(2.0 * energy), symmetric(gram)]), jnp.stack([gram, unit]))
-    alpha, inverse = both[0], both[1]
+    both = eliminate(jnp.stack([2.0 * energy, symmetric(gram)]), jnp.stack([gram, unit]))
+    alpha, inverse = transposed(both[0]), both[1]
 
     rows = spread.shape[0]
     wide = map_row.shape[1]
@@ -491,7 +490,7 @@
         for turn, side in enumerate(sides, 1)
     ]
     change = live * (own - jnp.concatenate(others, axis=1))
-    change = combine(alpha, jnp.concatenate([whole, change], axis=1))
+    change = product_of(alpha, jnp.concatenate([whole, change], axis=1))
     residual = residual_in[...] - change[:, :width]
     precond = precond_in[...] - change[:, width:]
 
@@ -519,31 +518,35 @@
     small_out[...] = jnp.concatenate([inverse, energy, alpha, jnp.zeros((nrhs, 128 - 3 * nrhs), F32)], axis=1)
 
 
+def assemble_kernel(count, image, got, from_outer, small, old_precond, part_out, first_out):
+    blk = lax.axis_index("blk")
+    nrhs, width = image.shape
+    image_beside = joined(blk % 2 == 0, got[:, : width // 2], from_outer[...])
+    part_out[...] = live_mask(blk, count, width) * (image[...] - image_beside)
+    first_out[...] = product_of(small[:, 2 * nrhs : 3 * nrhs], old_precond[...])
+
+
 def final_kernel(
-    count, corners, left, right, maps, got, from_outer, precond, image, residual, old_precond, old_image,
+    corners, left, right, maps, part, first, precond, residual, old_precond, old_image,
     old_solved, small, columns, map_row, sign, coarse_high, coarse_low,
     multipliers_out, residual_out,
 ):
-    blk = lax.axis_index("blk")
-    even = blk % 2 == 0
     nrhs, width = precond.shape
-    live = live_mask(blk, count, width)
     slots = columns.shape[0] // 2
     corner_sum, squares = total_of(left, right, maps, slots, corners)
     gram, new_new, old_new = untile(squares)
-    beta = combine(small[:, :nrhs], gram)
+    inverse, old_old = small[:, :nrhs], small[:, nrhs : 2 * nrhs]
+    beta = product_of(inverse, gram)
+    turned = product_of(transposed(gram), inverse)
     solved = coarse_solve(corner_sum, (coarse_high[...], coarse_low[...]))
-    old_old = symmetric(small[:, nrhs : 2 * nrhs])
-    old_new = old_new + 2.0 * dots(old_solved[...], corner_sum)
-    energy = new_new + combine(beta, old_new + combine(old_old, beta)) + dots(corner_sum, solved)
-    alpha = eliminate(symmetric(2.0 * energy)[None], gram[None])[0]
-    image_beside = joined(even, got[:, : width // 2], from_outer[...])
+    old_new = old_new + product_of(old_old, beta) + 2.0 * dots(old_solved[...], corner_sum)
+    energy = symmetric(new_new + product_of(turned, old_new)) + both_orders(corner_sum, solved)
+    alpha = transposed(eliminate(2.0 * energy[None], gram[None])[0])
     at = picked(solved, map_row[...])
-    whole = live * (image[...] - image_beside) + against(at[:, : columns.shape[0]], columns[...])
-    first = combine(small[:, 2 * nrhs : 3 * nrhs], old_precond[...])
-    carried = combine(beta, jnp.concatenate([old_precond[...], old_image[...]], axis=1))
-    change = combine(alpha, jnp.concatenate([precond[...], whole], axis=1) + carried)
-    multipliers_out[0] = sign[...] * (first + change[:, :width])
+    whole = part[...] + against(at[:, : columns.shape[0]], columns[...])
+    carried = product_of(turned, jnp.concatenate([old_precond[...], old_image[...]], axis=1))
+    change = product_of(alpha, jnp.concatenate([precond[...], whole], axis=1) + carried)
+    multipliers_out[0] = sign[...] * (first[...] + change[:, :width])
     residual_out[0] = sign[...] * (residual[...] - change[:, width:])
 
 
@@ -592,7 +595,7 @@
         squares = [part[:8] for part in parts]
         return jnp.concatenate([sum(squares[1:], squares[0])] + [part[8:] for part in parts], axis=0)
 
-    def region(tile, to_inner, to_outer, maps=None, follow=None):
+    def region(tile, to_inner, to_outer, follow, maps=None):
         from_outer = permute(to_outer, outer)
         got = permute(to_inner, inner)
         values = tile + got[:, got.shape[1] - TILE :]
@@ -605,13 +608,10 @@
                     known = known or (left, right)
                     left, right = densify(left, known[0]), densify(right, known[1])
                 values = united([left, right])
-            if follow is None and index == len(steps) - 1:
-                values, from_outer = lax.optimization_barrier((values, from_outer))
-                result = (got, from_outer)
-            if follow is not None and index == max(len(steps) - 2, 0):
-                *kept, to_inner, to_outer = follow(got, from_outer)
-                values, to_inner, to_outer = lax.optimization_barrier((values, to_inner, to_outer))
-                result = (*exchange(to_inner, to_outer), *kept)
+            if index == max(len(steps) - 2, 0):
+                result, sends = follow(got, from_outer)
+                values, result, sends = lax.optimization_barrier((values, result, sends))
+                result = (*(exchange(*sends) if sends else ()), *result)
             left = values
             right = united([permute(values, pairs) for pairs in turns])
         known = known or (left, right)
@@ -622,30 +622,30 @@
     wide = ((nrhs, width), F32)
     face = ((nrhs, half), F32)
     pieces = 4
-    product, to_inner, to_outer, residual0, sign, couple, map_row, *extras, held = call(
+    in_hbm = functools.partial(pltpu.with_memory_space_constraint, memory_space=pltpu.HBM)
+    coupling_shape, map_shape = corner_coupling.shape, corner_map.shape
+    product, to_inner, to_outer, residual0, sign, held = call(
         functools.partial(start_kernel, count),
-        [
-            wide, face, face, wide, ((1, width), F32), (corner_coupling.shape[1:], BF16),
-            ((1, 128), F32), face, face,
-            ((pieces, width // pieces, width), BF16),
-        ],
-        *[pltpu.with_memory_space_constraint(arg, pltpu.HBM) for arg in (dual_rhs, signs, prec_ops, corner_coupling, corner_map)],
-        specs=[HBM] * 5,
+        [wide, face, face, wide, ((1, width), F32), ((pieces, width // pieces, width), BF16)],
+        in_hbm(dual_rhs), in_hbm(signs), in_hbm(prec_ops),
+        specs=[HBM] * 3,
         scratch=[
             pltpu.VMEM(dual_rhs.shape, F32),
             pltpu.VMEM(signs.shape, jnp.int32),
-            pltpu.VMEM(corner_coupling.shape, BF16),
-            pltpu.VMEM(corner_map.shape, jnp.int32),
-            pltpu.SemaphoreType.DMA((pieces + 4,)),
+            pltpu.SemaphoreType.DMA((pieces + 2,)),
         ],
         flops=flops,
     )
-    (loaded,) = call(
+    loaded, couple, map_row, *extras = call(
         load_kernel,
-        [((width, width), BF16)],
-        pltpu.with_memory_space_constraint(dual_ops, pltpu.HBM), sign,
-        specs=[HBM, VMEM],
-        scratch=[pltpu.SemaphoreType.DMA((pieces,))],
+        [((width, width), BF16), (coupling_shape[1:], BF16), ((1, 128), F32), face, face],
+        in_hbm(dual_ops), in_hbm(corner_coupling), in_hbm(corner_map), sign,
+        specs=[HBM] * 3 + [VMEM],
+        scratch=[
+            pltpu.VMEM(coupling_shape, BF16),
+            pltpu.VMEM(map_shape, jnp.int32),
+            pltpu.SemaphoreType.DMA((pieces + 2,)),
+        ],
     )
     tile_shape = ((nrhs, TILE), F32)
     precond0, image0, tile, to_inner, to_outer = call(
@@ -659,7 +659,7 @@
     rows = nrhs + 2 * slots + 8
 
     def follow(got, from_outer):
-        return call(
+        *kept, to_inner, to_outer = call(
             functools.partial(follow_kernel, count),
             [
                 wide, wide, ((2 * slots, width), F32), ((2 * slots, width), BF16), ((1, 128), F32),
@@ -668,8 +668,13 @@
             image0, got, from_outer, couple, map_row, held,
             flops=5 * flops,
         )
-
-    maps, gathered = region(tile, to_inner, to_outer, follow=follow)
+        return tuple(kept), (to_inner, to_outer)
+
+    def assemble(got, from_outer):
+        body = functools.partial(assemble_kernel, count)
+        return tuple(call(body, [wide, wide], image1, got, from_outer, small, precond0, flops=5 * flops)), ()
+
+    maps, gathered = region(tile, to_inner, to_outer, follow)
     columns, index = gathered[-2:]
     solved0, residual1, whole0, precond1, image1, small, tile, to_inner, to_outer = call(
         functools.partial(middle_kernel, count, corners),
@@ -677,13 +682,13 @@
         *gathered, precond0, image0, residual0, loaded, couple, *coarse_parts,
         flops=flops,
     )
-    _, gathered = region(tile, to_inner, to_outer, maps=maps)
+    _, gathered = region(tile, to_inner, to_outer, assemble, maps)
     whole_out = ((1, nrhs, width), F32)
     return tuple(
         call(
-            functools.partial(final_kernel, count, corners),
+            functools.partial(final_kernel, corners),
             [whole_out, whole_out],
-            *gathered, precond1, image1, residual1, precond0, whole0, solved0, small,
+            *gathered, precond1, residual1, precond0, whole0, solved0, small,
             columns, index, sign, *coarse_parts,
             flops=flops,
         )

time: 49.1 us -> 47.3 us (0.963)
  starting transfers between devices: 23 us -> 21.7 us
  waiting for transfers between devices: 13 us -> 12.5 us
    ppermute x16, starting transfers between devices: 23 us -> 21.7 us  [permute(): return lax.ppermute(values, AXES, pairs)]
    ppermute x16, waiting for transfers between devices: 13 us -> 12.5 us  [permute(): return lax.ppermute(values, AXES, pairs)]
    pallas_call x9 -> x10, Pallas kernels: 12.2 us -> 12.2 us  [call(): pl.pallas_call(body, out_shape=shapes, in_specs=specs or [VMEM] * len(arg...]
  transfers between devices with their start and end apart: 16 -> 16, of which waited for: 12 -> 11; matrix products, arithmetic and copies ran while one was open for 0% -> 0% of each run, Pallas kernels for 7% -> 8%
where the time goes in v5:
time: 47.3 us; the launch traced here: 47.1 us
  starting transfers between devices  21.7 us (46%)
  waiting for transfers between devices  12.5 us (26%)
  Pallas kernels  12.2 us (26%)
  between operations  0.7 us (1%)
    ppermute x16, starting transfers between devices, permute(): return lax.ppermute(values, AXES, pairs)  21.7 us
    ppermute x16, waiting for transfers between devices, permute(): return lax.ppermute(values, AXES, pairs)  12.5 us
    pallas_call x10, Pallas kernels, call(): pl.pallas_call(body, out_shape=shapes, in_specs=specs or [VMEM] * len(arg...  12.2 us
  transfers between devices with their start and end apart: 16, of which 11 were waited for; matrix products, arithmetic and copies ran while one was open for 0% of the time, Pallas kernels for 8%

profile of v5, /device:TPU:0, one launch (start us, length us, event | category | flops | bytes accessed | tf_op | source)
XLA Modules:
  0.0 47.1 jit_solution(16576958300073764672)
XLA Ops:
  0.6 1.8 %shard_map.86 = (f32[16,1024]{1,0:T(8,128)S(1)}, f32[16,512]{1,0:T(8,128)S(1)}, f32[16,512]{1,0:T(8,128)S(1)}, f32[16,1024]{1,0:T(8,128)S(1)}, f32[1,1024]{1,0:T(1,128)S(1)}, /*index=5*/bf16[4,256,1024]{2,1,0:T(8,128)(2,1)S(1)}) custom-call(f32[1,16,1024]{2,1,0:T(8,128)} %rhs.1, s32[1,1024]{1,0:T(1,128)} %signs.1, bf16[1,1024,1024]{2,1,0:T(8,128)(2,1)} %blocks.2), custom_call_target="tpu_custom_call" | custom-call | flops 33554432 | bytes 2166784 | tf_op jit(solution)/shard_map/pallas_call | solution.py:560
  2.5 0.5 %collective-permute-start = (f32[16,512]{1,0:T(8,128)S(1)}, f32[16,512]{1,0:T(8,128)S(1)}, u32[]{:S(2)}, u32[]{:S(2)}) collective-permute-start(f32[16,512]{1,0:T(8,128)S(1)} %get-tuple-element.50), channel_id=1, source_target_pairs={{0,2},{1,3},{2,0},{3,1},{4,6},{5,7},{6,4},{7,5},{8,10},{9,11},{10,... | collective-permute-start | bytes 98312 | tf_op jit(solution)/shard_map/ppermute | solution.py:582
  3.0 2.6 %collective-permute-start.1 = (f32[16,512]{1,0:T(8,128)S(1)}, f32[16,512]{1,0:T(8,128)S(1)}, u32[]{:S(2)}, u32[]{:S(2)}) collective-permute-start(f32[16,512]{1,0:T(8,128)S(1)} %get-tuple-element.51), channel_id=1, source_target_pairs={{0,1},{1,0},{2,4},{3,5},{4,2},{5,3},{6,8},{7,9},{8,6},{9,7},{10,12... | collective-permute-start | bytes 98312 | tf_op jit(solution)/shard_map/ppermute | solution.py:582
  5.5 1.6 %shard_map.87 = (bf16[1024,1024]{1,0:T(8,128)(2,1)S(1)}, bf16[24,512]{1,0:T(8,128)(2,1)S(1)}, f32[1,128]{1,0:T(1,128)S(1)}, f32[16,512]{1,0:T(8,128)S(1)}, f32[16,512]{1,0:T(8,128)S(1)}) custom-call(bf16[1,1024,1024]{2,1,0:T(8,128)(2,1)} %blocks.3, bf16[1,24,512]{2,1,0:T(8,128)(2,1)} %coupling.1, s32[1,24]{1,0:T(1,128)} %corner_map.1, ...), custom_call_target="tpu_custom_call" | custom-call | bytes 2125920 | tf_op jit(solution)/shard_map/pallas_call | solution.py:560
  7.1 0.0 collective-permute-done.from_inner
  7.2 0.3 collective-permute-done.1.from_outer
  7.4 0.0 copy-start
  7.4 0.8 %shard_map.88 = (f32[16,1024]{1,0:T(8,128)S(1)}, f32[16,1024]{1,0:T(8,128)S(1)}, f32[16,128]{1,0:T(8,128)S(1)}, f32[16,1152]{1,0:T(8,128)S(1)}, f32[16,1024]{1,0:T(8,128)S(1)}) custom-call(f32[16,1024]{1,0:T(8,128)S(1)} %get-tuple-element.49.product, f32[16,512]{1,0:T(8,128)S(1)} %collective-permute-done.from_inner, ...), custom_call_target="tpu_custom_call" | custom-call | flops 33554432 | bytes 2384384 | tf_op jit(solution)/shard_map/pallas_call | solution.py:560
  8.2 0.1 collective-permute-start.2
  8.3 1.2 %collective-permute-done.2.got = f32[16,1152]{1,0:T(8,128)S(1)} collective-permute-done((f32[16,1152]{1,0:T(8,128)S(1)}, f32[16,1152]{1,0:T(8,128)S(1)}, u32[]{:S(2)}, u32[]{:S(2)}) %collective-permute-start.2) | collective-permute-done | bytes 73760 | tf_op jit(solution)/shard_map/ppermute | solution.py:582
  9.5 2.3 %collective-permute-start.3 = (f32[16,128]{1,0:T(8,128)S(1)}, f32[16,128]{1,0:T(8,128)S(1)}, u32[]{:S(2)}, u32[]{:S(2)}) collective-permute-start(f32[16,128]{1,0:T(8,128)S(1)} %slice_add_fusion.1), channel_id=1, source_target_pairs={{0,10},{1,11},{2,8},{3,9},{4,14},{5,15},{6,12},{7,13},{8,2},{9,3},... | collective-permute-start | bytes 24584 | tf_op jit(solution)/shard_map/ppermute | solution.py:582
  11.8 1.5 %collective-permute-start.5 = (f32[16,1024]{1,0:T(8,128)S(1)}, f32[16,1024]{1,0:T(8,128)S(1)}, u32[]{:S(2)}, u32[]{:S(2)}) collective-permute-start(f32[16,1024]{1,0:T(8,128)S(1)} %get-tuple-element.62), channel_id=1, source_target_pairs={{0,1},{1,0},{2,4},{3,5},{4,2},{5,3},{6,8},{7,9},{8,6},{9,7},{10,12... | collective-permute-start | bytes 196616 | tf_op jit(solution)/shard_map/ppermute | solution.py:582
  13.2 0.0 collective-permute-done.3
  13.3 2.6 %collective-permute-start.4 = (f32[24,128]{1,0:T(8,128)S(1)}, f32[24,128]{1,0:T(8,128)S(1)}, u32[]{:S(2)}, u32[]{:S(2)}) collective-permute-start(f32[24,128]{1,0:T(8,128)S(1)} %pad_maximum_fusion.4), channel_id=1, source_target_pairs={{0,18},{1,19},{2,16},{3,17},{4,22},{5,23},{6,20},{7,21},{8,26},{9,... | collective-permute-start | bytes 36872 | tf_op jit(solution)/shard_map/ppermute | solution.py:582
  15.9 0.2 collective-permute-done.5.from_outer
  16.0 0.5 %shard_map.89 = (f32[16,1024]{1,0:T(8,128)S(1)}, f32[16,1024]{1,0:T(8,128)S(1)}, f32[48,1024]{1,0:T(8,128)S(1)}, bf16[48,1024]{1,0:T(8,128)(2,1)S(1)}, f32[1,128...) custom-call(f32[16,1024]{1,0:T(8,128)S(1)} %get-tuple-element.61.image.image_in, ...), custom_call_target="tpu_custom_call" | custom-call | flops 167772160 | bytes 2327040 | tf_op jit(solution)/shard_map/pallas_call | solution.py:560
  16.5 0.8 %collective-permute-done.4 = f32[24,128]{1,0:T(8,128)S(1)} collective-permute-done((f32[24,128]{1,0:T(8,128)S(1)}, f32[24,128]{1,0:T(8,128)S(1)}, u32[]{:S(2)}, u32[]{:S(2)}) %collective-permute-start.4) | collective-permute-done | bytes 12320 | tf_op jit(solution)/shard_map/ppermute | solution.py:582
  17.4 1.5 %collective-permute-start.6 = (f32[40,128]{1,0:T(8,128)S(1)}, f32[40,128]{1,0:T(8,128)S(1)}, u32[]{:S(2)}, u32[]{:S(2)}) collective-permute-start(f32[40,128]{1,0:T(8,128)S(1)} %pad_maximum_fusion.2), channel_id=1, source_target_pairs={{0,3},{1,2},{2,1},{3,0},{4,7},{5,6},{6,5},{7,4},{8,11},{9,10},{10,... | collective-permute-start | bytes 61448 | tf_op jit(solution)/shard_map/ppermute | solution.py:582
  18.9 0.1 collective-permute-start.8
  18.9 0.6 %collective-permute-start.9 = (f32[72,512]{1,0:T(8,128)S(1)}, f32[72,512]{1,0:T(8,128)S(1)}, u32[]{:S(2)}, u32[]{:S(2)}) collective-permute-start(f32[72,512]{1,0:T(8,128)S(1)} %get-tuple-element.73), channel_id=1, source_target_pairs={{0,1},{1,0},{2,4},{3,5},{4,2},{5,3},{6,8},{7,9},{8,6},{9,7},{10,12... | collective-permute-start | bytes 442376 | tf_op jit(solution)/shard_map/ppermute | solution.py:582
  19.6 1.1 %collective-permute-done.6 = f32[40,128]{1,0:T(8,128)S(1)} collective-permute-done((f32[40,128]{1,0:T(8,128)S(1)}, f32[40,128]{1,0:T(8,128)S(1)}, u32[]{:S(2)}, u32[]{:S(2)}) %collective-permute-start.6) | collective-permute-done | bytes 20512 | tf_op jit(solution)/shard_map/ppermute | solution.py:582
  20.6 1.7 %collective-permute-start.7 = (f32[72,128]{1,0:T(8,128)S(1)}, f32[72,128]{1,0:T(8,128)S(1)}, u32[]{:S(2)}, u32[]{:S(2)}) collective-permute-start(f32[72,128]{1,0:T(8,128)S(1)} %pad_maximum_fusion.tiles.maps), channel_id=1, source_target_pairs={{0,6},{1,7},{2,4},{3,5},{4,2},{5,3},{6,0},{7,1},{8,14},{9,15},{10,... | collective-permute-start | bytes 110600 | tf_op jit(solution)/shard_map/ppermute | solution.py:582
  22.4 0.0 copy-done
  22.4 0.3 shard_map.91
  22.7 0.5 shard_map.90.left
  23.2 2.0 %collective-permute-done.7.right.maps = f32[72,128]{1,0:T(8,128)S(1)} collective-permute-done((f32[72,128]{1,0:T(8,128)S(1)}, f32[72,128]{1,0:T(8,128)S(1)}, u32[]{:S(2)}, u32[]{:S(2)}) %collective-permute-start.7) | collective-permute-done | bytes 36896 | tf_op jit(solution)/shard_map/ppermute | solution.py:582
  25.2 0.0 collective-permute-done.8.from_inner
  25.2 0.0 collective-permute-done.9.from_outer
  25.2 3.0 %shard_map.92 = (f32[16,768]{1,0:T(8,128)S(1)}, f32[16,1024]{1,0:T(8,128)S(1)}, f32[16,1024]{1,0:T(8,128)S(1)}, f32[16,1024]{1,0:T(8,128)S(1)}, f32[16,1024]{1,0...) custom-call(f32[16,896]{1,0:T(8,128)S(1)} %shard_map.90.left, ...), custom_call_target="tpu_custom_call" | custom-call | flops 33554432 | bytes 5530112 | tf_op jit(solution)/shard_map/pallas_call | solution.py:560
  28.3 0.4 collective-permute-start.10
  28.6 0.9 %collective-permute-done.10.got = f32[16,640]{1,0:T(8,128)S(1)} collective-permute-done((f32[16,640]{1,0:T(8,128)S(1)}, f32[16,640]{1,0:T(8,128)S(1)}, u32[]{:S(2)}, u32[]{:S(2)}) %collective-permute-start.10) | collective-permute-done | bytes 40992 | tf_op jit(solution)/shard_map/ppermute | solution.py:582
  29.5 2.3 %collective-permute-start.11 = (f32[16,128]{1,0:T(8,128)S(1)}, f32[16,128]{1,0:T(8,128)S(1)}, u32[]{:S(2)}, u32[]{:S(2)}) collective-permute-start(f32[16,128]{1,0:T(8,128)S(1)} %slice_add_fusion), channel_id=1, source_target_pairs={{0,10},{1,11},{2,8},{3,9},{4,14},{5,15},{6,12},{7,13},{8,2},{9,3},... | collective-permute-start | bytes 24584 | tf_op jit(solution)/shard_map/ppermute | solution.py:582
  31.8 0.5 %collective-permute-start.13 = (f32[16,512]{1,0:T(8,128)S(1)}, f32[16,512]{1,0:T(8,128)S(1)}, u32[]{:S(2)}, u32[]{:S(2)}) collective-permute-start(f32[16,512]{1,0:T(8,128)S(1)} %get-tuple-element.85), channel_id=1, source_target_pairs={{0,1},{1,0},{2,4},{3,5},{4,2},{5,3},{6,8},{7,9},{8,6},{9,7},{10,12... | collective-permute-start | bytes 98312 | tf_op jit(solution)/shard_map/ppermute | solution.py:582
  32.3 0.8 %collective-permute-done.11 = f32[16,128]{1,0:T(8,128)S(1)} collective-permute-done((f32[16,128]{1,0:T(8,128)S(1)}, f32[16,128]{1,0:T(8,128)S(1)}, u32[]{:S(2)}, u32[]{:S(2)}) %collective-permute-start.11) | collective-permute-done | bytes 8224 | tf_op jit(solution)/shard_map/ppermute | solution.py:582
  33.2 2.7 %collective-permute-start.12 = (f32[24,128]{1,0:T(8,128)S(1)}, f32[24,128]{1,0:T(8,128)S(1)}, u32[]{:S(2)}, u32[]{:S(2)}) collective-permute-start(f32[24,128]{1,0:T(8,128)S(1)} %pad_maximum_fusion.5), channel_id=1, source_target_pairs={{0,18},{1,19},{2,16},{3,17},{4,22},{5,23},{6,20},{7,21},{8,26},{9,... | collective-permute-start | bytes 36872 | tf_op jit(solution)/shard_map/ppermute | solution.py:582
  35.9 0.0 collective-permute-done.13.from_outer
  35.9 0.2 shard_map.93
  36.1 1.2 %collective-permute-done.12 = f32[24,128]{1,0:T(8,128)S(1)} collective-permute-done((f32[24,128]{1,0:T(8,128)S(1)}, f32[24,128]{1,0:T(8,128)S(1)}, u32[]{:S(2)}, u32[]{:S(2)}) %collective-permute-start.12) | collective-permute-done | bytes 12320 | tf_op jit(solution)/shard_map/ppermute | solution.py:582
  37.3 0.4 collective-permute-start.14
  37.7 2.9 %collective-permute-done.14 = f32[40,128]{1,0:T(8,128)S(1)} collective-permute-done((f32[40,128]{1,0:T(8,128)S(1)}, f32[40,128]{1,0:T(8,128)S(1)}, u32[]{:S(2)}, u32[]{:S(2)}) %collective-permute-start.14) | collective-permute-done | bytes 20512 | tf_op jit(solution)/shard_map/ppermute | solution.py:582
  40.6 1.9 %collective-permute-start.15 = (f32[72,128]{1,0:T(8,128)S(1)}, f32[72,128]{1,0:T(8,128)S(1)}, u32[]{:S(2)}, u32[]{:S(2)}) collective-permute-start(f32[72,128]{1,0:T(8,128)S(1)} %pad_maximum_fusion.1.tiles), channel_id=1, source_target_pairs={{0,6},{1,7},{2,4},{3,5},{4,2},{5,3},{6,0},{7,1},{8,14},{9,15},{10,... | collective-permute-start | bytes 110600 | tf_op jit(solution)/shard_map/ppermute | solution.py:582
  42.5 0.5 shard_map.94.left
  42.9 1.2 %collective-permute-done.15.right = f32[72,128]{1,0:T(8,128)S(1)} collective-permute-done((f32[72,128]{1,0:T(8,128)S(1)}, f32[72,128]{1,0:T(8,128)S(1)}, u32[]{:S(2)}, u32[]{:S(2)}) %collective-permute-start.15) | collective-permute-done | bytes 36896 | tf_op jit(solution)/shard_map/ppermute | solution.py:582
  44.1 3.0 %shard_map.95 = (f32[1,16,1024]{2,1,0:T(8,128)}, f32[1,16,1024]{2,1,0:T(8,128)}) custom-call(f32[16,896]{1,0:T(8,128)S(1)} %shard_map.94.left, f32[72,128]{1,0:T(8,128)S(1)} %collective-permute-done.15.right, f32[72,128]{1,0:T(8,128)S(1)} %collective-permute-done.7.right.maps, f32[16,1024]{1,0:T(8,128)S(1)} %get-tuple-element.90.part, ...), custom_call_target="tpu_custom_call" | custom-call | flops 33554432 | bytes 3043840 | tf_op jit(solution)/shard_map/pallas_call | solution.py:560
  (20 shorter events, 0.1 us)
Async XLA Ops:
  2.5 4.7 %collective-permute-start = (f32[16,512]{1,0:T(8,128)S(1)}, f32[16,512]{1,0:T(8,128)S(1)}, u32[]{:S(2)}, u32[]{:S(2)}) collective-permute-start(f32[16,512]{1,0:T(8,128)S(1)} %get-tuple-element.50), channel_id=1, source_target_pairs={{0,2},{1,3},{2,0},{3,1},{4,6},{5,7},{6,4},{7,5},{8,10},{9,11},{10,... | collective-permute-start | bytes 98312 | tf_op jit(solution)/shard_map/ppermute | solution.py:582
  3.0 4.5 %collective-permute-start.1 = (f32[16,512]{1,0:T(8,128)S(1)}, f32[16,512]{1,0:T(8,128)S(1)}, u32[]{:S(2)}, u32[]{:S(2)}) collective-permute-start(f32[16,512]{1,0:T(8,128)S(1)} %get-tuple-element.51), channel_id=1, source_target_pairs={{0,1},{1,0},{2,4},{3,5},{4,2},{5,3},{6,8},{7,9},{8,6},{9,7},{10,12... | collective-permute-start | bytes 98312 | tf_op jit(solution)/shard_map/ppermute | solution.py:582
  7.4 15.0 %copy-start = (f32[768,768]{1,0:T(8,128)S(1)}, f32[768,768]{1,0:T(8,128)}, u32[]{:S(2)}) copy-start(f32[768,768]{1,0:T(8,128)} %coarse.1) | copy-start | bytes 7077892
  8.2 1.3 %collective-permute-start.2 = (f32[16,1152]{1,0:T(8,128)S(1)}, f32[16,1152]{1,0:T(8,128)S(1)}, u32[]{:S(2)}, u32[]{:S(2)}) collective-permute-start(f32[16,1152]{1,0:T(8,128)S(1)} %get-tuple-element.60), channel_id=1, source_target_pairs={{0,2},{1,3},{2,0},{3,1},{4,6},{5,7},{6,4},{7,5},{8,10},{9,11},{10,... | collective-permute-start | bytes 221192 | tf_op jit(solution)/shard_map/ppermute | solution.py:582
  9.5 3.7 %collective-permute-start.3 = (f32[16,128]{1,0:T(8,128)S(1)}, f32[16,128]{1,0:T(8,128)S(1)}, u32[]{:S(2)}, u32[]{:S(2)}) collective-permute-start(f32[16,128]{1,0:T(8,128)S(1)} %slice_add_fusion.1), channel_id=1, source_target_pairs={{0,10},{1,11},{2,8},{3,9},{4,14},{5,15},{6,12},{7,13},{8,2},{9,3},... | collective-permute-start | bytes 24584 | tf_op jit(solution)/shard_map/ppermute | solution.py:582
  11.8 4.3 %collective-permute-start.5 = (f32[16,1024]{1,0:T(8,128)S(1)}, f32[16,1024]{1,0:T(8,128)S(1)}, u32[]{:S(2)}, u32[]{:S(2)}) collective-permute-start(f32[16,1024]{1,0:T(8,128)S(1)} %get-tuple-element.62), channel_id=1, source_target_pairs={{0,1},{1,0},{2,4},{3,5},{4,2},{5,3},{6,8},{7,9},{8,6},{9,7},{10,12... | collective-permute-start | bytes 196616 | tf_op jit(solution)/shard_map/ppermute | solution.py:582
  13.3 4.1 %collective-permute-start.4 = (f32[24,128]{1,0:T(8,128)S(1)}, f32[24,128]{1,0:T(8,128)S(1)}, u32[]{:S(2)}, u32[]{:S(2)}) collective-permute-start(f32[24,128]{1,0:T(8,128)S(1)} %pad_maximum_fusion.4), channel_id=1, source_target_pairs={{0,18},{1,19},{2,16},{3,17},{4,22},{5,23},{6,20},{7,21},{8,26},{9,... | collective-permute-start | bytes 36872 | tf_op jit(solution)/shard_map/ppermute | solution.py:582
  17.4 3.3 %collective-permute-start.6 = (f32[40,128]{1,0:T(8,128)S(1)}, f32[40,128]{1,0:T(8,128)S(1)}, u32[]{:S(2)}, u32[]{:S(2)}) collective-permute-start(f32[40,128]{1,0:T(8,128)S(1)} %pad_maximum_fusion.2), channel_id=1, source_target_pairs={{0,3},{1,2},{2,1},{3,0},{4,7},{5,6},{6,5},{7,4},{8,11},{9,10},{10,... | collective-permute-start | bytes 61448 | tf_op jit(solution)/shard_map/ppermute | solution.py:582
  18.9 6.3 %collective-permute-start.8 = (f32[72,512]{1,0:T(8,128)S(1)}, f32[72,512]{1,0:T(8,128)S(1)}, u32[]{:S(2)}, u32[]{:S(2)}) collective-permute-start(f32[72,512]{1,0:T(8,128)S(1)} %get-tuple-element.72), channel_id=1, source_target_pairs={{0,2},{1,3},{2,0},{3,1},{4,6},{5,7},{6,4},{7,5},{8,10},{9,11},{10,... | collective-permute-start | bytes 442376 | tf_op jit(solution)/shard_map/ppermute | solution.py:582
  18.9 6.3 %collective-permute-start.9 = (f32[72,512]{1,0:T(8,128)S(1)}, f32[72,512]{1,0:T(8,128)S(1)}, u32[]{:S(2)}, u32[]{:S(2)}) collective-permute-start(f32[72,512]{1,0:T(8,128)S(1)} %get-tuple-element.73), channel_id=1, source_target_pairs={{0,1},{1,0},{2,4},{3,5},{4,2},{5,3},{6,8},{7,9},{8,6},{9,7},{10,12... | collective-permute-start | bytes 442376 | tf_op jit(solution)/shard_map/ppermute | solution.py:582
  20.6 4.6 %collective-permute-start.7 = (f32[72,128]{1,0:T(8,128)S(1)}, f32[72,128]{1,0:T(8,128)S(1)}, u32[]{:S(2)}, u32[]{:S(2)}) collective-permute-start(f32[72,128]{1,0:T(8,128)S(1)} %pad_maximum_fusion.tiles.maps), channel_id=1, source_target_pairs={{0,6},{1,7},{2,4},{3,5},{4,2},{5,3},{6,0},{7,1},{8,14},{9,15},{10,... | collective-permute-start | bytes 110600 | tf_op jit(solution)/shard_map/ppermute | solution.py:582
  28.3 1.3 %collective-permute-start.10 = (f32[16,640]{1,0:T(8,128)S(1)}, f32[16,640]{1,0:T(8,128)S(1)}, u32[]{:S(2)}, u32[]{:S(2)}) collective-permute-start(f32[16,640]{1,0:T(8,128)S(1)} %get-tuple-element.83), channel_id=1, source_target_pairs={{0,2},{1,3},{2,0},{3,1},{4,6},{5,7},{6,4},{7,5},{8,10},{9,11},{10,... | collective-permute-start | bytes 122888 | tf_op jit(solution)/shard_map/ppermute | solution.py:582
  29.5 3.6 %collective-permute-start.11 = (f32[16,128]{1,0:T(8,128)S(1)}, f32[16,128]{1,0:T(8,128)S(1)}, u32[]{:S(2)}, u32[]{:S(2)}) collective-permute-start(f32[16,128]{1,0:T(8,128)S(1)} %slice_add_fusion), channel_id=1, source_target_pairs={{0,10},{1,11},{2,8},{3,9},{4,14},{5,15},{6,12},{7,13},{8,2},{9,3},... | collective-permute-start | bytes 24584 | tf_op jit(solution)/shard_map/ppermute | solution.py:582
  31.8 4.1 %collective-permute-start.13 = (f32[16,512]{1,0:T(8,128)S(1)}, f32[16,512]{1,0:T(8,128)S(1)}, u32[]{:S(2)}, u32[]{:S(2)}) collective-permute-start(f32[16,512]{1,0:T(8,128)S(1)} %get-tuple-element.85), channel_id=1, source_target_pairs={{0,1},{1,0},{2,4},{3,5},{4,2},{5,3},{6,8},{7,9},{8,6},{9,7},{10,12... | collective-permute-start | bytes 98312 | tf_op jit(solution)/shard_map/ppermute | solution.py:582
  33.2 4.1 %collective-permute-start.12 = (f32[24,128]{1,0:T(8,128)S(1)}, f32[24,128]{1,0:T(8,128)S(1)}, u32[]{:S(2)}, u32[]{:S(2)}) collective-permute-start(f32[24,128]{1,0:T(8,128)S(1)} %pad_maximum_fusion.5), channel_id=1, source_target_pairs={{0,18},{1,19},{2,16},{3,17},{4,22},{5,23},{6,20},{7,21},{8,26},{9,... | collective-permute-start | bytes 36872 | tf_op jit(solution)/shard_map/ppermute | solution.py:582
  37.3 3.3 %collective-permute-start.14 = (f32[40,128]{1,0:T(8,128)S(1)}, f32[40,128]{1,0:T(8,128)S(1)}, u32[]{:S(2)}, u32[]{:S(2)}) collective-permute-start(f32[40,128]{1,0:T(8,128)S(1)} %pad_maximum_fusion.3), channel_id=1, source_target_pairs={{0,3},{1,2},{2,1},{3,0},{4,7},{5,6},{6,5},{7,4},{8,11},{9,10},{10,... | collective-permute-start | bytes 61448 | tf_op jit(solution)/shard_map/ppermute | solution.py:582
  40.6 3.5 %collective-permute-start.15 = (f32[72,128]{1,0:T(8,128)S(1)}, f32[72,128]{1,0:T(8,128)S(1)}, u32[]{:S(2)}, u32[]{:S(2)}) collective-permute-start(f32[72,128]{1,0:T(8,128)S(1)} %pad_maximum_fusion.1.tiles), channel_id=1, source_target_pairs={{0,6},{1,7},{2,4},{3,5},{4,2},{5,3},{6,0},{7,1},{8,14},{9,15},{10,... | collective-permute-start | bytes 110600 | tf_op jit(solution)/shard_map/ppermute | solution.py:582

commit v6 on v5

--- a/solution.py
+++ b/solution.py
@@ -95,11 +95,9 @@
 
         return target
 
-    for stride, factor in blk_steps[1:]:
-        add_axis(blk_target(stride, factor), factor)
     for stride, factor in grp_steps:
         add_axis(grp_target(stride, factor), factor)
-    for stride, factor in blk_steps[:1]:
+    for stride, factor in blk_steps:
         add_axis(blk_target(stride, factor), factor)
     return steps
 
@@ -162,14 +160,14 @@
     return matrix.T
 
 
-def eliminate(matrix, target):
+def eliminate(matrix, target, guide):
     count = matrix.shape[1]
     row_index = lax.broadcasted_iota(jnp.int32, (1, count, 1), 1)
     column_index = lax.broadcasted_iota(jnp.int32, (1, count, count), 2)
-    diagonal = jnp.where(row_index == column_index, matrix, 0.0)
+    diagonal = jnp.where(row_index == column_index, guide, 0.0)
     scale = lax.rsqrt(jnp.sum(diagonal, axis=2, keepdims=True))
-    matrix = matrix * lax.rsqrt(jnp.sum(diagonal, axis=1, keepdims=True))
-    work = jnp.concatenate([matrix, target], axis=2) * scale
+    both = scale * lax.rsqrt(jnp.sum(diagonal, axis=1, keepdims=True))
+    work = jnp.concatenate([matrix * both, target * scale], axis=2)
     size = 8
     for start in range(0, count, size):
         at = [start + index for index in range(size)]
@@ -470,11 +468,14 @@
     live = live_mask(blk, count, width)
     slots = couple.shape[0]
     corner_sum, squares = total_of(left, right, maps, slots, corners)
-    gram, energy, _ = untile(squares)
+    gram, local_energy, _ = untile(squares)
     solved = coarse_solve(corner_sum, (coarse_high[...], coarse_low[...]))
-    energy = energy + both_orders(corner_sum, solved)
+    energy = local_energy + both_orders(corner_sum, solved)
     unit = (lax.broadcasted_iota(jnp.int32, (nrhs, nrhs), 0) == lanes_of((nrhs, nrhs))).astype(F32)
-    both = eliminate(jnp.stack([2.0 * energy, symmetric(gram)]), jnp.stack([gram, unit]))
+    old = symmetric(gram)
+    both = eliminate(
+        jnp.stack([2.0 * energy, old]), jnp.stack([gram, unit]), jnp.stack([2.0 * local_energy, old])
+    )
     alpha, inverse = transposed(both[0]), both[1]
 
     rows = spread.shape[0]
@@ -541,7 +542,7 @@
     solved = coarse_solve(corner_sum, (coarse_high[...], coarse_low[...]))
     old_new = old_new + product_of(old_old, beta) + 2.0 * dots(old_solved[...], corner_sum)
     energy = symmetric(new_new + product_of(turned, old_new)) + both_orders(corner_sum, solved)
-    alpha = transposed(eliminate(2.0 * energy[None], gram[None])[0])
+    alpha = transposed(eliminate(2.0 * energy[None], gram[None], 2.0 * new_new[None])[0])
     at = picked(solved, map_row[...])
     whole = part[...] + against(at[:, : columns.shape[0]], columns[...])
     carried = product_of(turned, jnp.concatenate([old_precond[...], old_image[...]], axis=1))
@@ -621,7 +622,7 @@
 
     wide = ((nrhs, width), F32)
     face = ((nrhs, half), F32)
-    pieces = 4
+    pieces = 8
     in_hbm = functools.partial(pltpu.with_memory_space_constraint, memory_space=pltpu.HBM)
     coupling_shape, map_shape = corner_coupling.shape, corner_map.shape
     product, to_inner, to_outer, residual0, sign, held = call(

time: 47.3 us -> 46.1 us (0.975)
  waiting for transfers between devices: 12.5 us -> 11.6 us
    ppermute x16, waiting for transfers between devices: 12.5 us -> 11.6 us  [permute(): return lax.ppermute(values, AXES, pairs)]
  transfers between devices with their start and end apart: 16 -> 16, of which waited for: 11 -> 13; matrix products, arithmetic and copies ran while one was open for 0% -> 0% of each run, Pallas kernels for 8% -> 8%
where the time goes in v6:
time: 46.1 us; the launch traced here: 45.9 us
  starting transfers between devices  21.6 us (47%)
  Pallas kernels  11.9 us (26%)
  waiting for transfers between devices  11.6 us (25%)
  between operations  0.7 us (2%)
    ppermute x16, starting transfers between devices, permute(): return lax.ppermute(values, AXES, pairs)  21.6 us
    pallas_call x10, Pallas kernels, call(): pl.pallas_call(body, out_shape=shapes, in_specs=specs or [VMEM] * len(arg...  11.9 us
    ppermute x16, waiting for transfers between devices, permute(): return lax.ppermute(values, AXES, pairs)  11.6 us
  transfers between devices with their start and end apart: 16, of which 13 were waited for; matrix products, arithmetic and copies ran while one was open for 0% of the time, Pallas kernels for 8%

profile of v6, /device:TPU:0, one launch (start us, length us, event | category | flops | bytes accessed | tf_op | source)
XLA Modules:
  0.0 45.9 jit_solution(3582617676523013124)
XLA Ops:
  0.6 1.8 %shard_map.86 = (f32[16,1024]{1,0:T(8,128)S(1)}, f32[16,512]{1,0:T(8,128)S(1)}, f32[16,512]{1,0:T(8,128)S(1)}, f32[16,1024]{1,0:T(8,128)S(1)}, f32[1,1024]{1,0:T(1,128)S(1)}, /*index=5*/bf16[8,128,1024]{2,1,0:T(8,128)(2,1)S(1)}) custom-call(f32[1,16,1024]{2,1,0:T(8,128)} %rhs.1, s32[1,1024]{1,0:T(1,128)} %signs.1, bf16[1,1024,1024]{2,1,0:T(8,128)(2,1)} %blocks.2), custom_call_target="tpu_custom_call" | custom-call | flops 33554432 | bytes 2166784 | tf_op jit(solution)/shard_map/pallas_call | solution.py:561
  2.4 0.5 %collective-permute-start = (f32[16,512]{1,0:T(8,128)S(1)}, f32[16,512]{1,0:T(8,128)S(1)}, u32[]{:S(2)}, u32[]{:S(2)}) collective-permute-start(f32[16,512]{1,0:T(8,128)S(1)} %get-tuple-element.50), channel_id=1, source_target_pairs={{0,2},{1,3},{2,0},{3,1},{4,6},{5,7},{6,4},{7,5},{8,10},{9,11},{10,... | collective-permute-start | bytes 98312 | tf_op jit(solution)/shard_map/ppermute | solution.py:583
  3.0 2.6 %collective-permute-start.1 = (f32[16,512]{1,0:T(8,128)S(1)}, f32[16,512]{1,0:T(8,128)S(1)}, u32[]{:S(2)}, u32[]{:S(2)}) collective-permute-start(f32[16,512]{1,0:T(8,128)S(1)} %get-tuple-element.51), channel_id=1, source_target_pairs={{0,1},{1,0},{2,4},{3,5},{4,2},{5,3},{6,8},{7,9},{8,6},{9,7},{10,12... | collective-permute-start | bytes 98312 | tf_op jit(solution)/shard_map/ppermute | solution.py:583
  5.5 1.6 %shard_map.87 = (bf16[1024,1024]{1,0:T(8,128)(2,1)S(1)}, bf16[24,512]{1,0:T(8,128)(2,1)S(1)}, f32[1,128]{1,0:T(1,128)S(1)}, f32[16,512]{1,0:T(8,128)S(1)}, f32[16,512]{1,0:T(8,128)S(1)}) custom-call(bf16[1,1024,1024]{2,1,0:T(8,128)(2,1)} %blocks.3, bf16[1,24,512]{2,1,0:T(8,128)(2,1)} %coupling.1, s32[1,24]{1,0:T(1,128)} %corner_map.1, ...), custom_call_target="tpu_custom_call" | custom-call | bytes 2125920 | tf_op jit(solution)/shard_map/pallas_call | solution.py:561
  7.1 0.0 collective-permute-done.from_inner
  7.2 0.3 collective-permute-done.1.from_outer
  7.4 0.0 copy-start
  7.4 0.8 %shard_map.88 = (f32[16,1024]{1,0:T(8,128)S(1)}, f32[16,1024]{1,0:T(8,128)S(1)}, f32[16,128]{1,0:T(8,128)S(1)}, f32[16,1152]{1,0:T(8,128)S(1)}, f32[16,1024]{1,0:T(8,128)S(1)}) custom-call(f32[16,1024]{1,0:T(8,128)S(1)} %get-tuple-element.49.product, f32[16,512]{1,0:T(8,128)S(1)} %collective-permute-done.from_inner, ...), custom_call_target="tpu_custom_call" | custom-call | flops 33554432 | bytes 2384384 | tf_op jit(solution)/shard_map/pallas_call | solution.py:561
  8.2 0.1 collective-permute-start.2
  8.3 1.2 %collective-permute-done.2.got = f32[16,1152]{1,0:T(8,128)S(1)} collective-permute-done((f32[16,1152]{1,0:T(8,128)S(1)}, f32[16,1152]{1,0:T(8,128)S(1)}, u32[]{:S(2)}, u32[]{:S(2)}) %collective-permute-start.2) | collective-permute-done | bytes 73760 | tf_op jit(solution)/shard_map/ppermute | solution.py:583
  9.5 1.8 %collective-permute-start.3 = (f32[16,128]{1,0:T(8,128)S(1)}, f32[16,128]{1,0:T(8,128)S(1)}, u32[]{:S(2)}, u32[]{:S(2)}) collective-permute-start(f32[16,128]{1,0:T(8,128)S(1)} %slice_add_fusion.1), channel_id=1, source_target_pairs={{0,3},{1,2},{2,1},{3,0},{4,7},{5,6},{6,5},{7,4},{8,11},{9,10},{10,... | collective-permute-start | bytes 24584 | tf_op jit(solution)/shard_map/ppermute | solution.py:583
  11.3 0.3 collective-permute-start.5
  11.5 1.1 %collective-permute-done.3 = f32[16,128]{1,0:T(8,128)S(1)} collective-permute-done((f32[16,128]{1,0:T(8,128)S(1)}, f32[16,128]{1,0:T(8,128)S(1)}, u32[]{:S(2)}, u32[]{:S(2)}) %collective-permute-start.3) | collective-permute-done | bytes 8224 | tf_op jit(solution)/shard_map/ppermute | solution.py:583
  12.6 2.3 %collective-permute-start.4 = (f32[24,128]{1,0:T(8,128)S(1)}, f32[24,128]{1,0:T(8,128)S(1)}, u32[]{:S(2)}, u32[]{:S(2)}) collective-permute-start(f32[24,128]{1,0:T(8,128)S(1)} %pad_maximum_fusion.4), channel_id=1, source_target_pairs={{0,6},{1,7},{2,4},{3,5},{4,2},{5,3},{6,0},{7,1},{8,14},{9,15},{10,... | collective-permute-start | bytes 36872 | tf_op jit(solution)/shard_map/ppermute | solution.py:583
  15.0 0.6 %collective-permute-done.5.from_outer = f32[16,1024]{1,0:T(8,128)S(1)} collective-permute-done((f32[16,1024]{1,0:T(8,128)S(1)}, f32[16,1024]{1,0:T(8,128)S(1)}, u32[]{:S(2)}, u32[]{:S(2)}) %collective-permute-start.5) | collective-permute-done | bytes 65568 | tf_op jit(solution)/shard_map/ppermute | solution.py:583
  15.5 0.5 %shard_map.89 = (f32[16,1024]{1,0:T(8,128)S(1)}, f32[16,1024]{1,0:T(8,128)S(1)}, f32[48,1024]{1,0:T(8,128)S(1)}, bf16[48,1024]{1,0:T(8,128)(2,1)S(1)}, f32[1,128...) custom-call(f32[16,1024]{1,0:T(8,128)S(1)} %get-tuple-element.61.image.image_in, ...), custom_call_target="tpu_custom_call" | custom-call | flops 167772160 | bytes 2327040 | tf_op jit(solution)/shard_map/pallas_call | solution.py:561
  16.0 0.4 collective-permute-done.4
  16.4 2.2 %collective-permute-start.6 = (f32[40,128]{1,0:T(8,128)S(1)}, f32[40,128]{1,0:T(8,128)S(1)}, u32[]{:S(2)}, u32[]{:S(2)}) collective-permute-start(f32[40,128]{1,0:T(8,128)S(1)} %pad_maximum_fusion.2), channel_id=1, source_target_pairs={{0,10},{1,11},{2,8},{3,9},{4,14},{5,15},{6,12},{7,13},{8,2},{9,3},... | collective-permute-start | bytes 61448 | tf_op jit(solution)/shard_map/ppermute | solution.py:583
  18.6 0.1 collective-permute-start.8
  18.7 1.3 %collective-permute-start.9 = (f32[72,512]{1,0:T(8,128)S(1)}, f32[72,512]{1,0:T(8,128)S(1)}, u32[]{:S(2)}, u32[]{:S(2)}) collective-permute-start(f32[72,512]{1,0:T(8,128)S(1)} %get-tuple-element.73), channel_id=1, source_target_pairs={{0,1},{1,0},{2,4},{3,5},{4,2},{5,3},{6,8},{7,9},{8,6},{9,7},{10,12... | collective-permute-start | bytes 442376 | tf_op jit(solution)/shard_map/ppermute | solution.py:583
  19.9 0.1 collective-permute-done.6
  20.1 2.8 %collective-permute-start.7 = (f32[72,128]{1,0:T(8,128)S(1)}, f32[72,128]{1,0:T(8,128)S(1)}, u32[]{:S(2)}, u32[]{:S(2)}) collective-permute-start(f32[72,128]{1,0:T(8,128)S(1)} %pad_maximum_fusion.tiles.maps), channel_id=1, source_target_pairs={{0,18},{1,19},{2,16},{3,17},{4,22},{5,23},{6,20},{7,21},{8,26},{9,... | collective-permute-start | bytes 110600 | tf_op jit(solution)/shard_map/ppermute | solution.py:583
  22.9 0.0 copy-done
  22.9 0.3 shard_map.91
  23.2 0.5 %shard_map.90.left = f32[16,896]{1,0:T(8,128)S(1)} custom-call(f32[72,128]{1,0:T(8,128)S(1)} %pad_maximum_fusion.tiles.maps, f32[72,128]{1,0:T(8,128)S(1)} %pad_maximum_fusion.tiles.maps), custom_call_target="tpu_custom_call" | custom-call | flops 33554432 | bytes 73728 | tf_op jit(solution)/shard_map/pallas_call | solution.py:561
  23.7 1.2 %collective-permute-done.7.right.maps = f32[72,128]{1,0:T(8,128)S(1)} collective-permute-done((f32[72,128]{1,0:T(8,128)S(1)}, f32[72,128]{1,0:T(8,128)S(1)}, u32[]{:S(2)}, u32[]{:S(2)}) %collective-permute-start.7) | collective-permute-done | bytes 36896 | tf_op jit(solution)/shard_map/ppermute | solution.py:583
  24.9 0.0 collective-permute-done.8.from_inner
  24.9 0.0 collective-permute-done.9.from_outer
  24.9 2.9 %shard_map.92 = (f32[16,768]{1,0:T(8,128)S(1)}, f32[16,1024]{1,0:T(8,128)S(1)}, f32[16,1024]{1,0:T(8,128)S(1)}, f32[16,1024]{1,0:T(8,128)S(1)}, f32[16,1024]{1,0...) custom-call(f32[16,896]{1,0:T(8,128)S(1)} %shard_map.90.left, ...), custom_call_target="tpu_custom_call" | custom-call | flops 33554432 | bytes 5530112 | tf_op jit(solution)/shard_map/pallas_call | solution.py:561
  27.8 0.5 %collective-permute-start.10 = (f32[16,640]{1,0:T(8,128)S(1)}, f32[16,640]{1,0:T(8,128)S(1)}, u32[]{:S(2)}, u32[]{:S(2)}) collective-permute-start(f32[16,640]{1,0:T(8,128)S(1)} %get-tuple-element.83), channel_id=1, source_target_pairs={{0,2},{1,3},{2,0},{3,1},{4,6},{5,7},{6,4},{7,5},{8,10},{9,11},{10,... | collective-permute-start | bytes 122888 | tf_op jit(solution)/shard_map/ppermute | solution.py:583
  28.3 0.9 %collective-permute-done.10.got = f32[16,640]{1,0:T(8,128)S(1)} collective-permute-done((f32[16,640]{1,0:T(8,128)S(1)}, f32[16,640]{1,0:T(8,128)S(1)}, u32[]{:S(2)}, u32[]{:S(2)}) %collective-permute-start.10) | collective-permute-done | bytes 40992 | tf_op jit(solution)/shard_map/ppermute | solution.py:583
  29.2 1.7 %collective-permute-start.11 = (f32[16,128]{1,0:T(8,128)S(1)}, f32[16,128]{1,0:T(8,128)S(1)}, u32[]{:S(2)}, u32[]{:S(2)}) collective-permute-start(f32[16,128]{1,0:T(8,128)S(1)} %slice_add_fusion), channel_id=1, source_target_pairs={{0,3},{1,2},{2,1},{3,0},{4,7},{5,6},{6,5},{7,4},{8,11},{9,10},{10,... | collective-permute-start | bytes 24584 | tf_op jit(solution)/shard_map/ppermute | solution.py:583
  30.9 0.3 collective-permute-start.13
  31.2 1.1 %collective-permute-done.11 = f32[16,128]{1,0:T(8,128)S(1)} collective-permute-done((f32[16,128]{1,0:T(8,128)S(1)}, f32[16,128]{1,0:T(8,128)S(1)}, u32[]{:S(2)}, u32[]{:S(2)}) %collective-permute-start.11) | collective-permute-done | bytes 8224 | tf_op jit(solution)/shard_map/ppermute | solution.py:583
  32.3 1.3 %collective-permute-start.12 = (f32[24,128]{1,0:T(8,128)S(1)}, f32[24,128]{1,0:T(8,128)S(1)}, u32[]{:S(2)}, u32[]{:S(2)}) collective-permute-start(f32[24,128]{1,0:T(8,128)S(1)} %pad_maximum_fusion.5), channel_id=1, source_target_pairs={{0,6},{1,7},{2,4},{3,5},{4,2},{5,3},{6,0},{7,1},{8,14},{9,15},{10,... | collective-permute-start | bytes 36872 | tf_op jit(solution)/shard_map/ppermute | solution.py:583
  33.5 1.3 %collective-permute-done.13.from_outer = f32[16,512]{1,0:T(8,128)S(1)} collective-permute-done((f32[16,512]{1,0:T(8,128)S(1)}, f32[16,512]{1,0:T(8,128)S(1)}, u32[]{:S(2)}, u32[]{:S(2)}) %collective-permute-start.13) | collective-permute-done | bytes 32800 | tf_op jit(solution)/shard_map/ppermute | solution.py:583
  34.8 0.2 shard_map.93
  35.0 0.4 collective-permute-done.12
  35.4 1.4 %collective-permute-start.14 = (f32[40,128]{1,0:T(8,128)S(1)}, f32[40,128]{1,0:T(8,128)S(1)}, u32[]{:S(2)}, u32[]{:S(2)}) collective-permute-start(f32[40,128]{1,0:T(8,128)S(1)} %pad_maximum_fusion.3), channel_id=1, source_target_pairs={{0,10},{1,11},{2,8},{3,9},{4,14},{5,15},{6,12},{7,13},{8,2},{9,3},... | collective-permute-start | bytes 61448 | tf_op jit(solution)/shard_map/ppermute | solution.py:583
  36.8 1.9 %collective-permute-done.14 = f32[40,128]{1,0:T(8,128)S(1)} collective-permute-done((f32[40,128]{1,0:T(8,128)S(1)}, f32[40,128]{1,0:T(8,128)S(1)}, u32[]{:S(2)}, u32[]{:S(2)}) %collective-permute-start.14) | collective-permute-done | bytes 20512 | tf_op jit(solution)/shard_map/ppermute | solution.py:583
  38.7 2.6 %collective-permute-start.15 = (f32[72,128]{1,0:T(8,128)S(1)}, f32[72,128]{1,0:T(8,128)S(1)}, u32[]{:S(2)}, u32[]{:S(2)}) collective-permute-start(f32[72,128]{1,0:T(8,128)S(1)} %pad_maximum_fusion.1.tiles), channel_id=1, source_target_pairs={{0,18},{1,19},{2,16},{3,17},{4,22},{5,23},{6,20},{7,21},{8,26},{9,... | collective-permute-start | bytes 110600 | tf_op jit(solution)/shard_map/ppermute | solution.py:583
  41.2 0.5 shard_map.94.left
  41.7 1.3 %collective-permute-done.15.right = f32[72,128]{1,0:T(8,128)S(1)} collective-permute-done((f32[72,128]{1,0:T(8,128)S(1)}, f32[72,128]{1,0:T(8,128)S(1)}, u32[]{:S(2)}, u32[]{:S(2)}) %collective-permute-start.15) | collective-permute-done | bytes 36896 | tf_op jit(solution)/shard_map/ppermute | solution.py:583
  43.0 2.9 %shard_map.95 = (f32[1,16,1024]{2,1,0:T(8,128)}, f32[1,16,1024]{2,1,0:T(8,128)}) custom-call(f32[16,896]{1,0:T(8,128)S(1)} %shard_map.94.left, f32[72,128]{1,0:T(8,128)S(1)} %collective-permute-done.15.right, f32[72,128]{1,0:T(8,128)S(1)} %collective-permute-done.7.right.maps, f32[16,1024]{1,0:T(8,128)S(1)} %get-tuple-element.90.part, ...), custom_call_target="tpu_custom_call" | custom-call | flops 33554432 | bytes 3043840 | tf_op jit(solution)/shard_map/pallas_call | solution.py:561
  (20 shorter events, 0.1 us)
Async XLA Ops:
  2.4 4.7 %collective-permute-start = (f32[16,512]{1,0:T(8,128)S(1)}, f32[16,512]{1,0:T(8,128)S(1)}, u32[]{:S(2)}, u32[]{:S(2)}) collective-permute-start(f32[16,512]{1,0:T(8,128)S(1)} %get-tuple-element.50), channel_id=1, source_target_pairs={{0,2},{1,3},{2,0},{3,1},{4,6},{5,7},{6,4},{7,5},{8,10},{9,11},{10,... | collective-permute-start | bytes 98312 | tf_op jit(solution)/shard_map/ppermute | solution.py:583
  3.0 4.5 %collective-permute-start.1 = (f32[16,512]{1,0:T(8,128)S(1)}, f32[16,512]{1,0:T(8,128)S(1)}, u32[]{:S(2)}, u32[]{:S(2)}) collective-permute-start(f32[16,512]{1,0:T(8,128)S(1)} %get-tuple-element.51), channel_id=1, source_target_pairs={{0,1},{1,0},{2,4},{3,5},{4,2},{5,3},{6,8},{7,9},{8,6},{9,7},{10,12... | collective-permute-start | bytes 98312 | tf_op jit(solution)/shard_map/ppermute | solution.py:583
  7.4 15.5 %copy-start = (f32[768,768]{1,0:T(8,128)S(1)}, f32[768,768]{1,0:T(8,128)}, u32[]{:S(2)}) copy-start(f32[768,768]{1,0:T(8,128)} %coarse.1) | copy-start | bytes 7077892
  8.2 1.3 %collective-permute-start.2 = (f32[16,1152]{1,0:T(8,128)S(1)}, f32[16,1152]{1,0:T(8,128)S(1)}, u32[]{:S(2)}, u32[]{:S(2)}) collective-permute-start(f32[16,1152]{1,0:T(8,128)S(1)} %get-tuple-element.60), channel_id=1, source_target_pairs={{0,2},{1,3},{2,0},{3,1},{4,6},{5,7},{6,4},{7,5},{8,10},{9,11},{10,... | collective-permute-start | bytes 221192 | tf_op jit(solution)/shard_map/ppermute | solution.py:583
  9.5 3.1 %collective-permute-start.3 = (f32[16,128]{1,0:T(8,128)S(1)}, f32[16,128]{1,0:T(8,128)S(1)}, u32[]{:S(2)}, u32[]{:S(2)}) collective-permute-start(f32[16,128]{1,0:T(8,128)S(1)} %slice_add_fusion.1), channel_id=1, source_target_pairs={{0,3},{1,2},{2,1},{3,0},{4,7},{5,6},{6,5},{7,4},{8,11},{9,10},{10,... | collective-permute-start | bytes 24584 | tf_op jit(solution)/shard_map/ppermute | solution.py:583
  11.3 4.3 %collective-permute-start.5 = (f32[16,1024]{1,0:T(8,128)S(1)}, f32[16,1024]{1,0:T(8,128)S(1)}, u32[]{:S(2)}, u32[]{:S(2)}) collective-permute-start(f32[16,1024]{1,0:T(8,128)S(1)} %get-tuple-element.62), channel_id=1, source_target_pairs={{0,1},{1,0},{2,4},{3,5},{4,2},{5,3},{6,8},{7,9},{8,6},{9,7},{10,12... | collective-permute-start | bytes 196616 | tf_op jit(solution)/shard_map/ppermute | solution.py:583
  12.6 3.7 %collective-permute-start.4 = (f32[24,128]{1,0:T(8,128)S(1)}, f32[24,128]{1,0:T(8,128)S(1)}, u32[]{:S(2)}, u32[]{:S(2)}) collective-permute-start(f32[24,128]{1,0:T(8,128)S(1)} %pad_maximum_fusion.4), channel_id=1, source_target_pairs={{0,6},{1,7},{2,4},{3,5},{4,2},{5,3},{6,0},{7,1},{8,14},{9,15},{10,... | collective-permute-start | bytes 36872 | tf_op jit(solution)/shard_map/ppermute | solution.py:583
  16.4 3.6 %collective-permute-start.6 = (f32[40,128]{1,0:T(8,128)S(1)}, f32[40,128]{1,0:T(8,128)S(1)}, u32[]{:S(2)}, u32[]{:S(2)}) collective-permute-start(f32[40,128]{1,0:T(8,128)S(1)} %pad_maximum_fusion.2), channel_id=1, source_target_pairs={{0,10},{1,11},{2,8},{3,9},{4,14},{5,15},{6,12},{7,13},{8,2},{9,3},... | collective-permute-start | bytes 61448 | tf_op jit(solution)/shard_map/ppermute | solution.py:583
  18.6 6.4 %collective-permute-start.8 = (f32[72,512]{1,0:T(8,128)S(1)}, f32[72,512]{1,0:T(8,128)S(1)}, u32[]{:S(2)}, u32[]{:S(2)}) collective-permute-start(f32[72,512]{1,0:T(8,128)S(1)} %get-tuple-element.72), channel_id=1, source_target_pairs={{0,2},{1,3},{2,0},{3,1},{4,6},{5,7},{6,4},{7,5},{8,10},{9,11},{10,... | collective-permute-start | bytes 442376 | tf_op jit(solution)/shard_map/ppermute | solution.py:583
  18.7 6.3 %collective-permute-start.9 = (f32[72,512]{1,0:T(8,128)S(1)}, f32[72,512]{1,0:T(8,128)S(1)}, u32[]{:S(2)}, u32[]{:S(2)}) collective-permute-start(f32[72,512]{1,0:T(8,128)S(1)} %get-tuple-element.73), channel_id=1, source_target_pairs={{0,1},{1,0},{2,4},{3,5},{4,2},{5,3},{6,8},{7,9},{8,6},{9,7},{10,12... | collective-permute-start | bytes 442376 | tf_op jit(solution)/shard_map/ppermute | solution.py:583
  20.1 4.9 %collective-permute-start.7 = (f32[72,128]{1,0:T(8,128)S(1)}, f32[72,128]{1,0:T(8,128)S(1)}, u32[]{:S(2)}, u32[]{:S(2)}) collective-permute-start(f32[72,128]{1,0:T(8,128)S(1)} %pad_maximum_fusion.tiles.maps), channel_id=1, source_target_pairs={{0,18},{1,19},{2,16},{3,17},{4,22},{5,23},{6,20},{7,21},{8,26},{9,... | collective-permute-start | bytes 110600 | tf_op jit(solution)/shard_map/ppermute | solution.py:583
  27.8 1.3 %collective-permute-start.10 = (f32[16,640]{1,0:T(8,128)S(1)}, f32[16,640]{1,0:T(8,128)S(1)}, u32[]{:S(2)}, u32[]{:S(2)}) collective-permute-start(f32[16,640]{1,0:T(8,128)S(1)} %get-tuple-element.83), channel_id=1, source_target_pairs={{0,2},{1,3},{2,0},{3,1},{4,6},{5,7},{6,4},{7,5},{8,10},{9,11},{10,... | collective-permute-start | bytes 122888 | tf_op jit(solution)/shard_map/ppermute | solution.py:583
  29.2 3.1 %collective-permute-start.11 = (f32[16,128]{1,0:T(8,128)S(1)}, f32[16,128]{1,0:T(8,128)S(1)}, u32[]{:S(2)}, u32[]{:S(2)}) collective-permute-start(f32[16,128]{1,0:T(8,128)S(1)} %slice_add_fusion), channel_id=1, source_target_pairs={{0,3},{1,2},{2,1},{3,0},{4,7},{5,6},{6,5},{7,4},{8,11},{9,10},{10,... | collective-permute-start | bytes 24584 | tf_op jit(solution)/shard_map/ppermute | solution.py:583
  30.9 3.9 %collective-permute-start.13 = (f32[16,512]{1,0:T(8,128)S(1)}, f32[16,512]{1,0:T(8,128)S(1)}, u32[]{:S(2)}, u32[]{:S(2)}) collective-permute-start(f32[16,512]{1,0:T(8,128)S(1)} %get-tuple-element.85), channel_id=1, source_target_pairs={{0,1},{1,0},{2,4},{3,5},{4,2},{5,3},{6,8},{7,9},{8,6},{9,7},{10,12... | collective-permute-start | bytes 98312 | tf_op jit(solution)/shard_map/ppermute | solution.py:583
  32.3 3.1 %collective-permute-start.12 = (f32[24,128]{1,0:T(8,128)S(1)}, f32[24,128]{1,0:T(8,128)S(1)}, u32[]{:S(2)}, u32[]{:S(2)}) collective-permute-start(f32[24,128]{1,0:T(8,128)S(1)} %pad_maximum_fusion.5), channel_id=1, source_target_pairs={{0,6},{1,7},{2,4},{3,5},{4,2},{5,3},{6,0},{7,1},{8,14},{9,15},{10,... | collective-permute-start | bytes 36872 | tf_op jit(solution)/shard_map/ppermute | solution.py:583
  35.4 3.3 %collective-permute-start.14 = (f32[40,128]{1,0:T(8,128)S(1)}, f32[40,128]{1,0:T(8,128)S(1)}, u32[]{:S(2)}, u32[]{:S(2)}) collective-permute-start(f32[40,128]{1,0:T(8,128)S(1)} %pad_maximum_fusion.3), channel_id=1, source_target_pairs={{0,10},{1,11},{2,8},{3,9},{4,14},{5,15},{6,12},{7,13},{8,2},{9,3},... | collective-permute-start | bytes 61448 | tf_op jit(solution)/shard_map/ppermute | solution.py:583
  38.7 4.3 %collective-permute-start.15 = (f32[72,128]{1,0:T(8,128)S(1)}, f32[72,128]{1,0:T(8,128)S(1)}, u32[]{:S(2)}, u32[]{:S(2)}) collective-permute-start(f32[72,128]{1,0:T(8,128)S(1)} %pad_maximum_fusion.1.tiles), channel_id=1, source_target_pairs={{0,18},{1,19},{2,16},{3,17},{4,22},{5,23},{6,20},{7,21},{8,26},{9,... | collective-permute-start | bytes 110600 | tf_op jit(solution)/shard_map/ppermute | solution.py:583

commit v7 on v6

--- a/solution.py
+++ b/solution.py
@@ -50,56 +50,53 @@
 
 def rotations(count, groups):
     core = 2 if count % 2 == 0 else 1
+    chips = count // core
     steps = []
 
-    def flipped(blk, turn):
-        return (blk ^ 1) if (core == 2 and turn) else blk
-
-    def add_axis(step_target, factor):
-        steps.append(
-            [
-                [
-                    (blk * groups + grp, step_target(blk, grp, turn))
-                    for blk in range(count)
-                    for grp in range(groups)
-                ]
-                for turn in range(1, factor)
-            ]
-        )
-
-    stride = 1
-    blk_steps = []
-    for factor in radices(count // core):
-        blk_steps.append((stride, factor))
-        stride *= factor
-    grp_steps = []
-    stride = 1
-    for factor in radices(groups):
-        grp_steps.append((stride, factor))
-        stride *= factor
-
-    def blk_target(stride, factor):
-        def target(blk, grp, turn):
-            chip = blk // core
-            digit = (chip // stride) % factor
-            moved = chip + ((digit + turn) % factor - digit) * stride
-            return flipped(moved * core + blk % core, turn) * groups + grp
-
-        return target
-
-    def grp_target(stride, factor):
-        def target(blk, grp, turn):
-            digit = (grp // stride) % factor
-            moved = grp + ((digit + turn) % factor - digit) * stride
-            return flipped(blk, turn) * groups + moved
-
-        return target
-
-    for stride, factor in grp_steps:
-        add_axis(grp_target(stride, factor), factor)
-    for stride, factor in blk_steps:
-        add_axis(blk_target(stride, factor), factor)
-    return steps
+    def pairs_of(target):
+        return [
+            (blk * groups + grp, target(blk // core, blk % core, grp)) for blk in range(count) for grp in range(groups)
+        ]
+
+    def place(chip, lane, grp):
+        return (chip * core + lane) * groups + grp
+
+    def turned(value, stride, factor, turn):
+        digit = (value // stride) % factor
+        return value + ((digit + turn) % factor - digit) * stride
+
+    def along(axis, stride, factor):
+        def pairs(turn):
+            def target(chip, lane, grp):
+                lane = (lane + 1) % core
+                if axis == "blk":
+                    return place(turned(chip, stride, factor, turn), lane, grp)
+                return place(chip, lane, turned(grp, stride, factor, turn))
+
+            return pairs_of(target)
+
+        return [pairs(turn) for turn in range(1, factor)], False
+
+    def both():
+        def split_target(chip, lane, grp):
+            return place(chip, 1, grp ^ 1) if lane == 0 else place(chip ^ 1, 0, grp)
+
+        def across_target(chip, lane, grp):
+            return place(chip ^ 1, lane ^ 1, grp ^ 1)
+
+        return [pairs_of(split_target), pairs_of(across_target)], True
+
+    todo = []
+    for axis, size in (("grp", groups), ("blk", chips)):
+        stride = 1
+        for factor in radices(size):
+            todo.append((axis, stride, factor))
+            stride *= factor
+    first = [("grp", 1, 2), ("blk", 1, 2)]
+    if core == 2 and all(step in todo for step in first):
+        todo = [step for step in todo if step not in first]
+        steps.append(both())
+    return steps + [along(*step) for step in todo]
 
 
 def mm(first, second, dims):
@@ -390,11 +387,10 @@
     precond_out[...] = precond
     image_out[...] = image
     grams = dots(
-        jnp.concatenate([residual[...], precond, image], axis=0), jnp.concatenate([precond, image], axis=0)
+        jnp.concatenate([residual[...], precond], axis=0), jnp.concatenate([precond, image], axis=0)
     )
     slots = couple.shape[0]
-    first = grams[:nrhs, :nrhs]
-    second = 0.5 * (grams[nrhs : 2 * nrhs, nrhs:] + grams[2 * nrhs :, :nrhs])
+    first, second = grams[:nrhs, :nrhs], grams[nrhs:, nrhs:]
     tile = tiles_of(
         even, corner_values(precond, couple[...]), map_row[:, :slots], first, second, jnp.zeros_like(first)
     )
@@ -469,6 +465,7 @@
     slots = couple.shape[0]
     corner_sum, squares = total_of(left, right, maps, slots, corners)
     gram, local_energy, _ = untile(squares)
+    local_energy = symmetric(local_energy)
     solved = coarse_solve(corner_sum, (coarse_high[...], coarse_low[...]))
     energy = local_energy + both_orders(corner_sum, solved)
     unit = (lax.broadcasted_iota(jnp.int32, (nrhs, nrhs), 0) == lanes_of((nrhs, nrhs))).astype(F32)
@@ -496,15 +493,15 @@
     precond = precond_in[...] - change[:, width:]
 
     image = mm(precond.astype(BF16), blocks[...], NN)
-    left = jnp.concatenate([residual, precond, precond_in[...], image_in[...]], axis=0)
-    grams = dots(left, jnp.concatenate([precond, image], axis=0))
+    early = dots(jnp.concatenate([residual, image_in[...]], axis=0), precond)
+    late = dots(jnp.concatenate([precond, precond_in[...]], axis=0), image)
     tile = tiles_of(
         even,
         corner_values(precond, couple[...]),
         jnp.zeros((1, slots), F32),
-        grams[:nrhs, :nrhs],
-        grams[nrhs : 2 * nrhs, nrhs:],
-        grams[2 * nrhs : 3 * nrhs, nrhs:] + grams[3 * nrhs :, :nrhs],
+        early[:nrhs],
+        late[:nrhs],
+        late[nrhs:] + early[nrhs:],
     )
     tile_out[...] = tile
     inner, outer = split(even, image[:, :half], image[:, half:])
@@ -602,19 +599,20 @@
         values = tile + got[:, got.shape[1] - TILE :]
         known = maps
         left, right = None, None
-        for index, turns in enumerate(steps):
+        for index, (turns, relayed) in enumerate(steps):
             if index > 0:
                 held = left.shape[0] + right.shape[0] - 16
-                if left.shape[1] == TILE and 8 * MOST < 2 * held * (1 + len(turns)):
+                if left.shape[1] == TILE and 8 * MOST < 2 * held * (1 + len(turns) + relayed):
                     known = known or (left, right)
                     left, right = densify(left, known[0]), densify(right, known[1])
                 values = united([left, right])
-            if index == max(len(steps) - 2, 0):
+            if index == max(len(steps) - (1 if maps else 2), 0):
                 result, sends = follow(got, from_outer)
                 values, result, sends = lax.optimization_barrier((values, result, sends))
                 result = (*(exchange(*sends) if sends else ()), *result)
             left = values
-            right = united([permute(values, pairs) for pairs in turns])
+            terms = [permute(values, pairs) for pairs in turns]
+            right = united(terms + [permute(terms[0], inner)] * relayed)
         known = known or (left, right)
         if left.shape[1] == TILE:
             left = densify(left, known[0])

time: 46.1 us -> 43.9 us (0.952)
  waiting for transfers between devices: 11.6 us -> 9.85 us
    ppermute x16 -> x18, waiting for transfers between devices: 11.6 us -> 9.85 us  [permute(): return lax.ppermute(values, AXES, pairs)]
    ppermute x16 -> x18, starting transfers between devices: 21.6 us -> 21.3 us  [permute(): return lax.ppermute(values, AXES, pairs)]
  transfers between devices with their start and end apart: 16 -> 18, of which waited for: 13 -> 11; matrix products, arithmetic and copies ran while one was open for 0% -> 0% of each run, Pallas kernels for 8% -> 8%
where the time goes in v7:
time: 43.9 us; the launch traced here: 43.7 us
  starting transfers between devices  21.3 us (49%)
  Pallas kernels  11.7 us (27%)
  waiting for transfers between devices  9.85 us (22%)
  between operations  0.78 us (2%)
    ppermute x18, starting transfers between devices, permute(): return lax.ppermute(values, AXES, pairs)  21.3 us
    pallas_call x10, Pallas kernels, call(): pl.pallas_call(body, out_shape=shapes, in_specs=specs or [VMEM] * len(arg...  11.7 us
    ppermute x18, waiting for transfers between devices, permute(): return lax.ppermute(values, AXES, pairs)  9.85 us
  transfers between devices with their start and end apart: 18, of which 11 were waited for; matrix products, arithmetic and copies ran while one was open for 0% of the time, Pallas kernels for 8%

profile of v7, /device:TPU:0, one launch (start us, length us, event | category | flops | bytes accessed | tf_op | source)
XLA Modules:
  0.0 43.7 jit_solution(13067169300083523856)
XLA Ops:
  0.6 1.8 %shard_map.86 = (f32[16,1024]{1,0:T(8,128)S(1)}, f32[16,512]{1,0:T(8,128)S(1)}, f32[16,512]{1,0:T(8,128)S(1)}, f32[16,1024]{1,0:T(8,128)S(1)}, f32[1,1024]{1,0:T(1,128)S(1)}, /*index=5*/bf16[8,128,1024]{2,1,0:T(8,128)(2,1)S(1)}) custom-call(f32[1,16,1024]{2,1,0:T(8,128)} %rhs.1, s32[1,1024]{1,0:T(1,128)} %signs.1, bf16[1,1024,1024]{2,1,0:T(8,128)(2,1)} %blocks.2), custom_call_target="tpu_custom_call" | custom-call | flops 33554432 | bytes 2166784 | tf_op jit(solution)/shard_map/pallas_call | solution.py:558
  2.4 0.5 %collective-permute-start = (f32[16,512]{1,0:T(8,128)S(1)}, f32[16,512]{1,0:T(8,128)S(1)}, u32[]{:S(2)}, u32[]{:S(2)}) collective-permute-start(f32[16,512]{1,0:T(8,128)S(1)} %get-tuple-element.50), channel_id=1, source_target_pairs={{0,2},{1,3},{2,0},{3,1},{4,6},{5,7},{6,4},{7,5},{8,10},{9,11},{10,... | collective-permute-start | bytes 98312 | tf_op jit(solution)/shard_map/ppermute | solution.py:580
  3.0 2.6 %collective-permute-start.1 = (f32[16,512]{1,0:T(8,128)S(1)}, f32[16,512]{1,0:T(8,128)S(1)}, u32[]{:S(2)}, u32[]{:S(2)}) collective-permute-start(f32[16,512]{1,0:T(8,128)S(1)} %get-tuple-element.51), channel_id=1, source_target_pairs={{0,1},{1,0},{2,4},{3,5},{4,2},{5,3},{6,8},{7,9},{8,6},{9,7},{10,12... | collective-permute-start | bytes 98312 | tf_op jit(solution)/shard_map/ppermute | solution.py:580
  5.5 1.6 %shard_map.87 = (bf16[1024,1024]{1,0:T(8,128)(2,1)S(1)}, bf16[24,512]{1,0:T(8,128)(2,1)S(1)}, f32[1,128]{1,0:T(1,128)S(1)}, f32[16,512]{1,0:T(8,128)S(1)}, f32[16,512]{1,0:T(8,128)S(1)}) custom-call(bf16[1,1024,1024]{2,1,0:T(8,128)(2,1)} %blocks.3, bf16[1,24,512]{2,1,0:T(8,128)(2,1)} %coupling.1, s32[1,24]{1,0:T(1,128)} %corner_map.1, ...), custom_call_target="tpu_custom_call" | custom-call | bytes 2125920 | tf_op jit(solution)/shard_map/pallas_call | solution.py:558
  7.1 0.0 collective-permute-done.from_inner
  7.2 0.3 collective-permute-done.1.from_outer
  7.4 0.0 copy-start
  7.4 0.7 %shard_map.88 = (f32[16,1024]{1,0:T(8,128)S(1)}, f32[16,1024]{1,0:T(8,128)S(1)}, f32[16,128]{1,0:T(8,128)S(1)}, f32[16,1152]{1,0:T(8,128)S(1)}, f32[16,1024]{1,0:T(8,128)S(1)}) custom-call(f32[16,1024]{1,0:T(8,128)S(1)} %get-tuple-element.49.product, f32[16,512]{1,0:T(8,128)S(1)} %collective-permute-done.from_inner, ...), custom_call_target="tpu_custom_call" | custom-call | flops 33554432 | bytes 2384384 | tf_op jit(solution)/shard_map/pallas_call | solution.py:558
  8.1 0.2 collective-permute-start.2
  8.2 2.0 %collective-permute-start.6 = (f32[16,1024]{1,0:T(8,128)S(1)}, f32[16,1024]{1,0:T(8,128)S(1)}, u32[]{:S(2)}, u32[]{:S(2)}) collective-permute-start(f32[16,1024]{1,0:T(8,128)S(1)} %get-tuple-element.62), channel_id=1, source_target_pairs={{0,1},{1,0},{2,4},{3,5},{4,2},{5,3},{6,8},{7,9},{8,6},{9,7},{10,12... | collective-permute-start | bytes 196616 | tf_op jit(solution)/shard_map/ppermute | solution.py:580
  10.3 0.0 collective-permute-done.2.got
  10.3 1.9 %collective-permute-start.3 = (f32[16,128]{1,0:T(8,128)S(1)}, f32[16,128]{1,0:T(8,128)S(1)}, u32[]{:S(2)}, u32[]{:S(2)}) collective-permute-start(f32[16,128]{1,0:T(8,128)S(1)} %slice_add_fusion.1), channel_id=1, source_target_pairs={{0,3},{1,2},{2,4},{3,5},{4,7},{5,6},{6,0},{7,1},{8,11},{9,10},{10,... | collective-permute-start | bytes 24584 | tf_op jit(solution)/shard_map/ppermute | solution.py:580
  12.1 0.7 %collective-permute-start.4 = (f32[16,128]{1,0:T(8,128)S(1)}, f32[16,128]{1,0:T(8,128)S(1)}, u32[]{:S(2)}, u32[]{:S(2)}) collective-permute-start(f32[16,128]{1,0:T(8,128)S(1)} %slice_add_fusion.1), channel_id=1, source_target_pairs={{0,7},{1,6},{2,5},{3,4},{4,3},{5,2},{6,1},{7,0},{8,15},{9,14},{10,... | collective-permute-start | bytes 24584 | tf_op jit(solution)/shard_map/ppermute | solution.py:580
  12.9 0.6 %collective-permute-done.3 = f32[16,128]{1,0:T(8,128)S(1)} collective-permute-done((f32[16,128]{1,0:T(8,128)S(1)}, f32[16,128]{1,0:T(8,128)S(1)}, u32[]{:S(2)}, u32[]{:S(2)}) %collective-permute-start.3) | collective-permute-done | bytes 8224 | tf_op jit(solution)/shard_map/ppermute | solution.py:580
  13.5 0.6 %collective-permute-start.5 = (f32[16,128]{1,0:T(8,128)S(1)}, f32[16,128]{1,0:T(8,128)S(1)}, u32[]{:S(2)}, u32[]{:S(2)}) collective-permute-start(f32[16,128]{1,0:T(8,128)S(1)} %collective-permute-done.3), channel_id=1, source_target_pairs={{0,2},{1,3},{2,0},{3,1},{4,6},{5,7},{6,4},{7,5},{8,10},{9,11},{10,... | collective-permute-start | bytes 24584 | tf_op jit(solution)/shard_map/ppermute | solution.py:580
  14.1 0.0 collective-permute-done.6.from_outer
  14.1 0.5 %shard_map.89 = (f32[16,1024]{1,0:T(8,128)S(1)}, f32[16,1024]{1,0:T(8,128)S(1)}, f32[48,1024]{1,0:T(8,128)S(1)}, bf16[48,1024]{1,0:T(8,128)(2,1)S(1)}, f32[1,128...) custom-call(f32[16,1024]{1,0:T(8,128)S(1)} %get-tuple-element.61.image.image_in, ...), custom_call_target="tpu_custom_call" | custom-call | flops 167772160 | bytes 2327040 | tf_op jit(solution)/shard_map/pallas_call | solution.py:558
  14.6 1.6 %collective-permute-done.4 = f32[16,128]{1,0:T(8,128)S(1)} collective-permute-done((f32[16,128]{1,0:T(8,128)S(1)}, f32[16,128]{1,0:T(8,128)S(1)}, u32[]{:S(2)}, u32[]{:S(2)}) %collective-permute-start.4) | collective-permute-done | bytes 8224 | tf_op jit(solution)/shard_map/ppermute | solution.py:580
  16.2 0.0 collective-permute-done.5
  16.3 1.4 %collective-permute-start.7 = (f32[40,128]{1,0:T(8,128)S(1)}, f32[40,128]{1,0:T(8,128)S(1)}, u32[]{:S(2)}, u32[]{:S(2)}) collective-permute-start(f32[40,128]{1,0:T(8,128)S(1)} %constant_dynamic-update-slice_fusion), channel_id=1, source_target_pairs={{0,10},{1,11},{2,8},{3,9},{4,14},{5,15},{6,12},{7,13},{8,2},{9,3},... | collective-permute-start | bytes 61448 | tf_op jit(solution)/shard_map/ppermute | solution.py:580
  17.6 0.4 collective-permute-start.9
  18.0 0.7 %collective-permute-start.10 = (f32[72,512]{1,0:T(8,128)S(1)}, f32[72,512]{1,0:T(8,128)S(1)}, u32[]{:S(2)}, u32[]{:S(2)}) collective-permute-start(f32[72,512]{1,0:T(8,128)S(1)} %get-tuple-element.73), channel_id=1, source_target_pairs={{0,1},{1,0},{2,4},{3,5},{4,2},{5,3},{6,8},{7,9},{8,6},{9,7},{10,12... | collective-permute-start | bytes 442376 | tf_op jit(solution)/shard_map/ppermute | solution.py:580
  18.7 0.8 %collective-permute-done.7 = f32[40,128]{1,0:T(8,128)S(1)} collective-permute-done((f32[40,128]{1,0:T(8,128)S(1)}, f32[40,128]{1,0:T(8,128)S(1)}, u32[]{:S(2)}, u32[]{:S(2)}) %collective-permute-start.7) | collective-permute-done | bytes 20512 | tf_op jit(solution)/shard_map/ppermute | solution.py:580
  19.5 2.4 %collective-permute-start.8 = (f32[72,128]{1,0:T(8,128)S(1)}, f32[72,128]{1,0:T(8,128)S(1)}, u32[]{:S(2)}, u32[]{:S(2)}) collective-permute-start(f32[72,128]{1,0:T(8,128)S(1)} %pad_maximum_fusion.tiles.maps), channel_id=1, source_target_pairs={{0,18},{1,19},{2,16},{3,17},{4,22},{5,23},{6,20},{7,21},{8,26},{9,... | collective-permute-start | bytes 110600 | tf_op jit(solution)/shard_map/ppermute | solution.py:580
  21.9 0.0 copy-done
  21.9 0.3 shard_map.91
  22.3 0.5 %shard_map.90.left = f32[16,896]{1,0:T(8,128)S(1)} custom-call(f32[72,128]{1,0:T(8,128)S(1)} %pad_maximum_fusion.tiles.maps, f32[72,128]{1,0:T(8,128)S(1)} %pad_maximum_fusion.tiles.maps), custom_call_target="tpu_custom_call" | custom-call | flops 33554432 | bytes 73728 | tf_op jit(solution)/shard_map/pallas_call | solution.py:558
  22.7 1.3 %collective-permute-done.8.right.maps = f32[72,128]{1,0:T(8,128)S(1)} collective-permute-done((f32[72,128]{1,0:T(8,128)S(1)}, f32[72,128]{1,0:T(8,128)S(1)}, u32[]{:S(2)}, u32[]{:S(2)}) %collective-permute-start.8) | collective-permute-done | bytes 36896 | tf_op jit(solution)/shard_map/ppermute | solution.py:580
  24.0 0.0 collective-permute-done.9.from_inner
  24.0 0.0 collective-permute-done.10.from_outer
  24.0 2.8 %shard_map.92 = (f32[16,768]{1,0:T(8,128)S(1)}, f32[16,1024]{1,0:T(8,128)S(1)}, f32[16,1024]{1,0:T(8,128)S(1)}, f32[16,1024]{1,0:T(8,128)S(1)}, f32[16,1024]{1,0...) custom-call(f32[16,896]{1,0:T(8,128)S(1)} %shard_map.90.left, ...), custom_call_target="tpu_custom_call" | custom-call | flops 33554432 | bytes 5530112 | tf_op jit(solution)/shard_map/pallas_call | solution.py:558
  26.8 0.1 collective-permute-start.11
  27.0 1.1 %collective-permute-done.11.got = f32[16,640]{1,0:T(8,128)S(1)} collective-permute-done((f32[16,640]{1,0:T(8,128)S(1)}, f32[16,640]{1,0:T(8,128)S(1)}, u32[]{:S(2)}, u32[]{:S(2)}) %collective-permute-start.11) | collective-permute-done | bytes 40992 | tf_op jit(solution)/shard_map/ppermute | solution.py:580
  28.1 1.1 %collective-permute-start.12 = (f32[16,128]{1,0:T(8,128)S(1)}, f32[16,128]{1,0:T(8,128)S(1)}, u32[]{:S(2)}, u32[]{:S(2)}) collective-permute-start(f32[16,128]{1,0:T(8,128)S(1)} %slice_add_fusion), channel_id=1, source_target_pairs={{0,3},{1,2},{2,4},{3,5},{4,7},{5,6},{6,0},{7,1},{8,11},{9,10},{10,... | collective-permute-start | bytes 24584 | tf_op jit(solution)/shard_map/ppermute | solution.py:580
  29.2 1.2 %collective-permute-start.13 = (f32[16,128]{1,0:T(8,128)S(1)}, f32[16,128]{1,0:T(8,128)S(1)}, u32[]{:S(2)}, u32[]{:S(2)}) collective-permute-start(f32[16,128]{1,0:T(8,128)S(1)} %slice_add_fusion), channel_id=1, source_target_pairs={{0,7},{1,6},{2,5},{3,4},{4,3},{5,2},{6,1},{7,0},{8,15},{9,14},{10,... | collective-permute-start | bytes 24584 | tf_op jit(solution)/shard_map/ppermute | solution.py:580
  30.4 0.7 %collective-permute-done.12 = f32[16,128]{1,0:T(8,128)S(1)} collective-permute-done((f32[16,128]{1,0:T(8,128)S(1)}, f32[16,128]{1,0:T(8,128)S(1)}, u32[]{:S(2)}, u32[]{:S(2)}) %collective-permute-start.12) | collective-permute-done | bytes 8224 | tf_op jit(solution)/shard_map/ppermute | solution.py:580
  31.1 0.2 collective-permute-start.14
  31.3 1.4 %collective-permute-start.16 = (f32[16,512]{1,0:T(8,128)S(1)}, f32[16,512]{1,0:T(8,128)S(1)}, u32[]{:S(2)}, u32[]{:S(2)}) collective-permute-start(f32[16,512]{1,0:T(8,128)S(1)} %get-tuple-element.85), channel_id=1, source_target_pairs={{0,1},{1,0},{2,4},{3,5},{4,2},{5,3},{6,8},{7,9},{8,6},{9,7},{10,12... | collective-permute-start | bytes 98312 | tf_op jit(solution)/shard_map/ppermute | solution.py:580
  32.7 0.5 %collective-permute-done.13 = f32[16,128]{1,0:T(8,128)S(1)} collective-permute-done((f32[16,128]{1,0:T(8,128)S(1)}, f32[16,128]{1,0:T(8,128)S(1)}, u32[]{:S(2)}, u32[]{:S(2)}) %collective-permute-start.13) | collective-permute-done | bytes 8224 | tf_op jit(solution)/shard_map/ppermute | solution.py:580
  33.2 0.0 collective-permute-done.14
  33.2 1.6 %collective-permute-start.15 = (f32[40,128]{1,0:T(8,128)S(1)}, f32[40,128]{1,0:T(8,128)S(1)}, u32[]{:S(2)}, u32[]{:S(2)}) collective-permute-start(f32[40,128]{1,0:T(8,128)S(1)} %constant_dynamic-update-slice_fusion.5), channel_id=1, source_target_pairs={{0,10},{1,11},{2,8},{3,9},{4,14},{5,15},{6,12},{7,13},{8,2},{9,3},... | collective-permute-start | bytes 61448 | tf_op jit(solution)/shard_map/ppermute | solution.py:580
  34.9 0.4 collective-permute-done.16.from_outer
  35.2 0.2 shard_map.93
  35.4 1.1 %collective-permute-done.15 = f32[40,128]{1,0:T(8,128)S(1)} collective-permute-done((f32[40,128]{1,0:T(8,128)S(1)}, f32[40,128]{1,0:T(8,128)S(1)}, u32[]{:S(2)}, u32[]{:S(2)}) %collective-permute-start.15) | collective-permute-done | bytes 20512 | tf_op jit(solution)/shard_map/ppermute | solution.py:580
  36.5 2.3 %collective-permute-start.17 = (f32[72,128]{1,0:T(8,128)S(1)}, f32[72,128]{1,0:T(8,128)S(1)}, u32[]{:S(2)}, u32[]{:S(2)}) collective-permute-start(f32[72,128]{1,0:T(8,128)S(1)} %constant_dynamic-update-slice_fusion.10.tiles), channel_id=1, source_target_pairs={{0,18},{1,19},{2,16},{3,17},{4,22},{5,23},{6,20},{7,21},{8,26},{9,... | collective-permute-start | bytes 110600 | tf_op jit(solution)/shard_map/ppermute | solution.py:580
  38.9 0.5 %shard_map.94.left = f32[16,896]{1,0:T(8,128)S(1)} custom-call(f32[72,128]{1,0:T(8,128)S(1)} %constant_dynamic-update-slice_fusion.10.tiles, f32[72,128]{1,0:T(8,128)S(1)} %pad_maximum_fusion.tiles.maps), custom_call_target="tpu_custom_call" | custom-call | flops 33554432 | bytes 73728 | tf_op jit(solution)/shard_map/pallas_call | solution.py:558
  39.3 1.5 %collective-permute-done.17.right = f32[72,128]{1,0:T(8,128)S(1)} collective-permute-done((f32[72,128]{1,0:T(8,128)S(1)}, f32[72,128]{1,0:T(8,128)S(1)}, u32[]{:S(2)}, u32[]{:S(2)}) %collective-permute-start.17) | collective-permute-done | bytes 36896 | tf_op jit(solution)/shard_map/ppermute | solution.py:580
  40.9 2.9 %shard_map.95 = (f32[1,16,1024]{2,1,0:T(8,128)}, f32[1,16,1024]{2,1,0:T(8,128)}) custom-call(f32[16,896]{1,0:T(8,128)S(1)} %shard_map.94.left, f32[72,128]{1,0:T(8,128)S(1)} %collective-permute-done.17.right, f32[72,128]{1,0:T(8,128)S(1)} %collective-permute-done.8.right.maps, f32[16,1024]{1,0:T(8,128)S(1)} %get-tuple-element.90.part, ...), custom_call_target="tpu_custom_call" | custom-call | flops 33554432 | bytes 3043840 | tf_op jit(solution)/shard_map/pallas_call | solution.py:558
  (22 shorter events, 0.1 us)
Async XLA Ops:
  2.4 4.7 %collective-permute-start = (f32[16,512]{1,0:T(8,128)S(1)}, f32[16,512]{1,0:T(8,128)S(1)}, u32[]{:S(2)}, u32[]{:S(2)}) collective-permute-start(f32[16,512]{1,0:T(8,128)S(1)} %get-tuple-element.50), channel_id=1, source_target_pairs={{0,2},{1,3},{2,0},{3,1},{4,6},{5,7},{6,4},{7,5},{8,10},{9,11},{10,... | collective-permute-start | bytes 98312 | tf_op jit(solution)/shard_map/ppermute | solution.py:580
  3.0 4.5 %collective-permute-start.1 = (f32[16,512]{1,0:T(8,128)S(1)}, f32[16,512]{1,0:T(8,128)S(1)}, u32[]{:S(2)}, u32[]{:S(2)}) collective-permute-start(f32[16,512]{1,0:T(8,128)S(1)} %get-tuple-element.51), channel_id=1, source_target_pairs={{0,1},{1,0},{2,4},{3,5},{4,2},{5,3},{6,8},{7,9},{8,6},{9,7},{10,12... | collective-permute-start | bytes 98312 | tf_op jit(solution)/shard_map/ppermute | solution.py:580
  7.4 14.5 %copy-start = (f32[768,768]{1,0:T(8,128)S(1)}, f32[768,768]{1,0:T(8,128)}, u32[]{:S(2)}) copy-start(f32[768,768]{1,0:T(8,128)} %coarse.1) | copy-start | bytes 7077892
  8.1 2.2 %collective-permute-start.2 = (f32[16,1152]{1,0:T(8,128)S(1)}, f32[16,1152]{1,0:T(8,128)S(1)}, u32[]{:S(2)}, u32[]{:S(2)}) collective-permute-start(f32[16,1152]{1,0:T(8,128)S(1)} %get-tuple-element.60), channel_id=1, source_target_pairs={{0,2},{1,3},{2,0},{3,1},{4,6},{5,7},{6,4},{7,5},{8,10},{9,11},{10,... | collective-permute-start | bytes 221192 | tf_op jit(solution)/shard_map/ppermute | solution.py:580
  8.2 5.9 %collective-permute-start.6 = (f32[16,1024]{1,0:T(8,128)S(1)}, f32[16,1024]{1,0:T(8,128)S(1)}, u32[]{:S(2)}, u32[]{:S(2)}) collective-permute-start(f32[16,1024]{1,0:T(8,128)S(1)} %get-tuple-element.62), channel_id=1, source_target_pairs={{0,1},{1,0},{2,4},{3,5},{4,2},{5,3},{6,8},{7,9},{8,6},{9,7},{10,12... | collective-permute-start | bytes 196616 | tf_op jit(solution)/shard_map/ppermute | solution.py:580
  10.3 3.2 %collective-permute-start.3 = (f32[16,128]{1,0:T(8,128)S(1)}, f32[16,128]{1,0:T(8,128)S(1)}, u32[]{:S(2)}, u32[]{:S(2)}) collective-permute-start(f32[16,128]{1,0:T(8,128)S(1)} %slice_add_fusion.1), channel_id=1, source_target_pairs={{0,3},{1,2},{2,4},{3,5},{4,7},{5,6},{6,0},{7,1},{8,11},{9,10},{10,... | collective-permute-start | bytes 24584 | tf_op jit(solution)/shard_map/ppermute | solution.py:580
  12.1 4.1 %collective-permute-start.4 = (f32[16,128]{1,0:T(8,128)S(1)}, f32[16,128]{1,0:T(8,128)S(1)}, u32[]{:S(2)}, u32[]{:S(2)}) collective-permute-start(f32[16,128]{1,0:T(8,128)S(1)} %slice_add_fusion.1), channel_id=1, source_target_pairs={{0,7},{1,6},{2,5},{3,4},{4,3},{5,2},{6,1},{7,0},{8,15},{9,14},{10,... | collective-permute-start | bytes 24584 | tf_op jit(solution)/shard_map/ppermute | solution.py:580
  13.5 2.7 %collective-permute-start.5 = (f32[16,128]{1,0:T(8,128)S(1)}, f32[16,128]{1,0:T(8,128)S(1)}, u32[]{:S(2)}, u32[]{:S(2)}) collective-permute-start(f32[16,128]{1,0:T(8,128)S(1)} %collective-permute-done.3), channel_id=1, source_target_pairs={{0,2},{1,3},{2,0},{3,1},{4,6},{5,7},{6,4},{7,5},{8,10},{9,11},{10,... | collective-permute-start | bytes 24584 | tf_op jit(solution)/shard_map/ppermute | solution.py:580
  16.3 3.3 %collective-permute-start.7 = (f32[40,128]{1,0:T(8,128)S(1)}, f32[40,128]{1,0:T(8,128)S(1)}, u32[]{:S(2)}, u32[]{:S(2)}) collective-permute-start(f32[40,128]{1,0:T(8,128)S(1)} %constant_dynamic-update-slice_fusion), channel_id=1, source_target_pairs={{0,10},{1,11},{2,8},{3,9},{4,14},{5,15},{6,12},{7,13},{8,2},{9,3},... | collective-permute-start | bytes 61448 | tf_op jit(solution)/shard_map/ppermute | solution.py:580
  17.6 6.4 %collective-permute-start.9 = (f32[72,512]{1,0:T(8,128)S(1)}, f32[72,512]{1,0:T(8,128)S(1)}, u32[]{:S(2)}, u32[]{:S(2)}) collective-permute-start(f32[72,512]{1,0:T(8,128)S(1)} %get-tuple-element.72), channel_id=1, source_target_pairs={{0,2},{1,3},{2,0},{3,1},{4,6},{5,7},{6,4},{7,5},{8,10},{9,11},{10,... | collective-permute-start | bytes 442376 | tf_op jit(solution)/shard_map/ppermute | solution.py:580
  18.0 6.0 %collective-permute-start.10 = (f32[72,512]{1,0:T(8,128)S(1)}, f32[72,512]{1,0:T(8,128)S(1)}, u32[]{:S(2)}, u32[]{:S(2)}) collective-permute-start(f32[72,512]{1,0:T(8,128)S(1)} %get-tuple-element.73), channel_id=1, source_target_pairs={{0,1},{1,0},{2,4},{3,5},{4,2},{5,3},{6,8},{7,9},{8,6},{9,7},{10,12... | collective-permute-start | bytes 442376 | tf_op jit(solution)/shard_map/ppermute | solution.py:580
  19.5 4.4 %collective-permute-start.8 = (f32[72,128]{1,0:T(8,128)S(1)}, f32[72,128]{1,0:T(8,128)S(1)}, u32[]{:S(2)}, u32[]{:S(2)}) collective-permute-start(f32[72,128]{1,0:T(8,128)S(1)} %pad_maximum_fusion.tiles.maps), channel_id=1, source_target_pairs={{0,18},{1,19},{2,16},{3,17},{4,22},{5,23},{6,20},{7,21},{8,26},{9,... | collective-permute-start | bytes 110600 | tf_op jit(solution)/shard_map/ppermute | solution.py:580
  26.8 1.3 %collective-permute-start.11 = (f32[16,640]{1,0:T(8,128)S(1)}, f32[16,640]{1,0:T(8,128)S(1)}, u32[]{:S(2)}, u32[]{:S(2)}) collective-permute-start(f32[16,640]{1,0:T(8,128)S(1)} %get-tuple-element.83), channel_id=1, source_target_pairs={{0,2},{1,3},{2,0},{3,1},{4,6},{5,7},{6,4},{7,5},{8,10},{9,11},{10,... | collective-permute-start | bytes 122888 | tf_op jit(solution)/shard_map/ppermute | solution.py:580
  28.1 3.1 %collective-permute-start.12 = (f32[16,128]{1,0:T(8,128)S(1)}, f32[16,128]{1,0:T(8,128)S(1)}, u32[]{:S(2)}, u32[]{:S(2)}) collective-permute-start(f32[16,128]{1,0:T(8,128)S(1)} %slice_add_fusion), channel_id=1, source_target_pairs={{0,3},{1,2},{2,4},{3,5},{4,7},{5,6},{6,0},{7,1},{8,11},{9,10},{10,... | collective-permute-start | bytes 24584 | tf_op jit(solution)/shard_map/ppermute | solution.py:580
  29.2 4.0 %collective-permute-start.13 = (f32[16,128]{1,0:T(8,128)S(1)}, f32[16,128]{1,0:T(8,128)S(1)}, u32[]{:S(2)}, u32[]{:S(2)}) collective-permute-start(f32[16,128]{1,0:T(8,128)S(1)} %slice_add_fusion), channel_id=1, source_target_pairs={{0,7},{1,6},{2,5},{3,4},{4,3},{5,2},{6,1},{7,0},{8,15},{9,14},{10,... | collective-permute-start | bytes 24584 | tf_op jit(solution)/shard_map/ppermute | solution.py:580
  31.1 2.0 %collective-permute-start.14 = (f32[16,128]{1,0:T(8,128)S(1)}, f32[16,128]{1,0:T(8,128)S(1)}, u32[]{:S(2)}, u32[]{:S(2)}) collective-permute-start(f32[16,128]{1,0:T(8,128)S(1)} %collective-permute-done.12), channel_id=1, source_target_pairs={{0,2},{1,3},{2,0},{3,1},{4,6},{5,7},{6,4},{7,5},{8,10},{9,11},{10,... | collective-permute-start | bytes 24584 | tf_op jit(solution)/shard_map/ppermute | solution.py:580
  31.3 3.9 %collective-permute-start.16 = (f32[16,512]{1,0:T(8,128)S(1)}, f32[16,512]{1,0:T(8,128)S(1)}, u32[]{:S(2)}, u32[]{:S(2)}) collective-permute-start(f32[16,512]{1,0:T(8,128)S(1)} %get-tuple-element.85), channel_id=1, source_target_pairs={{0,1},{1,0},{2,4},{3,5},{4,2},{5,3},{6,8},{7,9},{8,6},{9,7},{10,12... | collective-permute-start | bytes 98312 | tf_op jit(solution)/shard_map/ppermute | solution.py:580
  33.2 3.3 %collective-permute-start.15 = (f32[40,128]{1,0:T(8,128)S(1)}, f32[40,128]{1,0:T(8,128)S(1)}, u32[]{:S(2)}, u32[]{:S(2)}) collective-permute-start(f32[40,128]{1,0:T(8,128)S(1)} %constant_dynamic-update-slice_fusion.5), channel_id=1, source_target_pairs={{0,10},{1,11},{2,8},{3,9},{4,14},{5,15},{6,12},{7,13},{8,2},{9,3},... | collective-permute-start | bytes 61448 | tf_op jit(solution)/shard_map/ppermute | solution.py:580
  36.5 4.3 %collective-permute-start.17 = (f32[72,128]{1,0:T(8,128)S(1)}, f32[72,128]{1,0:T(8,128)S(1)}, u32[]{:S(2)}, u32[]{:S(2)}) collective-permute-start(f32[72,128]{1,0:T(8,128)S(1)} %constant_dynamic-update-slice_fusion.10.tiles), channel_id=1, source_target_pairs={{0,18},{1,19},{2,16},{3,17},{4,22},{5,23},{6,20},{7,21},{8,26},{9,... | collective-permute-start | bytes 110600 | tf_op jit(solution)/shard_map/ppermute | solution.py:580

commit v8 on v7

--- a/solution.py
+++ b/solution.py
@@ -118,9 +118,10 @@
 
 
 def dots(first, second):
-    product = folded(mm(stacked(first), stacked(second), NT))
-    count = second.shape[0]
-    return product[:, :count] + product[:, count:]
+    first_high, first_low = halves(first)
+    high, low = halves(second)
+    left = jnp.concatenate([first_high, first_low, first_high], axis=1)
+    return mm(left, jnp.concatenate([high, high, low], axis=1), NT)
 
 
 def against(values, exact):
@@ -155,6 +156,13 @@
 
 def transposed(matrix):
     return matrix.T
+
+
+def weighted(weights, values):
+    top = weights.astype(BF16).astype(F32)
+    left = transposed(jnp.concatenate([top, weights - top, top], axis=0)).astype(BF16)
+    high, low = halves(values)
+    return mm(left, jnp.concatenate([high, high, low], axis=0), NN)
 
 
 def eliminate(matrix, target, guide):
@@ -386,11 +394,8 @@
     image = mm(precond.astype(BF16), blocks[...], NN)
     precond_out[...] = precond
     image_out[...] = image
-    grams = dots(
-        jnp.concatenate([residual[...], precond], axis=0), jnp.concatenate([precond, image], axis=0)
-    )
+    first, second = dots(residual[...], precond), dots(precond, image)
     slots = couple.shape[0]
-    first, second = grams[:nrhs, :nrhs], grams[nrhs:, nrhs:]
     tile = tiles_of(
         even, corner_values(precond, couple[...]), map_row[:, :slots], first, second, jnp.zeros_like(first)
     )
@@ -473,7 +478,7 @@
     both = eliminate(
         jnp.stack([2.0 * energy, old]), jnp.stack([gram, unit]), jnp.stack([2.0 * local_energy, old])
     )
-    alpha, inverse = transposed(both[0]), both[1]
+    alpha, inverse = both[0], both[1]
 
     rows = spread.shape[0]
     wide = map_row.shape[1]
@@ -488,7 +493,7 @@
         for turn, side in enumerate(sides, 1)
     ]
     change = live * (own - jnp.concatenate(others, axis=1))
-    change = product_of(alpha, jnp.concatenate([whole, change], axis=1))
+    change = weighted(alpha, jnp.concatenate([whole, change], axis=1))
     residual = residual_in[...] - change[:, :width]
     precond = precond_in[...] - change[:, width:]
 
@@ -513,7 +518,7 @@
     whole_out[...] = whole
     precond_out[...] = precond
     image_out[...] = image
-    small_out[...] = jnp.concatenate([inverse, energy, alpha, jnp.zeros((nrhs, 128 - 3 * nrhs), F32)], axis=1)
+    small_out[...] = jnp.concatenate([inverse, energy, transposed(alpha), jnp.zeros((nrhs, 128 - 3 * nrhs), F32)], axis=1)
 
 
 def assemble_kernel(count, image, got, from_outer, small, old_precond, part_out, first_out):
@@ -539,11 +544,11 @@
     solved = coarse_solve(corner_sum, (coarse_high[...], coarse_low[...]))
     old_new = old_new + product_of(old_old, beta) + 2.0 * dots(old_solved[...], corner_sum)
     energy = symmetric(new_new + product_of(turned, old_new)) + both_orders(corner_sum, solved)
-    alpha = transposed(eliminate(2.0 * energy[None], gram[None], 2.0 * new_new[None])[0])
+    alpha = eliminate(2.0 * energy[None], gram[None], 2.0 * new_new[None])[0]
     at = picked(solved, map_row[...])
     whole = part[...] + against(at[:, : columns.shape[0]], columns[...])
     carried = product_of(turned, jnp.concatenate([old_precond[...], old_image[...]], axis=1))
-    change = product_of(alpha, jnp.concatenate([precond[...], whole], axis=1) + carried)
+    change = weighted(alpha, jnp.concatenate([precond[...], whole], axis=1) + carried)
     multipliers_out[0] = sign[...] * (first[...] + change[:, :width])
     residual_out[0] = sign[...] * (residual[...] - change[:, width:])
 

time: 43.9 us -> 43.7 us (level)
  no operation moved by 1% of the time
where the time goes in v8:
time: 43.7 us; the launch traced here: 43.6 us
  starting transfers between devices  21.4 us (49%)
  Pallas kernels  11.4 us (26%)
  waiting for transfers between devices  9.84 us (23%)
  between operations  0.79 us (2%)
    ppermute x18, starting transfers between devices, permute(): return lax.ppermute(values, AXES, pairs)  21.4 us
    pallas_call x10, Pallas kernels, call(): pl.pallas_call(body, out_shape=shapes, in_specs=specs or [VMEM] * len(arg...  11.4 us
    ppermute x18, waiting for transfers between devices, permute(): return lax.ppermute(values, AXES, pairs)  9.84 us
  transfers between devices with their start and end apart: 18, of which 11 were waited for; matrix products, arithmetic and copies ran while one was open for 0% of the time, Pallas kernels for 8%

profile of v8, /device:TPU:0, one launch (start us, length us, event | category | flops | bytes accessed | tf_op | source)
XLA Modules:
  0.0 43.6 jit_solution(10273661191589267604)
XLA Ops:
  0.6 1.8 %shard_map.86 = (f32[16,1024]{1,0:T(8,128)S(1)}, f32[16,512]{1,0:T(8,128)S(1)}, f32[16,512]{1,0:T(8,128)S(1)}, f32[16,1024]{1,0:T(8,128)S(1)}, f32[1,1024]{1,0:T(1,128)S(1)}, /*index=5*/bf16[8,128,1024]{2,1,0:T(8,128)(2,1)S(1)}) custom-call(f32[1,16,1024]{2,1,0:T(8,128)} %rhs.1, s32[1,1024]{1,0:T(1,128)} %signs.1, bf16[1,1024,1024]{2,1,0:T(8,128)(2,1)} %blocks.2), custom_call_target="tpu_custom_call" | custom-call | flops 33554432 | bytes 2166784 | tf_op jit(solution)/shard_map/pallas_call | solution.py:563
  2.4 0.5 %collective-permute-start = (f32[16,512]{1,0:T(8,128)S(1)}, f32[16,512]{1,0:T(8,128)S(1)}, u32[]{:S(2)}, u32[]{:S(2)}) collective-permute-start(f32[16,512]{1,0:T(8,128)S(1)} %get-tuple-element.50), channel_id=1, source_target_pairs={{0,2},{1,3},{2,0},{3,1},{4,6},{5,7},{6,4},{7,5},{8,10},{9,11},{10,... | collective-permute-start | bytes 98312 | tf_op jit(solution)/shard_map/ppermute | solution.py:585
  3.0 2.6 %collective-permute-start.1 = (f32[16,512]{1,0:T(8,128)S(1)}, f32[16,512]{1,0:T(8,128)S(1)}, u32[]{:S(2)}, u32[]{:S(2)}) collective-permute-start(f32[16,512]{1,0:T(8,128)S(1)} %get-tuple-element.51), channel_id=1, source_target_pairs={{0,1},{1,0},{2,4},{3,5},{4,2},{5,3},{6,8},{7,9},{8,6},{9,7},{10,12... | collective-permute-start | bytes 98312 | tf_op jit(solution)/shard_map/ppermute | solution.py:585
  5.5 1.6 %shard_map.87 = (bf16[1024,1024]{1,0:T(8,128)(2,1)S(1)}, bf16[24,512]{1,0:T(8,128)(2,1)S(1)}, f32[1,128]{1,0:T(1,128)S(1)}, f32[16,512]{1,0:T(8,128)S(1)}, f32[16,512]{1,0:T(8,128)S(1)}) custom-call(bf16[1,1024,1024]{2,1,0:T(8,128)(2,1)} %blocks.3, bf16[1,24,512]{2,1,0:T(8,128)(2,1)} %coupling.1, s32[1,24]{1,0:T(1,128)} %corner_map.1, ...), custom_call_target="tpu_custom_call" | custom-call | bytes 2125920 | tf_op jit(solution)/shard_map/pallas_call | solution.py:563
  7.1 0.0 collective-permute-done.from_inner
  7.2 0.3 collective-permute-done.1.from_outer
  7.4 0.0 copy-start
  7.4 0.6 %shard_map.88 = (f32[16,1024]{1,0:T(8,128)S(1)}, f32[16,1024]{1,0:T(8,128)S(1)}, f32[16,128]{1,0:T(8,128)S(1)}, f32[16,1152]{1,0:T(8,128)S(1)}, f32[16,1024]{1,0:T(8,128)S(1)}) custom-call(f32[16,1024]{1,0:T(8,128)S(1)} %get-tuple-element.49.product, f32[16,512]{1,0:T(8,128)S(1)} %collective-permute-done.from_inner, ...), custom_call_target="tpu_custom_call" | custom-call | flops 33554432 | bytes 2384384 | tf_op jit(solution)/shard_map/pallas_call | solution.py:563
  8.1 0.2 collective-permute-start.2
  8.2 2.0 %collective-permute-start.6 = (f32[16,1024]{1,0:T(8,128)S(1)}, f32[16,1024]{1,0:T(8,128)S(1)}, u32[]{:S(2)}, u32[]{:S(2)}) collective-permute-start(f32[16,1024]{1,0:T(8,128)S(1)} %get-tuple-element.62), channel_id=1, source_target_pairs={{0,1},{1,0},{2,4},{3,5},{4,2},{5,3},{6,8},{7,9},{8,6},{9,7},{10,12... | collective-permute-start | bytes 196616 | tf_op jit(solution)/shard_map/ppermute | solution.py:585
  10.3 0.0 collective-permute-done.2.got
  10.3 1.9 %collective-permute-start.3 = (f32[16,128]{1,0:T(8,128)S(1)}, f32[16,128]{1,0:T(8,128)S(1)}, u32[]{:S(2)}, u32[]{:S(2)}) collective-permute-start(f32[16,128]{1,0:T(8,128)S(1)} %slice_add_fusion.1), channel_id=1, source_target_pairs={{0,3},{1,2},{2,4},{3,5},{4,7},{5,6},{6,0},{7,1},{8,11},{9,10},{10,... | collective-permute-start | bytes 24584 | tf_op jit(solution)/shard_map/ppermute | solution.py:585
  12.2 0.7 %collective-permute-start.4 = (f32[16,128]{1,0:T(8,128)S(1)}, f32[16,128]{1,0:T(8,128)S(1)}, u32[]{:S(2)}, u32[]{:S(2)}) collective-permute-start(f32[16,128]{1,0:T(8,128)S(1)} %slice_add_fusion.1), channel_id=1, source_target_pairs={{0,7},{1,6},{2,5},{3,4},{4,3},{5,2},{6,1},{7,0},{8,15},{9,14},{10,... | collective-permute-start | bytes 24584 | tf_op jit(solution)/shard_map/ppermute | solution.py:585
  12.9 0.6 %collective-permute-done.3 = f32[16,128]{1,0:T(8,128)S(1)} collective-permute-done((f32[16,128]{1,0:T(8,128)S(1)}, f32[16,128]{1,0:T(8,128)S(1)}, u32[]{:S(2)}, u32[]{:S(2)}) %collective-permute-start.3) | collective-permute-done | bytes 8224 | tf_op jit(solution)/shard_map/ppermute | solution.py:585
  13.5 0.6 %collective-permute-start.5 = (f32[16,128]{1,0:T(8,128)S(1)}, f32[16,128]{1,0:T(8,128)S(1)}, u32[]{:S(2)}, u32[]{:S(2)}) collective-permute-start(f32[16,128]{1,0:T(8,128)S(1)} %collective-permute-done.3), channel_id=1, source_target_pairs={{0,2},{1,3},{2,0},{3,1},{4,6},{5,7},{6,4},{7,5},{8,10},{9,11},{10,... | collective-permute-start | bytes 24584 | tf_op jit(solution)/shard_map/ppermute | solution.py:585
  14.1 0.0 collective-permute-done.6.from_outer
  14.1 0.5 %shard_map.89 = (f32[16,1024]{1,0:T(8,128)S(1)}, f32[16,1024]{1,0:T(8,128)S(1)}, f32[48,1024]{1,0:T(8,128)S(1)}, bf16[48,1024]{1,0:T(8,128)(2,1)S(1)}, f32[1,128...) custom-call(f32[16,1024]{1,0:T(8,128)S(1)} %get-tuple-element.61.image.image_in, ...), custom_call_target="tpu_custom_call" | custom-call | flops 167772160 | bytes 2327040 | tf_op jit(solution)/shard_map/pallas_call | solution.py:563
  14.6 1.6 %collective-permute-done.4 = f32[16,128]{1,0:T(8,128)S(1)} collective-permute-done((f32[16,128]{1,0:T(8,128)S(1)}, f32[16,128]{1,0:T(8,128)S(1)}, u32[]{:S(2)}, u32[]{:S(2)}) %collective-permute-start.4) | collective-permute-done | bytes 8224 | tf_op jit(solution)/shard_map/ppermute | solution.py:585
  16.2 0.0 collective-permute-done.5
  16.3 1.4 %collective-permute-start.7 = (f32[40,128]{1,0:T(8,128)S(1)}, f32[40,128]{1,0:T(8,128)S(1)}, u32[]{:S(2)}, u32[]{:S(2)}) collective-permute-start(f32[40,128]{1,0:T(8,128)S(1)} %constant_dynamic-update-slice_fusion), channel_id=1, source_target_pairs={{0,10},{1,11},{2,8},{3,9},{4,14},{5,15},{6,12},{7,13},{8,2},{9,3},... | collective-permute-start | bytes 61448 | tf_op jit(solution)/shard_map/ppermute | solution.py:585
  17.6 0.4 collective-permute-start.9
  18.0 0.7 %collective-permute-start.10 = (f32[72,512]{1,0:T(8,128)S(1)}, f32[72,512]{1,0:T(8,128)S(1)}, u32[]{:S(2)}, u32[]{:S(2)}) collective-permute-start(f32[72,512]{1,0:T(8,128)S(1)} %get-tuple-element.73), channel_id=1, source_target_pairs={{0,1},{1,0},{2,4},{3,5},{4,2},{5,3},{6,8},{7,9},{8,6},{9,7},{10,12... | collective-permute-start | bytes 442376 | tf_op jit(solution)/shard_map/ppermute | solution.py:585
  18.7 0.8 %collective-permute-done.7 = f32[40,128]{1,0:T(8,128)S(1)} collective-permute-done((f32[40,128]{1,0:T(8,128)S(1)}, f32[40,128]{1,0:T(8,128)S(1)}, u32[]{:S(2)}, u32[]{:S(2)}) %collective-permute-start.7) | collective-permute-done | bytes 20512 | tf_op jit(solution)/shard_map/ppermute | solution.py:585
  19.6 2.4 %collective-permute-start.8 = (f32[72,128]{1,0:T(8,128)S(1)}, f32[72,128]{1,0:T(8,128)S(1)}, u32[]{:S(2)}, u32[]{:S(2)}) collective-permute-start(f32[72,128]{1,0:T(8,128)S(1)} %pad_maximum_fusion.tiles.maps), channel_id=1, source_target_pairs={{0,18},{1,19},{2,16},{3,17},{4,22},{5,23},{6,20},{7,21},{8,26},{9,... | collective-permute-start | bytes 110600 | tf_op jit(solution)/shard_map/ppermute | solution.py:585
  21.9 0.0 copy-done
  21.9 0.3 shard_map.91
  22.3 0.5 %shard_map.90.left = f32[16,896]{1,0:T(8,128)S(1)} custom-call(f32[72,128]{1,0:T(8,128)S(1)} %pad_maximum_fusion.tiles.maps, f32[72,128]{1,0:T(8,128)S(1)} %pad_maximum_fusion.tiles.maps), custom_call_target="tpu_custom_call" | custom-call | flops 33554432 | bytes 73728 | tf_op jit(solution)/shard_map/pallas_call | solution.py:563
  22.7 1.3 %collective-permute-done.8.right.maps = f32[72,128]{1,0:T(8,128)S(1)} collective-permute-done((f32[72,128]{1,0:T(8,128)S(1)}, f32[72,128]{1,0:T(8,128)S(1)}, u32[]{:S(2)}, u32[]{:S(2)}) %collective-permute-start.8) | collective-permute-done | bytes 36896 | tf_op jit(solution)/shard_map/ppermute | solution.py:585
  24.0 0.0 collective-permute-done.9.from_inner
  24.0 0.0 collective-permute-done.10.from_outer
  24.0 2.7 %shard_map.92 = (f32[16,768]{1,0:T(8,128)S(1)}, f32[16,1024]{1,0:T(8,128)S(1)}, f32[16,1024]{1,0:T(8,128)S(1)}, f32[16,1024]{1,0:T(8,128)S(1)}, f32[16,1024]{1,0...) custom-call(f32[16,896]{1,0:T(8,128)S(1)} %shard_map.90.left, ...), custom_call_target="tpu_custom_call" | custom-call | flops 33554432 | bytes 5530112 | tf_op jit(solution)/shard_map/pallas_call | solution.py:563
  26.7 0.2 collective-permute-start.11
  26.9 1.1 %collective-permute-done.11.got = f32[16,640]{1,0:T(8,128)S(1)} collective-permute-done((f32[16,640]{1,0:T(8,128)S(1)}, f32[16,640]{1,0:T(8,128)S(1)}, u32[]{:S(2)}, u32[]{:S(2)}) %collective-permute-start.11) | collective-permute-done | bytes 40992 | tf_op jit(solution)/shard_map/ppermute | solution.py:585
  28.0 1.1 %collective-permute-start.12 = (f32[16,128]{1,0:T(8,128)S(1)}, f32[16,128]{1,0:T(8,128)S(1)}, u32[]{:S(2)}, u32[]{:S(2)}) collective-permute-start(f32[16,128]{1,0:T(8,128)S(1)} %slice_add_fusion), channel_id=1, source_target_pairs={{0,3},{1,2},{2,4},{3,5},{4,7},{5,6},{6,0},{7,1},{8,11},{9,10},{10,... | collective-permute-start | bytes 24584 | tf_op jit(solution)/shard_map/ppermute | solution.py:585
  29.1 1.2 %collective-permute-start.13 = (f32[16,128]{1,0:T(8,128)S(1)}, f32[16,128]{1,0:T(8,128)S(1)}, u32[]{:S(2)}, u32[]{:S(2)}) collective-permute-start(f32[16,128]{1,0:T(8,128)S(1)} %slice_add_fusion), channel_id=1, source_target_pairs={{0,7},{1,6},{2,5},{3,4},{4,3},{5,2},{6,1},{7,0},{8,15},{9,14},{10,... | collective-permute-start | bytes 24584 | tf_op jit(solution)/shard_map/ppermute | solution.py:585
  30.4 0.7 %collective-permute-done.12 = f32[16,128]{1,0:T(8,128)S(1)} collective-permute-done((f32[16,128]{1,0:T(8,128)S(1)}, f32[16,128]{1,0:T(8,128)S(1)}, u32[]{:S(2)}, u32[]{:S(2)}) %collective-permute-start.12) | collective-permute-done | bytes 8224 | tf_op jit(solution)/shard_map/ppermute | solution.py:585
  31.1 0.2 collective-permute-start.14
  31.2 1.4 %collective-permute-start.16 = (f32[16,512]{1,0:T(8,128)S(1)}, f32[16,512]{1,0:T(8,128)S(1)}, u32[]{:S(2)}, u32[]{:S(2)}) collective-permute-start(f32[16,512]{1,0:T(8,128)S(1)} %get-tuple-element.85), channel_id=1, source_target_pairs={{0,1},{1,0},{2,4},{3,5},{4,2},{5,3},{6,8},{7,9},{8,6},{9,7},{10,12... | collective-permute-start | bytes 98312 | tf_op jit(solution)/shard_map/ppermute | solution.py:585
  32.6 0.5 %collective-permute-done.13 = f32[16,128]{1,0:T(8,128)S(1)} collective-permute-done((f32[16,128]{1,0:T(8,128)S(1)}, f32[16,128]{1,0:T(8,128)S(1)}, u32[]{:S(2)}, u32[]{:S(2)}) %collective-permute-start.13) | collective-permute-done | bytes 8224 | tf_op jit(solution)/shard_map/ppermute | solution.py:585
  33.1 0.0 collective-permute-done.14
  33.2 1.6 %collective-permute-start.15 = (f32[40,128]{1,0:T(8,128)S(1)}, f32[40,128]{1,0:T(8,128)S(1)}, u32[]{:S(2)}, u32[]{:S(2)}) collective-permute-start(f32[40,128]{1,0:T(8,128)S(1)} %constant_dynamic-update-slice_fusion.5), channel_id=1, source_target_pairs={{0,10},{1,11},{2,8},{3,9},{4,14},{5,15},{6,12},{7,13},{8,2},{9,3},... | collective-permute-start | bytes 61448 | tf_op jit(solution)/shard_map/ppermute | solution.py:585
  34.8 0.3 collective-permute-done.16.from_outer
  35.2 0.2 shard_map.93
  35.4 1.1 %collective-permute-done.15 = f32[40,128]{1,0:T(8,128)S(1)} collective-permute-done((f32[40,128]{1,0:T(8,128)S(1)}, f32[40,128]{1,0:T(8,128)S(1)}, u32[]{:S(2)}, u32[]{:S(2)}) %collective-permute-start.15) | collective-permute-done | bytes 20512 | tf_op jit(solution)/shard_map/ppermute | solution.py:585
  36.5 2.3 %collective-permute-start.17 = (f32[72,128]{1,0:T(8,128)S(1)}, f32[72,128]{1,0:T(8,128)S(1)}, u32[]{:S(2)}, u32[]{:S(2)}) collective-permute-start(f32[72,128]{1,0:T(8,128)S(1)} %constant_dynamic-update-slice_fusion.10.tiles), channel_id=1, source_target_pairs={{0,18},{1,19},{2,16},{3,17},{4,22},{5,23},{6,20},{7,21},{8,26},{9,... | collective-permute-start | bytes 110600 | tf_op jit(solution)/shard_map/ppermute | solution.py:585
  38.8 0.5 %shard_map.94.left = f32[16,896]{1,0:T(8,128)S(1)} custom-call(f32[72,128]{1,0:T(8,128)S(1)} %constant_dynamic-update-slice_fusion.10.tiles, f32[72,128]{1,0:T(8,128)S(1)} %pad_maximum_fusion.tiles.maps), custom_call_target="tpu_custom_call" | custom-call | flops 33554432 | bytes 73728 | tf_op jit(solution)/shard_map/pallas_call | solution.py:563
  39.3 1.5 %collective-permute-done.17.right = f32[72,128]{1,0:T(8,128)S(1)} collective-permute-done((f32[72,128]{1,0:T(8,128)S(1)}, f32[72,128]{1,0:T(8,128)S(1)}, u32[]{:S(2)}, u32[]{:S(2)}) %collective-permute-start.17) | collective-permute-done | bytes 36896 | tf_op jit(solution)/shard_map/ppermute | solution.py:585
  40.8 2.7 %shard_map.95 = (f32[1,16,1024]{2,1,0:T(8,128)}, f32[1,16,1024]{2,1,0:T(8,128)}) custom-call(f32[16,896]{1,0:T(8,128)S(1)} %shard_map.94.left, f32[72,128]{1,0:T(8,128)S(1)} %collective-permute-done.17.right, f32[72,128]{1,0:T(8,128)S(1)} %collective-permute-done.8.right.maps, f32[16,1024]{1,0:T(8,128)S(1)} %get-tuple-element.90.part, ...), custom_call_target="tpu_custom_call" | custom-call | flops 33554432 | bytes 3043840 | tf_op jit(solution)/shard_map/pallas_call | solution.py:563
  (22 shorter events, 0.1 us)
Async XLA Ops:
  2.4 4.7 %collective-permute-start = (f32[16,512]{1,0:T(8,128)S(1)}, f32[16,512]{1,0:T(8,128)S(1)}, u32[]{:S(2)}, u32[]{:S(2)}) collective-permute-start(f32[16,512]{1,0:T(8,128)S(1)} %get-tuple-element.50), channel_id=1, source_target_pairs={{0,2},{1,3},{2,0},{3,1},{4,6},{5,7},{6,4},{7,5},{8,10},{9,11},{10,... | collective-permute-start | bytes 98312 | tf_op jit(solution)/shard_map/ppermute | solution.py:585
  3.0 4.5 %collective-permute-start.1 = (f32[16,512]{1,0:T(8,128)S(1)}, f32[16,512]{1,0:T(8,128)S(1)}, u32[]{:S(2)}, u32[]{:S(2)}) collective-permute-start(f32[16,512]{1,0:T(8,128)S(1)} %get-tuple-element.51), channel_id=1, source_target_pairs={{0,1},{1,0},{2,4},{3,5},{4,2},{5,3},{6,8},{7,9},{8,6},{9,7},{10,12... | collective-permute-start | bytes 98312 | tf_op jit(solution)/shard_map/ppermute | solution.py:585
  7.4 14.5 %copy-start = (f32[768,768]{1,0:T(8,128)S(1)}, f32[768,768]{1,0:T(8,128)}, u32[]{:S(2)}) copy-start(f32[768,768]{1,0:T(8,128)} %coarse.1) | copy-start | bytes 7077892
  8.1 2.2 %collective-permute-start.2 = (f32[16,1152]{1,0:T(8,128)S(1)}, f32[16,1152]{1,0:T(8,128)S(1)}, u32[]{:S(2)}, u32[]{:S(2)}) collective-permute-start(f32[16,1152]{1,0:T(8,128)S(1)} %get-tuple-element.60), channel_id=1, source_target_pairs={{0,2},{1,3},{2,0},{3,1},{4,6},{5,7},{6,4},{7,5},{8,10},{9,11},{10,... | collective-permute-start | bytes 221192 | tf_op jit(solution)/shard_map/ppermute | solution.py:585
  8.2 5.9 %collective-permute-start.6 = (f32[16,1024]{1,0:T(8,128)S(1)}, f32[16,1024]{1,0:T(8,128)S(1)}, u32[]{:S(2)}, u32[]{:S(2)}) collective-permute-start(f32[16,1024]{1,0:T(8,128)S(1)} %get-tuple-element.62), channel_id=1, source_target_pairs={{0,1},{1,0},{2,4},{3,5},{4,2},{5,3},{6,8},{7,9},{8,6},{9,7},{10,12... | collective-permute-start | bytes 196616 | tf_op jit(solution)/shard_map/ppermute | solution.py:585
  10.3 3.2 %collective-permute-start.3 = (f32[16,128]{1,0:T(8,128)S(1)}, f32[16,128]{1,0:T(8,128)S(1)}, u32[]{:S(2)}, u32[]{:S(2)}) collective-permute-start(f32[16,128]{1,0:T(8,128)S(1)} %slice_add_fusion.1), channel_id=1, source_target_pairs={{0,3},{1,2},{2,4},{3,5},{4,7},{5,6},{6,0},{7,1},{8,11},{9,10},{10,... | collective-permute-start | bytes 24584 | tf_op jit(solution)/shard_map/ppermute | solution.py:585
  12.2 4.1 %collective-permute-start.4 = (f32[16,128]{1,0:T(8,128)S(1)}, f32[16,128]{1,0:T(8,128)S(1)}, u32[]{:S(2)}, u32[]{:S(2)}) collective-permute-start(f32[16,128]{1,0:T(8,128)S(1)} %slice_add_fusion.1), channel_id=1, source_target_pairs={{0,7},{1,6},{2,5},{3,4},{4,3},{5,2},{6,1},{7,0},{8,15},{9,14},{10,... | collective-permute-start | bytes 24584 | tf_op jit(solution)/shard_map/ppermute | solution.py:585
  13.5 2.7 %collective-permute-start.5 = (f32[16,128]{1,0:T(8,128)S(1)}, f32[16,128]{1,0:T(8,128)S(1)}, u32[]{:S(2)}, u32[]{:S(2)}) collective-permute-start(f32[16,128]{1,0:T(8,128)S(1)} %collective-permute-done.3), channel_id=1, source_target_pairs={{0,2},{1,3},{2,0},{3,1},{4,6},{5,7},{6,4},{7,5},{8,10},{9,11},{10,... | collective-permute-start | bytes 24584 | tf_op jit(solution)/shard_map/ppermute | solution.py:585
  16.3 3.3 %collective-permute-start.7 = (f32[40,128]{1,0:T(8,128)S(1)}, f32[40,128]{1,0:T(8,128)S(1)}, u32[]{:S(2)}, u32[]{:S(2)}) collective-permute-start(f32[40,128]{1,0:T(8,128)S(1)} %constant_dynamic-update-slice_fusion), channel_id=1, source_target_pairs={{0,10},{1,11},{2,8},{3,9},{4,14},{5,15},{6,12},{7,13},{8,2},{9,3},... | collective-permute-start | bytes 61448 | tf_op jit(solution)/shard_map/ppermute | solution.py:585
  17.6 6.4 %collective-permute-start.9 = (f32[72,512]{1,0:T(8,128)S(1)}, f32[72,512]{1,0:T(8,128)S(1)}, u32[]{:S(2)}, u32[]{:S(2)}) collective-permute-start(f32[72,512]{1,0:T(8,128)S(1)} %get-tuple-element.72), channel_id=1, source_target_pairs={{0,2},{1,3},{2,0},{3,1},{4,6},{5,7},{6,4},{7,5},{8,10},{9,11},{10,... | collective-permute-start | bytes 442376 | tf_op jit(solution)/shard_map/ppermute | solution.py:585
  18.0 6.0 %collective-permute-start.10 = (f32[72,512]{1,0:T(8,128)S(1)}, f32[72,512]{1,0:T(8,128)S(1)}, u32[]{:S(2)}, u32[]{:S(2)}) collective-permute-start(f32[72,512]{1,0:T(8,128)S(1)} %get-tuple-element.73), channel_id=1, source_target_pairs={{0,1},{1,0},{2,4},{3,5},{4,2},{5,3},{6,8},{7,9},{8,6},{9,7},{10,12... | collective-permute-start | bytes 442376 | tf_op jit(solution)/shard_map/ppermute | solution.py:585
  19.6 4.4 %collective-permute-start.8 = (f32[72,128]{1,0:T(8,128)S(1)}, f32[72,128]{1,0:T(8,128)S(1)}, u32[]{:S(2)}, u32[]{:S(2)}) collective-permute-start(f32[72,128]{1,0:T(8,128)S(1)} %pad_maximum_fusion.tiles.maps), channel_id=1, source_target_pairs={{0,18},{1,19},{2,16},{3,17},{4,22},{5,23},{6,20},{7,21},{8,26},{9,... | collective-permute-start | bytes 110600 | tf_op jit(solution)/shard_map/ppermute | solution.py:585
  26.7 1.3 %collective-permute-start.11 = (f32[16,640]{1,0:T(8,128)S(1)}, f32[16,640]{1,0:T(8,128)S(1)}, u32[]{:S(2)}, u32[]{:S(2)}) collective-permute-start(f32[16,640]{1,0:T(8,128)S(1)} %get-tuple-element.83), channel_id=1, source_target_pairs={{0,2},{1,3},{2,0},{3,1},{4,6},{5,7},{6,4},{7,5},{8,10},{9,11},{10,... | collective-permute-start | bytes 122888 | tf_op jit(solution)/shard_map/ppermute | solution.py:585
  28.0 3.1 %collective-permute-start.12 = (f32[16,128]{1,0:T(8,128)S(1)}, f32[16,128]{1,0:T(8,128)S(1)}, u32[]{:S(2)}, u32[]{:S(2)}) collective-permute-start(f32[16,128]{1,0:T(8,128)S(1)} %slice_add_fusion), channel_id=1, source_target_pairs={{0,3},{1,2},{2,4},{3,5},{4,7},{5,6},{6,0},{7,1},{8,11},{9,10},{10,... | collective-permute-start | bytes 24584 | tf_op jit(solution)/shard_map/ppermute | solution.py:585
  29.1 4.0 %collective-permute-start.13 = (f32[16,128]{1,0:T(8,128)S(1)}, f32[16,128]{1,0:T(8,128)S(1)}, u32[]{:S(2)}, u32[]{:S(2)}) collective-permute-start(f32[16,128]{1,0:T(8,128)S(1)} %slice_add_fusion), channel_id=1, source_target_pairs={{0,7},{1,6},{2,5},{3,4},{4,3},{5,2},{6,1},{7,0},{8,15},{9,14},{10,... | collective-permute-start | bytes 24584 | tf_op jit(solution)/shard_map/ppermute | solution.py:585
  31.1 2.0 %collective-permute-start.14 = (f32[16,128]{1,0:T(8,128)S(1)}, f32[16,128]{1,0:T(8,128)S(1)}, u32[]{:S(2)}, u32[]{:S(2)}) collective-permute-start(f32[16,128]{1,0:T(8,128)S(1)} %collective-permute-done.12), channel_id=1, source_target_pairs={{0,2},{1,3},{2,0},{3,1},{4,6},{5,7},{6,4},{7,5},{8,10},{9,11},{10,... | collective-permute-start | bytes 24584 | tf_op jit(solution)/shard_map/ppermute | solution.py:585
  31.2 3.9 %collective-permute-start.16 = (f32[16,512]{1,0:T(8,128)S(1)}, f32[16,512]{1,0:T(8,128)S(1)}, u32[]{:S(2)}, u32[]{:S(2)}) collective-permute-start(f32[16,512]{1,0:T(8,128)S(1)} %get-tuple-element.85), channel_id=1, source_target_pairs={{0,1},{1,0},{2,4},{3,5},{4,2},{5,3},{6,8},{7,9},{8,6},{9,7},{10,12... | collective-permute-start | bytes 98312 | tf_op jit(solution)/shard_map/ppermute | solution.py:585
  33.2 3.3 %collective-permute-start.15 = (f32[40,128]{1,0:T(8,128)S(1)}, f32[40,128]{1,0:T(8,128)S(1)}, u32[]{:S(2)}, u32[]{:S(2)}) collective-permute-start(f32[40,128]{1,0:T(8,128)S(1)} %constant_dynamic-update-slice_fusion.5), channel_id=1, source_target_pairs={{0,10},{1,11},{2,8},{3,9},{4,14},{5,15},{6,12},{7,13},{8,2},{9,3},... | collective-permute-start | bytes 61448 | tf_op jit(solution)/shard_map/ppermute | solution.py:585
  36.5 4.3 %collective-permute-start.17 = (f32[72,128]{1,0:T(8,128)S(1)}, f32[72,128]{1,0:T(8,128)S(1)}, u32[]{:S(2)}, u32[]{:S(2)}) collective-permute-start(f32[72,128]{1,0:T(8,128)S(1)} %constant_dynamic-update-slice_fusion.10.tiles), channel_id=1, source_target_pairs={{0,18},{1,19},{2,16},{3,17},{4,22},{5,23},{6,20},{7,21},{8,26},{9,... | collective-permute-start | bytes 110600 | tf_op jit(solution)/shard_map/ppermute | solution.py:585

commit v9 on v8

--- a/solution.py
+++ b/solution.py
@@ -84,7 +84,7 @@
         def across_target(chip, lane, grp):
             return place(chip ^ 1, lane ^ 1, grp ^ 1)
 
-        return [pairs_of(split_target), pairs_of(across_target)], True
+        return [pairs_of(across_target), pairs_of(split_target)], True
 
     todo = []
     for axis, size in (("grp", groups), ("blk", chips)):
@@ -617,7 +617,7 @@
                 result = (*(exchange(*sends) if sends else ()), *result)
             left = values
             terms = [permute(values, pairs) for pairs in turns]
-            right = united(terms + [permute(terms[0], inner)] * relayed)
+            right = united(terms + [permute(terms[-1], inner)] * relayed)
         known = known or (left, right)
         if left.shape[1] == TILE:
             left = densify(left, known[0])

time: 43.7 us -> 43.7 us (level)
  no operation moved by 1% of the time
where the time goes in v9:
time: 43.7 us; the launch traced here: 43.6 us
  starting transfers between devices  21.4 us (49%)
  Pallas kernels  11.4 us (26%)
  waiting for transfers between devices  9.84 us (23%)
  between operations  0.79 us (2%)
    ppermute x18, starting transfers between devices, permute(): return lax.ppermute(values, AXES, pairs)  21.4 us
    pallas_call x10, Pallas kernels, call(): pl.pallas_call(body, out_shape=shapes, in_specs=specs or [VMEM] * len(arg...  11.4 us
    ppermute x18, waiting for transfers between devices, permute(): return lax.ppermute(values, AXES, pairs)  9.84 us
  transfers between devices with their start and end apart: 18, of which 11 were waited for; matrix products, arithmetic and copies ran while one was open for 0% of the time, Pallas kernels for 8%

profile of v9, /device:TPU:0, one launch (start us, length us, event | category | flops | bytes accessed | tf_op | source)
XLA Modules:
  0.0 43.6 jit_solution(2366593623235218307)
XLA Ops:
  0.6 1.8 %shard_map.86 = (f32[16,1024]{1,0:T(8,128)S(1)}, f32[16,512]{1,0:T(8,128)S(1)}, f32[16,512]{1,0:T(8,128)S(1)}, f32[16,1024]{1,0:T(8,128)S(1)}, f32[1,1024]{1,0:T(1,128)S(1)}, /*index=5*/bf16[8,128,1024]{2,1,0:T(8,128)(2,1)S(1)}) custom-call(f32[1,16,1024]{2,1,0:T(8,128)} %rhs.1, s32[1,1024]{1,0:T(1,128)} %signs.1, bf16[1,1024,1024]{2,1,0:T(8,128)(2,1)} %blocks.2), custom_call_target="tpu_custom_call" | custom-call | flops 33554432 | bytes 2166784 | tf_op jit(solution)/shard_map/pallas_call | solution.py:563
  2.4 0.5 %collective-permute-start = (f32[16,512]{1,0:T(8,128)S(1)}, f32[16,512]{1,0:T(8,128)S(1)}, u32[]{:S(2)}, u32[]{:S(2)}) collective-permute-start(f32[16,512]{1,0:T(8,128)S(1)} %get-tuple-element.50), channel_id=1, source_target_pairs={{0,2},{1,3},{2,0},{3,1},{4,6},{5,7},{6,4},{7,5},{8,10},{9,11},{10,... | collective-permute-start | bytes 98312 | tf_op jit(solution)/shard_map/ppermute | solution.py:585
  3.0 2.6 %collective-permute-start.1 = (f32[16,512]{1,0:T(8,128)S(1)}, f32[16,512]{1,0:T(8,128)S(1)}, u32[]{:S(2)}, u32[]{:S(2)}) collective-permute-start(f32[16,512]{1,0:T(8,128)S(1)} %get-tuple-element.51), channel_id=1, source_target_pairs={{0,1},{1,0},{2,4},{3,5},{4,2},{5,3},{6,8},{7,9},{8,6},{9,7},{10,12... | collective-permute-start | bytes 98312 | tf_op jit(solution)/shard_map/ppermute | solution.py:585
  5.5 1.6 %shard_map.87 = (bf16[1024,1024]{1,0:T(8,128)(2,1)S(1)}, bf16[24,512]{1,0:T(8,128)(2,1)S(1)}, f32[1,128]{1,0:T(1,128)S(1)}, f32[16,512]{1,0:T(8,128)S(1)}, f32[16,512]{1,0:T(8,128)S(1)}) custom-call(bf16[1,1024,1024]{2,1,0:T(8,128)(2,1)} %blocks.3, bf16[1,24,512]{2,1,0:T(8,128)(2,1)} %coupling.1, s32[1,24]{1,0:T(1,128)} %corner_map.1, ...), custom_call_target="tpu_custom_call" | custom-call | bytes 2125920 | tf_op jit(solution)/shard_map/pallas_call | solution.py:563
  7.1 0.0 collective-permute-done.from_inner
  7.2 0.3 collective-permute-done.1.from_outer
  7.4 0.0 copy-start
  7.4 0.6 %shard_map.88 = (f32[16,1024]{1,0:T(8,128)S(1)}, f32[16,1024]{1,0:T(8,128)S(1)}, f32[16,128]{1,0:T(8,128)S(1)}, f32[16,1152]{1,0:T(8,128)S(1)}, f32[16,1024]{1,0:T(8,128)S(1)}) custom-call(f32[16,1024]{1,0:T(8,128)S(1)} %get-tuple-element.49.product, f32[16,512]{1,0:T(8,128)S(1)} %collective-permute-done.from_inner, ...), custom_call_target="tpu_custom_call" | custom-call | flops 33554432 | bytes 2384384 | tf_op jit(solution)/shard_map/pallas_call | solution.py:563
  8.1 0.2 collective-permute-start.2
  8.2 2.0 %collective-permute-start.6 = (f32[16,1024]{1,0:T(8,128)S(1)}, f32[16,1024]{1,0:T(8,128)S(1)}, u32[]{:S(2)}, u32[]{:S(2)}) collective-permute-start(f32[16,1024]{1,0:T(8,128)S(1)} %get-tuple-element.62), channel_id=1, source_target_pairs={{0,1},{1,0},{2,4},{3,5},{4,2},{5,3},{6,8},{7,9},{8,6},{9,7},{10,12... | collective-permute-start | bytes 196616 | tf_op jit(solution)/shard_map/ppermute | solution.py:585
  10.3 0.0 collective-permute-done.2.got
  10.3 1.9 %collective-permute-start.4 = (f32[16,128]{1,0:T(8,128)S(1)}, f32[16,128]{1,0:T(8,128)S(1)}, u32[]{:S(2)}, u32[]{:S(2)}) collective-permute-start(f32[16,128]{1,0:T(8,128)S(1)} %slice_add_fusion.1), channel_id=1, source_target_pairs={{0,3},{1,2},{2,4},{3,5},{4,7},{5,6},{6,0},{7,1},{8,11},{9,10},{10,... | collective-permute-start | bytes 24584 | tf_op jit(solution)/shard_map/ppermute | solution.py:585
  12.2 0.7 %collective-permute-start.3 = (f32[16,128]{1,0:T(8,128)S(1)}, f32[16,128]{1,0:T(8,128)S(1)}, u32[]{:S(2)}, u32[]{:S(2)}) collective-permute-start(f32[16,128]{1,0:T(8,128)S(1)} %slice_add_fusion.1), channel_id=1, source_target_pairs={{0,7},{1,6},{2,5},{3,4},{4,3},{5,2},{6,1},{7,0},{8,15},{9,14},{10,... | collective-permute-start | bytes 24584 | tf_op jit(solution)/shard_map/ppermute | solution.py:585
  12.9 0.6 %collective-permute-done.4 = f32[16,128]{1,0:T(8,128)S(1)} collective-permute-done((f32[16,128]{1,0:T(8,128)S(1)}, f32[16,128]{1,0:T(8,128)S(1)}, u32[]{:S(2)}, u32[]{:S(2)}) %collective-permute-start.4) | collective-permute-done | bytes 8224 | tf_op jit(solution)/shard_map/ppermute | solution.py:585
  13.5 0.6 %collective-permute-start.5 = (f32[16,128]{1,0:T(8,128)S(1)}, f32[16,128]{1,0:T(8,128)S(1)}, u32[]{:S(2)}, u32[]{:S(2)}) collective-permute-start(f32[16,128]{1,0:T(8,128)S(1)} %collective-permute-done.4), channel_id=1, source_target_pairs={{0,2},{1,3},{2,0},{3,1},{4,6},{5,7},{6,4},{7,5},{8,10},{9,11},{10,... | collective-permute-start | bytes 24584 | tf_op jit(solution)/shard_map/ppermute | solution.py:585
  14.1 0.0 collective-permute-done.6.from_outer
  14.1 0.5 %shard_map.89 = (f32[16,1024]{1,0:T(8,128)S(1)}, f32[16,1024]{1,0:T(8,128)S(1)}, f32[48,1024]{1,0:T(8,128)S(1)}, bf16[48,1024]{1,0:T(8,128)(2,1)S(1)}, f32[1,128...) custom-call(f32[16,1024]{1,0:T(8,128)S(1)} %get-tuple-element.61.image.image_in, ...), custom_call_target="tpu_custom_call" | custom-call | flops 167772160 | bytes 2327040 | tf_op jit(solution)/shard_map/pallas_call | solution.py:563
  14.6 1.6 %collective-permute-done.3 = f32[16,128]{1,0:T(8,128)S(1)} collective-permute-done((f32[16,128]{1,0:T(8,128)S(1)}, f32[16,128]{1,0:T(8,128)S(1)}, u32[]{:S(2)}, u32[]{:S(2)}) %collective-permute-start.3) | collective-permute-done | bytes 8224 | tf_op jit(solution)/shard_map/ppermute | solution.py:585
  16.2 0.0 collective-permute-done.5
  16.3 1.4 %collective-permute-start.7 = (f32[40,128]{1,0:T(8,128)S(1)}, f32[40,128]{1,0:T(8,128)S(1)}, u32[]{:S(2)}, u32[]{:S(2)}) collective-permute-start(f32[40,128]{1,0:T(8,128)S(1)} %constant_dynamic-update-slice_fusion), channel_id=1, source_target_pairs={{0,10},{1,11},{2,8},{3,9},{4,14},{5,15},{6,12},{7,13},{8,2},{9,3},... | collective-permute-start | bytes 61448 | tf_op jit(solution)/shard_map/ppermute | solution.py:585
  17.6 0.4 collective-permute-start.9
  18.0 0.7 %collective-permute-start.10 = (f32[72,512]{1,0:T(8,128)S(1)}, f32[72,512]{1,0:T(8,128)S(1)}, u32[]{:S(2)}, u32[]{:S(2)}) collective-permute-start(f32[72,512]{1,0:T(8,128)S(1)} %get-tuple-element.73), channel_id=1, source_target_pairs={{0,1},{1,0},{2,4},{3,5},{4,2},{5,3},{6,8},{7,9},{8,6},{9,7},{10,12... | collective-permute-start | bytes 442376 | tf_op jit(solution)/shard_map/ppermute | solution.py:585
  18.7 0.8 %collective-permute-done.7 = f32[40,128]{1,0:T(8,128)S(1)} collective-permute-done((f32[40,128]{1,0:T(8,128)S(1)}, f32[40,128]{1,0:T(8,128)S(1)}, u32[]{:S(2)}, u32[]{:S(2)}) %collective-permute-start.7) | collective-permute-done | bytes 20512 | tf_op jit(solution)/shard_map/ppermute | solution.py:585
  19.6 2.4 %collective-permute-start.8 = (f32[72,128]{1,0:T(8,128)S(1)}, f32[72,128]{1,0:T(8,128)S(1)}, u32[]{:S(2)}, u32[]{:S(2)}) collective-permute-start(f32[72,128]{1,0:T(8,128)S(1)} %pad_maximum_fusion.tiles.maps), channel_id=1, source_target_pairs={{0,18},{1,19},{2,16},{3,17},{4,22},{5,23},{6,20},{7,21},{8,26},{9,... | collective-permute-start | bytes 110600 | tf_op jit(solution)/shard_map/ppermute | solution.py:585
  21.9 0.0 copy-done
  21.9 0.3 shard_map.91
  22.3 0.5 %shard_map.90.left = f32[16,896]{1,0:T(8,128)S(1)} custom-call(f32[72,128]{1,0:T(8,128)S(1)} %pad_maximum_fusion.tiles.maps, f32[72,128]{1,0:T(8,128)S(1)} %pad_maximum_fusion.tiles.maps), custom_call_target="tpu_custom_call" | custom-call | flops 33554432 | bytes 73728 | tf_op jit(solution)/shard_map/pallas_call | solution.py:563
  22.7 1.3 %collective-permute-done.8.right.maps = f32[72,128]{1,0:T(8,128)S(1)} collective-permute-done((f32[72,128]{1,0:T(8,128)S(1)}, f32[72,128]{1,0:T(8,128)S(1)}, u32[]{:S(2)}, u32[]{:S(2)}) %collective-permute-start.8) | collective-permute-done | bytes 36896 | tf_op jit(solution)/shard_map/ppermute | solution.py:585
  24.0 0.0 collective-permute-done.9.from_inner
  24.0 0.0 collective-permute-done.10.from_outer
  24.0 2.7 %shard_map.92 = (f32[16,768]{1,0:T(8,128)S(1)}, f32[16,1024]{1,0:T(8,128)S(1)}, f32[16,1024]{1,0:T(8,128)S(1)}, f32[16,1024]{1,0:T(8,128)S(1)}, f32[16,1024]{1,0...) custom-call(f32[16,896]{1,0:T(8,128)S(1)} %shard_map.90.left, ...), custom_call_target="tpu_custom_call" | custom-call | flops 33554432 | bytes 5530112 | tf_op jit(solution)/shard_map/pallas_call | solution.py:563
  26.7 0.2 collective-permute-start.11
  26.9 1.1 %collective-permute-done.11.got = f32[16,640]{1,0:T(8,128)S(1)} collective-permute-done((f32[16,640]{1,0:T(8,128)S(1)}, f32[16,640]{1,0:T(8,128)S(1)}, u32[]{:S(2)}, u32[]{:S(2)}) %collective-permute-start.11) | collective-permute-done | bytes 40992 | tf_op jit(solution)/shard_map/ppermute | solution.py:585
  28.0 1.1 %collective-permute-start.13 = (f32[16,128]{1,0:T(8,128)S(1)}, f32[16,128]{1,0:T(8,128)S(1)}, u32[]{:S(2)}, u32[]{:S(2)}) collective-permute-start(f32[16,128]{1,0:T(8,128)S(1)} %slice_add_fusion), channel_id=1, source_target_pairs={{0,3},{1,2},{2,4},{3,5},{4,7},{5,6},{6,0},{7,1},{8,11},{9,10},{10,... | collective-permute-start | bytes 24584 | tf_op jit(solution)/shard_map/ppermute | solution.py:585
  29.1 1.2 %collective-permute-start.12 = (f32[16,128]{1,0:T(8,128)S(1)}, f32[16,128]{1,0:T(8,128)S(1)}, u32[]{:S(2)}, u32[]{:S(2)}) collective-permute-start(f32[16,128]{1,0:T(8,128)S(1)} %slice_add_fusion), channel_id=1, source_target_pairs={{0,7},{1,6},{2,5},{3,4},{4,3},{5,2},{6,1},{7,0},{8,15},{9,14},{10,... | collective-permute-start | bytes 24584 | tf_op jit(solution)/shard_map/ppermute | solution.py:585
  30.4 0.7 %collective-permute-done.13 = f32[16,128]{1,0:T(8,128)S(1)} collective-permute-done((f32[16,128]{1,0:T(8,128)S(1)}, f32[16,128]{1,0:T(8,128)S(1)}, u32[]{:S(2)}, u32[]{:S(2)}) %collective-permute-start.13) | collective-permute-done | bytes 8224 | tf_op jit(solution)/shard_map/ppermute | solution.py:585
  31.1 0.2 collective-permute-start.14
  31.2 1.4 %collective-permute-start.16 = (f32[16,512]{1,0:T(8,128)S(1)}, f32[16,512]{1,0:T(8,128)S(1)}, u32[]{:S(2)}, u32[]{:S(2)}) collective-permute-start(f32[16,512]{1,0:T(8,128)S(1)} %get-tuple-element.85), channel_id=1, source_target_pairs={{0,1},{1,0},{2,4},{3,5},{4,2},{5,3},{6,8},{7,9},{8,6},{9,7},{10,12... | collective-permute-start | bytes 98312 | tf_op jit(solution)/shard_map/ppermute | solution.py:585
  32.6 0.5 %collective-permute-done.12 = f32[16,128]{1,0:T(8,128)S(1)} collective-permute-done((f32[16,128]{1,0:T(8,128)S(1)}, f32[16,128]{1,0:T(8,128)S(1)}, u32[]{:S(2)}, u32[]{:S(2)}) %collective-permute-start.12) | collective-permute-done | bytes 8224 | tf_op jit(solution)/shard_map/ppermute | solution.py:585
  33.1 0.0 collective-permute-done.14
  33.2 1.6 %collective-permute-start.15 = (f32[40,128]{1,0:T(8,128)S(1)}, f32[40,128]{1,0:T(8,128)S(1)}, u32[]{:S(2)}, u32[]{:S(2)}) collective-permute-start(f32[40,128]{1,0:T(8,128)S(1)} %constant_dynamic-update-slice_fusion.5), channel_id=1, source_target_pairs={{0,10},{1,11},{2,8},{3,9},{4,14},{5,15},{6,12},{7,13},{8,2},{9,3},... | collective-permute-start | bytes 61448 | tf_op jit(solution)/shard_map/ppermute | solution.py:585
  34.8 0.3 collective-permute-done.16.from_outer
  35.2 0.2 shard_map.93
  35.4 1.1 %collective-permute-done.15 = f32[40,128]{1,0:T(8,128)S(1)} collective-permute-done((f32[40,128]{1,0:T(8,128)S(1)}, f32[40,128]{1,0:T(8,128)S(1)}, u32[]{:S(2)}, u32[]{:S(2)}) %collective-permute-start.15) | collective-permute-done | bytes 20512 | tf_op jit(solution)/shard_map/ppermute | solution.py:585
  36.5 2.3 %collective-permute-start.17 = (f32[72,128]{1,0:T(8,128)S(1)}, f32[72,128]{1,0:T(8,128)S(1)}, u32[]{:S(2)}, u32[]{:S(2)}) collective-permute-start(f32[72,128]{1,0:T(8,128)S(1)} %constant_dynamic-update-slice_fusion.10.tiles), channel_id=1, source_target_pairs={{0,18},{1,19},{2,16},{3,17},{4,22},{5,23},{6,20},{7,21},{8,26},{9,... | collective-permute-start | bytes 110600 | tf_op jit(solution)/shard_map/ppermute | solution.py:585
  38.8 0.5 %shard_map.94.left = f32[16,896]{1,0:T(8,128)S(1)} custom-call(f32[72,128]{1,0:T(8,128)S(1)} %constant_dynamic-update-slice_fusion.10.tiles, f32[72,128]{1,0:T(8,128)S(1)} %pad_maximum_fusion.tiles.maps), custom_call_target="tpu_custom_call" | custom-call | flops 33554432 | bytes 73728 | tf_op jit(solution)/shard_map/pallas_call | solution.py:563
  39.3 1.5 %collective-permute-done.17.right = f32[72,128]{1,0:T(8,128)S(1)} collective-permute-done((f32[72,128]{1,0:T(8,128)S(1)}, f32[72,128]{1,0:T(8,128)S(1)}, u32[]{:S(2)}, u32[]{:S(2)}) %collective-permute-start.17) | collective-permute-done | bytes 36896 | tf_op jit(solution)/shard_map/ppermute | solution.py:585
  40.8 2.7 %shard_map.95 = (f32[1,16,1024]{2,1,0:T(8,128)}, f32[1,16,1024]{2,1,0:T(8,128)}) custom-call(f32[16,896]{1,0:T(8,128)S(1)} %shard_map.94.left, f32[72,128]{1,0:T(8,128)S(1)} %collective-permute-done.17.right, f32[72,128]{1,0:T(8,128)S(1)} %collective-permute-done.8.right.maps, f32[16,1024]{1,0:T(8,128)S(1)} %get-tuple-element.90.part, ...), custom_call_target="tpu_custom_call" | custom-call | flops 33554432 | bytes 3043840 | tf_op jit(solution)/shard_map/pallas_call | solution.py:563
  (22 shorter events, 0.1 us)
Async XLA Ops:
  2.4 4.7 %collective-permute-start = (f32[16,512]{1,0:T(8,128)S(1)}, f32[16,512]{1,0:T(8,128)S(1)}, u32[]{:S(2)}, u32[]{:S(2)}) collective-permute-start(f32[16,512]{1,0:T(8,128)S(1)} %get-tuple-element.50), channel_id=1, source_target_pairs={{0,2},{1,3},{2,0},{3,1},{4,6},{5,7},{6,4},{7,5},{8,10},{9,11},{10,... | collective-permute-start | bytes 98312 | tf_op jit(solution)/shard_map/ppermute | solution.py:585
  3.0 4.5 %collective-permute-start.1 = (f32[16,512]{1,0:T(8,128)S(1)}, f32[16,512]{1,0:T(8,128)S(1)}, u32[]{:S(2)}, u32[]{:S(2)}) collective-permute-start(f32[16,512]{1,0:T(8,128)S(1)} %get-tuple-element.51), channel_id=1, source_target_pairs={{0,1},{1,0},{2,4},{3,5},{4,2},{5,3},{6,8},{7,9},{8,6},{9,7},{10,12... | collective-permute-start | bytes 98312 | tf_op jit(solution)/shard_map/ppermute | solution.py:585
  7.4 14.5 %copy-start = (f32[768,768]{1,0:T(8,128)S(1)}, f32[768,768]{1,0:T(8,128)}, u32[]{:S(2)}) copy-start(f32[768,768]{1,0:T(8,128)} %coarse.1) | copy-start | bytes 7077892
  8.1 2.2 %collective-permute-start.2 = (f32[16,1152]{1,0:T(8,128)S(1)}, f32[16,1152]{1,0:T(8,128)S(1)}, u32[]{:S(2)}, u32[]{:S(2)}) collective-permute-start(f32[16,1152]{1,0:T(8,128)S(1)} %get-tuple-element.60), channel_id=1, source_target_pairs={{0,2},{1,3},{2,0},{3,1},{4,6},{5,7},{6,4},{7,5},{8,10},{9,11},{10,... | collective-permute-start | bytes 221192 | tf_op jit(solution)/shard_map/ppermute | solution.py:585
  8.2 5.9 %collective-permute-start.6 = (f32[16,1024]{1,0:T(8,128)S(1)}, f32[16,1024]{1,0:T(8,128)S(1)}, u32[]{:S(2)}, u32[]{:S(2)}) collective-permute-start(f32[16,1024]{1,0:T(8,128)S(1)} %get-tuple-element.62), channel_id=1, source_target_pairs={{0,1},{1,0},{2,4},{3,5},{4,2},{5,3},{6,8},{7,9},{8,6},{9,7},{10,12... | collective-permute-start | bytes 196616 | tf_op jit(solution)/shard_map/ppermute | solution.py:585
  10.3 3.2 %collective-permute-start.4 = (f32[16,128]{1,0:T(8,128)S(1)}, f32[16,128]{1,0:T(8,128)S(1)}, u32[]{:S(2)}, u32[]{:S(2)}) collective-permute-start(f32[16,128]{1,0:T(8,128)S(1)} %slice_add_fusion.1), channel_id=1, source_target_pairs={{0,3},{1,2},{2,4},{3,5},{4,7},{5,6},{6,0},{7,1},{8,11},{9,10},{10,... | collective-permute-start | bytes 24584 | tf_op jit(solution)/shard_map/ppermute | solution.py:585
  12.2 4.1 %collective-permute-start.3 = (f32[16,128]{1,0:T(8,128)S(1)}, f32[16,128]{1,0:T(8,128)S(1)}, u32[]{:S(2)}, u32[]{:S(2)}) collective-permute-start(f32[16,128]{1,0:T(8,128)S(1)} %slice_add_fusion.1), channel_id=1, source_target_pairs={{0,7},{1,6},{2,5},{3,4},{4,3},{5,2},{6,1},{7,0},{8,15},{9,14},{10,... | collective-permute-start | bytes 24584 | tf_op jit(solution)/shard_map/ppermute | solution.py:585
  13.5 2.7 %collective-permute-start.5 = (f32[16,128]{1,0:T(8,128)S(1)}, f32[16,128]{1,0:T(8,128)S(1)}, u32[]{:S(2)}, u32[]{:S(2)}) collective-permute-start(f32[16,128]{1,0:T(8,128)S(1)} %collective-permute-done.4), channel_id=1, source_target_pairs={{0,2},{1,3},{2,0},{3,1},{4,6},{5,7},{6,4},{7,5},{8,10},{9,11},{10,... | collective-permute-start | bytes 24584 | tf_op jit(solution)/shard_map/ppermute | solution.py:585
  16.3 3.3 %collective-permute-start.7 = (f32[40,128]{1,0:T(8,128)S(1)}, f32[40,128]{1,0:T(8,128)S(1)}, u32[]{:S(2)}, u32[]{:S(2)}) collective-permute-start(f32[40,128]{1,0:T(8,128)S(1)} %constant_dynamic-update-slice_fusion), channel_id=1, source_target_pairs={{0,10},{1,11},{2,8},{3,9},{4,14},{5,15},{6,12},{7,13},{8,2},{9,3},... | collective-permute-start | bytes 61448 | tf_op jit(solution)/shard_map/ppermute | solution.py:585
  17.6 6.4 %collective-permute-start.9 = (f32[72,512]{1,0:T(8,128)S(1)}, f32[72,512]{1,0:T(8,128)S(1)}, u32[]{:S(2)}, u32[]{:S(2)}) collective-permute-start(f32[72,512]{1,0:T(8,128)S(1)} %get-tuple-element.72), channel_id=1, source_target_pairs={{0,2},{1,3},{2,0},{3,1},{4,6},{5,7},{6,4},{7,5},{8,10},{9,11},{10,... | collective-permute-start | bytes 442376 | tf_op jit(solution)/shard_map/ppermute | solution.py:585
  18.0 6.0 %collective-permute-start.10 = (f32[72,512]{1,0:T(8,128)S(1)}, f32[72,512]{1,0:T(8,128)S(1)}, u32[]{:S(2)}, u32[]{:S(2)}) collective-permute-start(f32[72,512]{1,0:T(8,128)S(1)} %get-tuple-element.73), channel_id=1, source_target_pairs={{0,1},{1,0},{2,4},{3,5},{4,2},{5,3},{6,8},{7,9},{8,6},{9,7},{10,12... | collective-permute-start | bytes 442376 | tf_op jit(solution)/shard_map/ppermute | solution.py:585
  19.6 4.4 %collective-permute-start.8 = (f32[72,128]{1,0:T(8,128)S(1)}, f32[72,128]{1,0:T(8,128)S(1)}, u32[]{:S(2)}, u32[]{:S(2)}) collective-permute-start(f32[72,128]{1,0:T(8,128)S(1)} %pad_maximum_fusion.tiles.maps), channel_id=1, source_target_pairs={{0,18},{1,19},{2,16},{3,17},{4,22},{5,23},{6,20},{7,21},{8,26},{9,... | collective-permute-start | bytes 110600 | tf_op jit(solution)/shard_map/ppermute | solution.py:585
  26.7 1.3 %collective-permute-start.11 = (f32[16,640]{1,0:T(8,128)S(1)}, f32[16,640]{1,0:T(8,128)S(1)}, u32[]{:S(2)}, u32[]{:S(2)}) collective-permute-start(f32[16,640]{1,0:T(8,128)S(1)} %get-tuple-element.83), channel_id=1, source_target_pairs={{0,2},{1,3},{2,0},{3,1},{4,6},{5,7},{6,4},{7,5},{8,10},{9,11},{10,... | collective-permute-start | bytes 122888 | tf_op jit(solution)/shard_map/ppermute | solution.py:585
  28.0 3.1 %collective-permute-start.13 = (f32[16,128]{1,0:T(8,128)S(1)}, f32[16,128]{1,0:T(8,128)S(1)}, u32[]{:S(2)}, u32[]{:S(2)}) collective-permute-start(f32[16,128]{1,0:T(8,128)S(1)} %slice_add_fusion), channel_id=1, source_target_pairs={{0,3},{1,2},{2,4},{3,5},{4,7},{5,6},{6,0},{7,1},{8,11},{9,10},{10,... | collective-permute-start | bytes 24584 | tf_op jit(solution)/shard_map/ppermute | solution.py:585
  29.1 4.0 %collective-permute-start.12 = (f32[16,128]{1,0:T(8,128)S(1)}, f32[16,128]{1,0:T(8,128)S(1)}, u32[]{:S(2)}, u32[]{:S(2)}) collective-permute-start(f32[16,128]{1,0:T(8,128)S(1)} %slice_add_fusion), channel_id=1, source_target_pairs={{0,7},{1,6},{2,5},{3,4},{4,3},{5,2},{6,1},{7,0},{8,15},{9,14},{10,... | collective-permute-start | bytes 24584 | tf_op jit(solution)/shard_map/ppermute | solution.py:585
  31.1 2.0 %collective-permute-start.14 = (f32[16,128]{1,0:T(8,128)S(1)}, f32[16,128]{1,0:T(8,128)S(1)}, u32[]{:S(2)}, u32[]{:S(2)}) collective-permute-start(f32[16,128]{1,0:T(8,128)S(1)} %collective-permute-done.13), channel_id=1, source_target_pairs={{0,2},{1,3},{2,0},{3,1},{4,6},{5,7},{6,4},{7,5},{8,10},{9,11},{10,... | collective-permute-start | bytes 24584 | tf_op jit(solution)/shard_map/ppermute | solution.py:585
  31.2 3.9 %collective-permute-start.16 = (f32[16,512]{1,0:T(8,128)S(1)}, f32[16,512]{1,0:T(8,128)S(1)}, u32[]{:S(2)}, u32[]{:S(2)}) collective-permute-start(f32[16,512]{1,0:T(8,128)S(1)} %get-tuple-element.85), channel_id=1, source_target_pairs={{0,1},{1,0},{2,4},{3,5},{4,2},{5,3},{6,8},{7,9},{8,6},{9,7},{10,12... | collective-permute-start | bytes 98312 | tf_op jit(solution)/shard_map/ppermute | solution.py:585
  33.2 3.3 %collective-permute-start.15 = (f32[40,128]{1,0:T(8,128)S(1)}, f32[40,128]{1,0:T(8,128)S(1)}, u32[]{:S(2)}, u32[]{:S(2)}) collective-permute-start(f32[40,128]{1,0:T(8,128)S(1)} %constant_dynamic-update-slice_fusion.5), channel_id=1, source_target_pairs={{0,10},{1,11},{2,8},{3,9},{4,14},{5,15},{6,12},{7,13},{8,2},{9,3},... | collective-permute-start | bytes 61448 | tf_op jit(solution)/shard_map/ppermute | solution.py:585
  36.5 4.3 %collective-permute-start.17 = (f32[72,128]{1,0:T(8,128)S(1)}, f32[72,128]{1,0:T(8,128)S(1)}, u32[]{:S(2)}, u32[]{:S(2)}) collective-permute-start(f32[72,128]{1,0:T(8,128)S(1)} %constant_dynamic-update-slice_fusion.10.tiles), channel_id=1, source_target_pairs={{0,18},{1,19},{2,16},{3,17},{4,22},{5,23},{6,20},{7,21},{8,26},{9,... | collective-permute-start | bytes 110600 | tf_op jit(solution)/shard_map/ppermute | solution.py:585
